TPU v7x, 512 devices: a whole 4x4x16 slice. The times are simulated.
512 devices in a mesh: seq: 128 (over z, x, core), head: 4 (over y).
Axes of the slice: x: 4, y: 4, z: 16, core: 2. Of those that a mesh axis runs over, the one named last changes fastest.
Arguments:
- queries: bfloat16 [16384, 2560], P('seq', 'head'), may hold values from -6 to 6
- keys: bfloat16 [16384, 2560], P('seq', 'head'), may hold values from -6 to 6
- values: bfloat16 [16384, 2560], P('seq', 'head'), may hold values from -6 to 6
- head_class: int32 [20], replicated, may hold values from 0 to 1, as said below
- window_lengths: int32 [128, 4], P('seq'), may hold values from 1 to 64, 128 in all within a row
- out_weight: bfloat16 [2560, 5120], P('seq', 'head'), may hold values from -0.125 to 0.125
Outputs:
- projected: bfloat16 [16384, 5120], P('seq', 'head')
Inputs may be any that keep to these rules, and one draw needn't show every extreme that they name: `head_class`: each group of 5 consecutive heads holds 1 to 3 temporal heads, and some group holds exactly 3. `window_lengths`: the 4 lengths of each block sum to 128, and the longest is exactly 64.
All inputs are finite; a program needn't handle non-finite values.
Results may differ from a plain program's by a relative error of at most 0.0057.
Values may be sent and summed in bfloat16 or wider, within the bound.
No kernel may reach another device: no remote copies, remote signals or barrier semaphores. Data moves between devices by JAX's collectives and lax.ppermute only.
A program may use at most 64 MiB of HBM per device.

v0:
```python
import math

import jax
import jax.numpy as jnp
from jax import lax
from jax.sharding import PartitionSpec as P

HD = 128
TMAX = 3
FRAMES = 8


def softmax_rows(scores):
    highest = jnp.max(scores, axis=-1, keepdims=True)
    weights = jnp.exp(scores - highest)
    return weights / jnp.sum(weights, axis=-1, keepdims=True)


def compact_heads(source, picker):
    return jnp.einsum("shd,th->std", source, picker, preferred_element_type=jnp.float32).astype(
        jnp.bfloat16
    )


def expand_heads(source, picker):
    return jnp.einsum("std,th->shd", source, picker, preferred_element_type=jnp.float32).astype(
        jnp.bfloat16
    )


def window_attention(query, key_rows, value_rows, lengths, scaling):
    ends = jnp.cumsum(lengths)
    positions = jnp.arange(query.shape[0], dtype=jnp.int32)
    window_ids = jnp.sum((positions[:, None] >= ends[None, :]).astype(jnp.int32), axis=1)
    same_window = window_ids[:, None] == window_ids[None, :]
    scores = (
        jnp.einsum("shd,thd->hst", query, key_rows, preferred_element_type=jnp.float32) * scaling
    )
    scores = jnp.where(same_window[None], scores, -1e30)
    weights = softmax_rows(scores).astype(jnp.bfloat16)
    return jnp.einsum(
        "hst,thd->shd", weights, value_rows, preferred_element_type=jnp.float32
    ).astype(jnp.bfloat16)


def body(queries, keys, values, head_class, window_lengths, out_weight):
    tok_len, columns = queries.shape
    local_heads = columns // HD
    scaling = 1.0 / math.sqrt(HD)
    head_group = lax.axis_index("head")
    classes = lax.dynamic_slice_in_dim(head_class, head_group * local_heads, local_heads)
    temporal_mask = classes == 1
    slot_rank = jnp.cumsum(temporal_mask.astype(jnp.int32)) - 1
    slot_ids = jnp.arange(TMAX, dtype=jnp.int32)
    picker = ((slot_rank[None, :] == slot_ids[:, None]) & temporal_mask[None, :]).astype(
        jnp.bfloat16
    )
    shaped = [array_in.reshape(tok_len, local_heads, HD) for array_in in (queries, keys, values)]
    lengths = window_lengths[0]
    spatial_out = window_attention(shaped[0], shaped[1], shaped[2], lengths, scaling)
    packed = [compact_heads(array_in, picker)[None] for array_in in shaped]
    query = lax.all_to_all(packed[0], "seq", split_axis=1, concat_axis=0, tiled=True)
    key_rows = lax.all_to_all(packed[1], "seq", split_axis=1, concat_axis=0, tiled=True)
    value_rows = lax.all_to_all(packed[2], "seq", split_axis=1, concat_axis=0, tiled=True)
    sources, width, count, size = query.shape
    groups = sources // FRAMES
    query = query.reshape(FRAMES, groups, width, count, size)
    key_rows = key_rows.reshape(FRAMES, groups, width, count, size)
    value_rows = value_rows.reshape(FRAMES, groups, width, count, size)
    scores = (
        jnp.einsum("fjcnd,gjcnd->jcnfg", query, key_rows, preferred_element_type=jnp.float32)
        * scaling
    )
    weights = softmax_rows(scores).astype(jnp.bfloat16)
    attended = jnp.einsum(
        "jcnfg,gjcnd->fjcnd", weights, value_rows, preferred_element_type=jnp.float32
    ).astype(jnp.bfloat16)
    attended = attended.reshape(sources, width, count, size)
    returned = lax.all_to_all(attended, "seq", split_axis=0, concat_axis=1, tiled=True)
    temporal_out = expand_heads(returned[0], picker)
    mixed = jnp.where(temporal_mask[None, :, None], temporal_out, spatial_out)
    mixed_local = mixed.reshape(tok_len, local_heads * HD)
    mixed_all = lax.all_gather(mixed_local, "head", axis=1, tiled=True)
    summed = jnp.dot(
        mixed_all,
        lax.all_gather(out_weight, "seq", axis=0, tiled=True),
        preferred_element_type=jnp.float32,
    )
    return summed.astype(jnp.bfloat16)


def solution(mesh):
    placed = (
        P("seq", "head"),
        P("seq", "head"),
        P("seq", "head"),
        P(),
        P("seq", None),
        P("seq", "head"),
    )
    return jax.shard_map(
        body, mesh=mesh, in_specs=placed, out_specs=P("seq", "head"), check_vma=False
    )
```

profile of v0, /device:TPU:1, one launch (start us, length us, event | category | flops | bytes accessed | tf_op | source)
XLA Modules:
  0.0 188.0 jit_solution(7246510899896471097)
XLA Ops:
  6.5 0.7 all-gather.3.cloned.1.call-update
  7.3 0.7 convert_bitcast_fusion
  8.2 1.1 copy.81
  9.2 0.2 copy.82
  9.5 0.9 fusion.11
  10.3 20.4 %all-to-all-start.2 = ((bf16[1,128,3,128]{3,2,0,1:T(4,128)(2,1)}), bf16[1,128,3,128]{3,2,0,1:T(4,128)(2,1)S(1)}, u32[]{:S(2)}, u32[]{:S(2)}) async-start(bf16[1,128,3,128]{3,2,0,1:T(4,128)(2,1)} %fusion.11), calls=%async_computation.2 | async-start | bytes 262144 | tf_op jit(solution)/shard_map/all_to_all | solution.py:63
  30.7 1.1 copy.77
  31.8 0.2 copy.78
  32.0 0.9 fusion.10
  32.9 14.7 %all-to-all-done.2 = bf16[1,128,3,128]{3,2,0,1:T(4,128)(2,1)S(1)} async-done(((bf16[1,128,3,128]{3,2,0,1:T(4,128)(2,1)}), bf16[1,128,3,128]{3,2,0,1:T(4,128)(2,1)S(1)}, u32[]{:S(2)}, u32[]{:S(2)}) %all-to-all-start.2) | async-done | bytes 98336 | tf_op jit(solution)/shard_map/all_to_all | solution.py:63
  47.6 6.9 %all-to-all-start.1 = ((bf16[1,128,3,128]{3,2,0,1:T(4,128)(2,1)}), bf16[1,128,3,128]{3,2,0,1:T(4,128)(2,1)S(1)}, u32[]{:S(2)}, u32[]{:S(2)}) async-start(bf16[1,128,3,128]{3,2,0,1:T(4,128)(2,1)} %fusion.10), calls=%async_computation.1 | async-start | bytes 262144 | tf_op jit(solution)/shard_map/all_to_all | solution.py:62
  54.5 0.8 reduce-window.17
  55.3 1.1 copy.73
  56.4 0.2 copy.74
  56.7 0.9 fusion.9
  57.6 13.6 %all-to-all-done.1 = bf16[1,128,3,128]{3,2,0,1:T(4,128)(2,1)S(1)} async-done(((bf16[1,128,3,128]{3,2,0,1:T(4,128)(2,1)}), bf16[1,128,3,128]{3,2,0,1:T(4,128)(2,1)S(1)}, u32[]{:S(2)}, u32[]{:S(2)}) %all-to-all-start.1) | async-done | bytes 98336 | tf_op jit(solution)/shard_map/all_to_all | solution.py:62
  71.1 7.2 %all-to-all-start = ((bf16[1,128,3,128]{3,2,0,1:T(4,128)(2,1)}), bf16[1,128,3,128]{3,2,0,1:T(4,128)(2,1)S(1)}, u32[]{:S(2)}, u32[]{:S(2)}) async-start(bf16[1,128,3,128]{3,2,0,1:T(4,128)(2,1)} %fusion.9), calls=%async_computation | async-start | bytes 262144 | tf_op jit(solution)/shard_map/all_to_all | solution.py:64
  78.4 0.3 fusion.38
  78.7 15.6 %all-to-all-done = bf16[1,128,3,128]{3,2,0,1:T(4,128)(2,1)S(1)} async-done(((bf16[1,128,3,128]{3,2,0,1:T(4,128)(2,1)}), bf16[1,128,3,128]{3,2,0,1:T(4,128)(2,1)S(1)}, u32[]{:S(2)}, u32[]{:S(2)}) %all-to-all-start) | async-done | bytes 98336 | tf_op jit(solution)/shard_map/all_to_all | solution.py:64
  94.3 0.3 fusion.12
  94.6 0.7 copy.90
  95.4 7.4 %all-to-all-start.3 = ((bf16[128,1,3,128]{3,2,1,0:T(4,128)(2,1)}), bf16[128,1,3,128]{3,2,1,0:T(4,128)(2,1)S(1)}, u32[]{:S(2)}, u32[]{:S(2)}) async-start(bf16[128,1,3,128]{3,2,1,0:T(4,128)(2,1)} %copy.90), calls=%async_computation.3 | async-start | bytes 262144 | tf_op jit(solution)/shard_map/all_to_all | solution.py:79
  102.8 0.3 fusion.3
  103.2 0.2 fusion.13
  103.4 0.2 copy.94
  103.6 16.8 %all-to-all-done.3 = bf16[128,1,3,128]{3,2,1,0:T(4,128)(2,1)S(1)} async-done(((bf16[128,1,3,128]{3,2,1,0:T(4,128)(2,1)}), bf16[128,1,3,128]{3,2,1,0:T(4,128)(2,1)S(1)}, u32[]{:S(2)}, u32[]{:S(2)}) %all-to-all-start.3) | async-done | bytes 98336 | tf_op jit(solution)/shard_map/all_to_all | solution.py:79
  120.4 0.3 fusion.7
  120.6 0.2 copy.95
  120.9 12.3 %all_gather.6 = bf16[128,2560]{0,1:T(8,128)(2,1)S(1)} all-gather(bf16[128,640]{0,1:T(8,128)(2,1)S(1)} %bitcast.64), channel_id=1, replica_groups=mesh['seq'=128,'head'=4] {'head'}, dimensions={1}, use_global_device_ids=true | all-gather | bytes 819200 | tf_op jit(solution)/shard_map/all_gather | solution.py:83
  133.1 32.8 %all-gather.3.cloned.1.call-done = bf16[128,20,1280]{2,1,0:T(8,128)(2,1)} async-done(((bf16[1,20,1280]{2,1,0:T(8,128)(2,1)}), bf16[128,20,1280]{2,1,0:T(8,128)(2,1)}) %all-gather.3.cloned.1.call-update) | async-done | bytes 6553616 | tf_op jit(solution)/shard_map/all_gather | solution.py:86
  165.9 10.6 %reshape.162 = bf16[2560,1280]{1,0:T(8,128)(2,1)} reshape(bf16[128,20,1280]{2,1,0:T(8,128)(2,1)} %all-gather.3.cloned.1.call-done) | data formatting | bytes 13107200
  176.5 4.7 %convolution_convert_fusion = bf16[128,1280]{1,0:T(8,128)(2,1)} fusion(bf16[128,2560]{0,1:T(8,128)(2,1)S(1)} %all_gather.6, bf16[2560,1280]{1,0:T(8,128)(2,1)} %reshape.162), kind=kOutput, calls=%fused_computation.2 | convolution fusion | flops 839024640 | bytes 7536640 | tf_op jit(solution)/shard_map/dot_general | solution.py:84
  (7 shorter events, 0.5 us)
Async XLA Ops:
  6.5 159.4 %all-gather.3.cloned.1.call-start = ((), (), s32[]{:S(2)}) async-start(), calls=%async_computation.4 | async-start | bytes 7925760 | tf_op jit(solution)/shard_map/all_gather | solution.py:86
  10.3 37.3 %all-to-all-start.2 = ((bf16[1,128,3,128]{3,2,0,1:T(4,128)(2,1)}), bf16[1,128,3,128]{3,2,0,1:T(4,128)(2,1)S(1)}, u32[]{:S(2)}, u32[]{:S(2)}) async-start(bf16[1,128,3,128]{3,2,0,1:T(4,128)(2,1)} %fusion.11), calls=%async_computation.2 | async-start | bytes 262144 | tf_op jit(solution)/shard_map/all_to_all | solution.py:63
  47.6 23.5 %all-to-all-start.1 = ((bf16[1,128,3,128]{3,2,0,1:T(4,128)(2,1)}), bf16[1,128,3,128]{3,2,0,1:T(4,128)(2,1)S(1)}, u32[]{:S(2)}, u32[]{:S(2)}) async-start(bf16[1,128,3,128]{3,2,0,1:T(4,128)(2,1)} %fusion.10), calls=%async_computation.1 | async-start | bytes 262144 | tf_op jit(solution)/shard_map/all_to_all | solution.py:62
  71.1 23.2 %all-to-all-start = ((bf16[1,128,3,128]{3,2,0,1:T(4,128)(2,1)}), bf16[1,128,3,128]{3,2,0,1:T(4,128)(2,1)S(1)}, u32[]{:S(2)}, u32[]{:S(2)}) async-start(bf16[1,128,3,128]{3,2,0,1:T(4,128)(2,1)} %fusion.9), calls=%async_computation | async-start | bytes 262144 | tf_op jit(solution)/shard_map/all_to_all | solution.py:64
  95.4 25.0 %all-to-all-start.3 = ((bf16[128,1,3,128]{3,2,1,0:T(4,128)(2,1)}), bf16[128,1,3,128]{3,2,1,0:T(4,128)(2,1)S(1)}, u32[]{:S(2)}, u32[]{:S(2)}) async-start(bf16[128,1,3,128]{3,2,1,0:T(4,128)(2,1)} %copy.90), calls=%async_computation.3 | async-start | bytes 262144 | tf_op jit(solution)/shard_map/all_to_all | solution.py:79
Sparse Core Ops, SparseCore 0:
  10.4 155.4 all-gather.2
where the time goes:
time: 189 us; the launch traced here: 188 us
  waiting for transfers between devices  94.1 us (50%)
  starting transfers between devices  41.9 us (22%)
  local copies, waits for them, and re-layouts  15.6 us (8%)
  between operations  13.5 us (7%)
  blocking collectives  12.3 us (7%)
  matrix products  8.6 us (5%)
  other arithmetic  2.01 us (1%)
    all_gather x1, waiting for transfers between devices, body(): lax.all_gather(out_weight, 'seq', axis=0, tiled=True)  32.8 us
    all_to_all x1, starting transfers between devices, body(): lax.all_to_all(packed[1], 'seq', split_axis=1, concat_axis=0, tiled=True)  20.4 us
    all_to_all x1, waiting for transfers between devices, body(): lax.all_to_all(attended, 'seq', split_axis=0, concat_axis=1, tiled=True)  16.8 us
    all_to_all x1, waiting for transfers between devices, body(): lax.all_to_all(packed[2], 'seq', split_axis=1, concat_axis=0, tiled=True)  15.6 us
    all_to_all x1, waiting for transfers between devices, body(): lax.all_to_all(packed[1], 'seq', split_axis=1, concat_axis=0, tiled=True)  14.7 us
    unnamed x4, local copies, waits for them, and re-layouts  13.8 us
    all_to_all x1, waiting for transfers between devices, body(): lax.all_to_all(packed[0], 'seq', split_axis=1, concat_axis=0, tiled=True)  13.6 us
    all_gather x1, blocking collectives, body(): mixed_all = lax.all_gather(mixed_local, 'head', axis=1, tiled=True)  12.3 us
  transfers between devices with their start and end apart: 5, of which 5 were waited for; matrix products, arithmetic and copies ran while one was open for 6% of the time, Pallas kernels for 0%

commit v1 on v0

v1 whole, which is shorter than its diff:
```python
import functools
import math

import jax
import jax.numpy as jnp
from jax import lax
from jax.experimental import pallas as pl
from jax.experimental.pallas import tpu as pltpu
from jax.sharding import Mesh, PartitionSpec as P

HD = 128
TMAX = 3
FRAMES = 8
TOK = 128
LOCAL = 5
COLS = LOCAL * HD
SCALE = 1.0 / math.sqrt(HD)
TOKEN_AXES = ("frame", "half", "x", "core")
VMEM = pl.BlockSpec(memory_space=pltpu.VMEM)
SMEM = pl.BlockSpec(memory_space=pltpu.SMEM)
PARAMS = pltpu.CompilerParams(vmem_limit_bytes=32 * 1024 * 1024)


def columns(head):
    return pl.ds(pl.multiple_of(head * HD, HD), HD)


def pack_kernel(slots_ref, q_ref, k_ref, v_ref, out_ref):
    for slot in range(TMAX):
        cols = columns(slots_ref[slot])
        for part, source in enumerate((q_ref, k_ref, v_ref)):
            first = (part * TMAX + slot) * HD
            out_ref[:, first : first + HD] = source[:, cols]


def attend(query, key, value, same):
    scores = lax.dot_general(
        query, key, (((1,), (1,)), ((), ())), preferred_element_type=jnp.float32
    )
    scores = jnp.where(same, scores * SCALE, -1e30)
    weights = jnp.exp(scores - jnp.max(scores, axis=-1, keepdims=True))
    weights = weights / jnp.sum(weights, axis=-1, keepdims=True)
    return jnp.dot(
        weights.astype(jnp.bfloat16), value, preferred_element_type=jnp.float32
    ).astype(jnp.bfloat16)


def window_kernel(lengths_ref, q_ref, k_ref, v_ref, out_ref):
    rows = lax.broadcasted_iota(jnp.int32, (TOK, TOK), 0)
    cols = lax.broadcasted_iota(jnp.int32, (TOK, TOK), 1)
    row_id = jnp.zeros((TOK, TOK), jnp.int32)
    col_id = jnp.zeros((TOK, TOK), jnp.int32)
    end = 0
    for window in range(4):
        end = end + lengths_ref[0, window]
        row_id = row_id + (rows >= end).astype(jnp.int32)
        col_id = col_id + (cols >= end).astype(jnp.int32)
    same = row_id == col_id
    for head in range(LOCAL):
        span = slice(head * HD, (head + 1) * HD)
        out_ref[:, span] = attend(q_ref[:, span], k_ref[:, span], v_ref[:, span], same)


def frame_kernel(packed_ref, out_ref):
    width = TOK // FRAMES
    rows = lax.broadcasted_iota(jnp.int32, (TOK, TOK), 0)
    cols = lax.broadcasted_iota(jnp.int32, (TOK, TOK), 1)
    same = (rows & (width - 1)) == (cols & (width - 1))
    for slot in range(TMAX):
        span = [
            slice((part * TMAX + slot) * HD, (part * TMAX + slot + 1) * HD) for part in range(3)
        ]
        out_ref[:, slot * HD : (slot + 1) * HD] = attend(
            packed_ref[:, span[0]], packed_ref[:, span[1]], packed_ref[:, span[2]], same
        )


def mix_kernel(rank_ref, spatial_ref, temporal_ref, out_ref):
    for head in range(LOCAL):
        span = slice(head * HD, (head + 1) * HD)
        rank = rank_ref[head]

        @pl.when(rank < 0)
        def _():
            for copy in range(4):
                out_ref[copy, :, span] = spatial_ref[:, span]

        @pl.when(rank >= 0)
        def _():
            for copy in range(4):
                out_ref[copy, :, span] = temporal_ref[:, columns(jnp.maximum(rank, 0))]


def spread_kernel(weight_ref, out_ref):
    for x in range(4):
        for core in range(2):
            out_ref[2 * x + core] = weight_ref[:, core * COLS : (core + 1) * COLS]


def project_kernel(own_ref, other_ref, weight_ref, out_ref):
    for place, source in enumerate((own_ref, other_ref)):
        total = jnp.zeros((TOK, COLS), jnp.float32)
        for group in range(4):
            total = total + jnp.dot(
                source[group],
                weight_ref[group * COLS : (group + 1) * COLS, :],
                preferred_element_type=jnp.float32,
            )
        out_ref[place] = total.astype(jnp.bfloat16)


def join_kernel(core_ref, both_ref, arrived_ref, out_ref):
    core = core_ref[0]
    out_ref[:, pl.ds(pl.multiple_of(core * COLS, HD), COLS)] = both_ref[0]
    out_ref[:, pl.ds(pl.multiple_of((1 - core) * COLS, HD), COLS)] = arrived_ref[...]


def call(kernel, out_shape, specs, *args, scratch=(), flops=0):
    size = sum(a.size * a.dtype.itemsize for a in args) + math.prod(out_shape) * 2
    return pl.pallas_call(
        kernel,
        out_shape=jax.ShapeDtypeStruct(out_shape, jnp.bfloat16),
        in_specs=specs,
        out_specs=VMEM,
        scratch_shapes=scratch,
        compiler_params=PARAMS,
        cost_estimate=pl.CostEstimate(flops=flops, bytes_accessed=size, transcendentals=0),
    )(*args)


def body(queries, keys, values, head_class, window_lengths, out_weight):
    core = lax.axis_index("core")
    group = lax.axis_index("head")
    classes = lax.dynamic_slice_in_dim(head_class, group * LOCAL, LOCAL)
    temporal = classes == 1
    rank = jnp.where(temporal, jnp.cumsum(temporal.astype(jnp.int32)) - 1, -1)
    slots = jnp.sum(
        jnp.where(
            rank[None, :] == jnp.arange(TMAX, dtype=jnp.int32)[:, None],
            jnp.arange(LOCAL, dtype=jnp.int32)[None, :],
            0,
        ),
        axis=1,
    ).astype(jnp.int32)

    weight = call(spread_kernel, (8, 20, COLS), [VMEM], out_weight)
    weight = lax.all_to_all(weight, ("x", "core"), 0, 0, tiled=True).reshape(160, COLS)

    width = TOK // FRAMES
    packed = call(
        pack_kernel, (TOK, 3 * TMAX * HD), [SMEM] + [VMEM] * 3, slots, queries, keys, values
    )
    packed, weight = lax.optimization_barrier((packed, weight))
    weight = lax.all_gather(weight, ("frame", "half"), axis=0, tiled=True)
    packed = lax.all_to_all(
        packed.reshape(FRAMES, width, 3 * TMAX * HD), "frame", 0, 0, tiled=True
    ).reshape(TOK, 3 * TMAX * HD)
    spatial = call(
        window_kernel, (TOK, COLS), [SMEM] + [VMEM] * 3, window_lengths, queries, keys, values
    )
    attended = call(frame_kernel, (TOK, TMAX * HD), [VMEM], packed)
    attended = lax.all_to_all(
        attended.reshape(FRAMES, width, TMAX * HD), "frame", 0, 0, tiled=True
    ).reshape(TOK, TMAX * HD)

    mixed = call(
        mix_kernel, (4, TOK, COLS), [SMEM] + [VMEM] * 2, rank, spatial, attended
    )
    mixed = lax.all_to_all(mixed, "head", 0, 0, tiled=True)
    swap = [(0, 1), (1, 0)]
    other = lax.ppermute(mixed, "core", swap)
    both = call(
        project_kernel,
        (2, TOK, COLS),
        [VMEM] * 3,
        mixed,
        other,
        weight,
        flops=2 * TOK * 2560 * 1280,
    )
    arrived = lax.ppermute(both[1], "core", swap)
    return call(
        join_kernel,
        (TOK, 2 * COLS),
        [SMEM] + [VMEM] * 2,
        core.astype(jnp.int32).reshape(1),
        both,
        arrived,
    )


def solution(mesh):
    mesh = Mesh(mesh.devices.reshape(8, 2, 4, 2, 4), TOKEN_AXES + ("head",))
    split = P(TOKEN_AXES, "head")
    placed = (split, split, split, P(), P(TOKEN_AXES, None), split)
    return jax.shard_map(body, mesh=mesh, in_specs=placed, out_specs=split, check_vma=False)
```

time: 189 us -> 126 us (0.67)
  waiting for transfers between devices: 94.1 us -> 18.3 us
  blocking collectives: 12.3 us -> 40.3 us
  local copies, waits for them, and re-layouts: 15.6 us -> 6.31 us
  matrix products: 8.6 us -> 0 us
  Pallas kernels: 0 us -> 8.12 us
  starting transfers between devices: 41.9 us -> 37 us
    all_to_all x4 -> x2, waiting for transfers between devices: 60.7 us -> 11.5 us  [the longest x1 10.3 us: body(): lax.all_to_all(attended.reshape(FRAMES, width, TMAX * HD), 'frame', 0, 0,...]
    all_to_all x0 -> x2, blocking collectives: none -> 40.3 us  [the longest x1 26.8 us: body(): lax.all_to_all(packed.reshape(FRAMES, width, 3 * TMAX * HD), 'frame', 0,...]
    all_gather x1, waiting for transfers between devices: 32.8 us -> 4.03 us  [body(): weight = lax.all_gather(weight, ('frame', 'half'), axis=0, tiled=True)]
    all_to_all x4 -> x2, starting transfers between devices: 41.9 us -> 19.6 us  [the longest x1 10.2 us: body(): lax.all_to_all(weight, ('x', 'core'), 0, 0, tiled=True).reshape(160, COLS)]
    ppermute x0 -> x2, starting transfers between devices: none -> 17.4 us  [the longest x1 10.8 us: body(): arrived = lax.ppermute(both[1], 'core', swap)]
    all_gather x1 -> x0, blocking collectives: 12.3 us -> none  [body(): mixed_all = lax.all_gather(mixed_local, 'head', axis=1, tiled=True)]
    dot_general x8 -> x0, matrix products: 8.28 us -> none  [the longest x1 4.65 us: body(): jnp.dot(mixed_all, lax.all_gather(out_weight, 'seq', axis=0, tiled=True),...]
    unnamed x4 -> x18, local copies, waits for them, and re-layouts: 13.8 us -> 5.57 us
  transfers between devices with their start and end apart: 5 -> 5, of which waited for: 5 -> 5; matrix products, arithmetic and copies ran while one was open for 6% -> 1% of each run, Pallas kernels for 0% -> 4%
where the time goes in v1:
time: 126 us; the launch traced here: 125 us
  blocking collectives  40.3 us (32%)
  starting transfers between devices  37 us (29%)
  waiting for transfers between devices  18.3 us (15%)
  between operations  13.5 us (11%)
  Pallas kernels  8.12 us (6%)
  local copies, waits for them, and re-layouts  6.31 us (5%)
  other arithmetic  1.76 us (1%)
    all_to_all x1, blocking collectives, body(): lax.all_to_all(packed.reshape(FRAMES, width, 3 * TMAX * HD), 'frame', 0,...  26.8 us
    all_to_all x1, blocking collectives, body(): mixed = lax.all_to_all(mixed, 'head', 0, 0, tiled=True)  13.5 us
    ppermute x1, starting transfers between devices, body(): arrived = lax.ppermute(both[1], 'core', swap)  10.8 us
    all_to_all x1, waiting for transfers between devices, body(): lax.all_to_all(attended.reshape(FRAMES, width, TMAX * HD), 'frame', 0, 0,...  10.3 us
    all_to_all x1, starting transfers between devices, body(): lax.all_to_all(weight, ('x', 'core'), 0, 0, tiled=True).reshape(160, COLS)  10.2 us
    all_to_all x1, starting transfers between devices, body(): lax.all_to_all(attended.reshape(FRAMES, width, TMAX * HD), 'frame', 0, 0,...  9.45 us
    pallas_call x7, Pallas kernels, call(): pl.pallas_call(kernel, out_shape=jax.ShapeDtypeStruct(out_shape, jnp.bflo...  8.12 us
    ppermute x1, starting transfers between devices, body(): other = lax.ppermute(mixed, 'core', swap)  6.57 us
  transfers between devices with their start and end apart: 5, of which 5 were waited for; matrix products, arithmetic and copies ran while one was open for 1% of the time, Pallas kernels for 4%

profile of v1, /device:TPU:1, one launch (start us, length us, event | category | flops | bytes accessed | tf_op | source)
XLA Modules:
  0.0 125.3 jit_solution(3567192056121543303)
XLA Ops:
  6.5 0.9 copy-done.7
  7.4 0.7 shard_map.66
  8.1 10.2 %all-to-all-start = ((bf16[8,20,640]{2,1,0:T(8,128)(2,1)}), bf16[8,20,640]{2,1,0:T(8,128)(2,1)S(1)}, u32[]{:S(2)}, u32[]{:S(2)}) async-start(bf16[8,20,640]{2,1,0:T(8,128)(2,1)} %shard_map.66), calls=%async_computation | async-start | bytes 491520 | tf_op jit(solution)/shard_map/all_to_all | solution.py:147
  18.3 0.0 all-gather.2.cloned.1.call-start
  18.3 0.7 fusion
  19.1 0.2 reduce-window.9
  19.2 0.7 compare_select_fusion.rank_ref
  20.0 0.1 select_reduce_fusion.slots_ref
  20.1 0.9 copy-done.1
  21.0 0.9 copy-done.3
  21.9 0.9 copy-done.5
  22.8 0.6 shard_map.65
  23.4 1.3 all-to-all-done
  24.7 0.7 reshape.48
  25.4 0.0 all-gather.2.cloned.1.call-update
  25.4 26.8 %all_to_all.20 = bf16[8,16,1152]{2,1,0:T(8,128)(2,1)S(1)} all-to-all(bf16[8,16,1152]{2,1,0:T(8,128)(2,1)S(1)} %bitcast.12), channel_id=1, replica_groups=mesh['frame'=8,'half'=2,'x'=4,'core'=2,'head'=4] {'frame'}, dimensions={0} | all-to-all | bytes 589824 | tf_op jit(solution)/shard_map/all_to_all | solution.py:155
  52.2 1.7 %shard_map.67 = bf16[128,384]{1,0:T(8,128)(2,1)} custom-call(bf16[128,1152]{1,0:T(8,128)(2,1)S(1)} %bitcast.11), custom_call_target="tpu_custom_call" | custom-call | bytes 393216 | tf_op jit(solution)/shard_map/pallas_call | solution.py:120
  53.9 9.5 %all-to-all-start.2 = ((bf16[8,16,384]{2,1,0:T(8,128)(2,1)}), bf16[8,16,384]{2,1,0:T(8,128)(2,1)S(1)}, u32[]{:S(2)}, u32[]{:S(2)}) async-start(bf16[8,16,384]{2,1,0:T(8,128)(2,1)} %bitcast.5), calls=%async_computation.2 | async-start | bytes 196608 | tf_op jit(solution)/shard_map/all_to_all | solution.py:162
  63.4 0.0 copy-done.6
  63.4 0.0 copy-done.4
  63.4 2.3 %shard_map.64.spatial_ref = bf16[128,640]{1,0:T(8,128)(2,1)S(1)} custom-call(s32[1,4]{1,0:T(1,128)S(1)} %copy-done.8, bf16[128,640]{1,0:T(8,128)(2,1)S(1)} %copy-done.2, bf16[128,640]{1,0:T(8,128)(2,1)S(1)} %copy-done.4, bf16[128,640]{1,0:T(8,128)(2,1)S(1)} %copy-done.6), custom_call_target="tpu_custom_call" | custom-call | bytes 655376 | tf_op jit(solution)/shard_map/pallas_call | solution.py:120
  65.7 10.3 %all-to-all-done.2 = bf16[8,16,384]{2,1,0:T(8,128)(2,1)S(1)} async-done(((bf16[8,16,384]{2,1,0:T(8,128)(2,1)}), bf16[8,16,384]{2,1,0:T(8,128)(2,1)S(1)}, u32[]{:S(2)}, u32[]{:S(2)}) %all-to-all-start.2) | async-done | bytes 98336 | tf_op jit(solution)/shard_map/all_to_all | solution.py:162
  76.0 0.7 shard_map.68
  76.7 13.5 %all_to_all.21.own_ref = bf16[4,128,640]{2,1,0:T(8,128)(2,1)S(1)} all-to-all(bf16[4,128,640]{2,1,0:T(8,128)(2,1)S(1)} %shard_map.68), channel_id=1, replica_groups=mesh['frame'=8,'half'=2,'x'=4,'core'=2,'head'=4] {'head'}, dimensions={0} | all-to-all | bytes 1310720 | tf_op jit(solution)/shard_map/all_to_all | solution.py:169
  90.2 6.6 %collective-permute-start = (bf16[4,128,640]{2,1,0:T(8,128)(2,1)S(1)}, bf16[4,128,640]{2,1,0:T(8,128)(2,1)S(1)}, u32[]{:S(2)}, u32[]{:S(2)}) collective-permute-start(bf16[4,128,640]{2,1,0:T(8,128)(2,1)S(1)} %all_to_all.21.own_ref), channel_id=1, source_target_pairs={{0,4},{4,0},{1,5},{5,1},{2,6},{6,2},{3,7},{7,3},{8,12},{12,8},{9,1... | collective-permute-start | bytes 1966088 | tf_op jit(solution)/shard_map/ppermute | solution.py:171
  96.8 1.7 %collective-permute-done.other_ref = bf16[4,128,640]{2,1,0:T(8,128)(2,1)S(1)} collective-permute-done((bf16[4,128,640]{2,1,0:T(8,128)(2,1)S(1)}, bf16[4,128,640]{2,1,0:T(8,128)(2,1)S(1)}, u32[]{:S(2)}, u32[]{:S(2)}) %collective-permute-start) | collective-permute-done | bytes 655392 | tf_op jit(solution)/shard_map/ppermute | solution.py:171
  98.5 4.0 %all-gather.2.cloned.1.call-done.weight_ref = bf16[2560,640]{1,0:T(8,128)(2,1)} async-done(((bf16[160,640]{1,0:T(8,128)(2,1)}), bf16[2560,640]{1,0:T(8,128)(2,1)}) %all-gather.2.cloned.1.call-update) | async-done | bytes 3276816 | tf_op jit(solution)/shard_map/all_gather | solution.py:154
  102.5 1.9 %copy-done = bf16[2560,640]{1,0:T(8,128)(2,1)S(1)} copy-done((bf16[2560,640]{1,0:T(8,128)(2,1)S(1)}, bf16[2560,640]{1,0:T(8,128)(2,1)}, u32[]{:S(2)}) %copy-start) | copy-done | bytes 3276824
  104.4 1.4 %shard_map.69.both_ref = bf16[2,128,640]{2,1,0:T(8,128)(2,1)S(1)} custom-call(bf16[4,128,640]{2,1,0:T(8,128)(2,1)S(1)} %all_to_all.21.own_ref, bf16[4,128,640]{2,1,0:T(8,128)(2,1)S(1)} %collective-permute-done.other_ref, bf16[2560,640]{1,0:T(8,128)(2,1)S(1)} %copy-done), custom_call_target="tpu_custom_call" | custom-call | flops 838860800 | bytes 4915200 | tf_op jit(solution)/shard_map/pallas_call | solution.py:120
  105.9 10.8 %collective-permute-start.1 = (bf16[128,640]{1,0:T(8,128)(2,1)S(1)}, bf16[128,640]{1,0:T(8,128)(2,1)S(1)}, u32[]{:S(2)}, u32[]{:S(2)}) collective-permute-start(bf16[128,640]{1,0:T(8,128)(2,1)S(1)} %slice_bitcast_fusion), channel_id=1, source_target_pairs={{0,4},{4,0},{1,5},{5,1},{2,6},{6,2},{3,7},{7,3},{8,12},{12,8},{9,1... | collective-permute-start | bytes 491528 | tf_op jit(solution)/shard_map/ppermute | solution.py:181
  116.7 1.0 collective-permute-done.1.arrived_ref
  117.7 0.8 shard_map.70
  (12 shorter events, 0.0 us)
Async XLA Ops:
  6.5 56.9 %copy-start.6 = (bf16[128,640]{1,0:T(8,128)(2,1)S(1)}, bf16[128,640]{1,0:T(8,128)(2,1)}, u32[]{:S(2)}) copy-start(bf16[128,640]{1,0:T(8,128)(2,1)} %v_ref.3) | copy-start | bytes 491524
  6.5 56.9 %copy-start.4 = (bf16[128,640]{1,0:T(8,128)(2,1)S(1)}, bf16[128,640]{1,0:T(8,128)(2,1)}, u32[]{:S(2)}) copy-start(bf16[128,640]{1,0:T(8,128)(2,1)} %k_ref.3) | copy-start | bytes 491524
  6.5 56.9 %copy-start.2 = (bf16[128,640]{1,0:T(8,128)(2,1)S(1)}, bf16[128,640]{1,0:T(8,128)(2,1)}, u32[]{:S(2)}) copy-start(bf16[128,640]{1,0:T(8,128)(2,1)} %q_ref.3) | copy-start | bytes 491524
  6.5 0.9 copy-start.7
  7.4 56.0 %copy-start.8 = (s32[1,4]{1,0:T(1,128)S(1)}, s32[1,4]{1,0:T(1,128)}, u32[]{:S(2)}) copy-start(s32[1,4]{1,0:T(1,128)} %lengths_ref.1) | copy-start | bytes 52
  8.1 16.6 %all-to-all-start = ((bf16[8,20,640]{2,1,0:T(8,128)(2,1)}), bf16[8,20,640]{2,1,0:T(8,128)(2,1)S(1)}, u32[]{:S(2)}, u32[]{:S(2)}) async-start(bf16[8,20,640]{2,1,0:T(8,128)(2,1)} %shard_map.66), calls=%async_computation | async-start | bytes 491520 | tf_op jit(solution)/shard_map/all_to_all | solution.py:147
  18.3 84.2 %all-gather.2.cloned.1.call-start = ((), (), s32[]{:S(2)}) async-start(), calls=%async_computation.4 | async-start | bytes 3481600 | tf_op jit(solution)/shard_map/all_gather | solution.py:154
  20.1 0.9 copy-start.1
  21.0 0.9 copy-start.3
  21.9 0.9 copy-start.5
  53.9 22.0 %all-to-all-start.2 = ((bf16[8,16,384]{2,1,0:T(8,128)(2,1)}), bf16[8,16,384]{2,1,0:T(8,128)(2,1)S(1)}, u32[]{:S(2)}, u32[]{:S(2)}) async-start(bf16[8,16,384]{2,1,0:T(8,128)(2,1)} %bitcast.5), calls=%async_computation.2 | async-start | bytes 196608 | tf_op jit(solution)/shard_map/all_to_all | solution.py:162
  90.2 8.3 %collective-permute-start = (bf16[4,128,640]{2,1,0:T(8,128)(2,1)S(1)}, bf16[4,128,640]{2,1,0:T(8,128)(2,1)S(1)}, u32[]{:S(2)}, u32[]{:S(2)}) collective-permute-start(bf16[4,128,640]{2,1,0:T(8,128)(2,1)S(1)} %all_to_all.21.own_ref), channel_id=1, source_target_pairs={{0,4},{4,0},{1,5},{5,1},{2,6},{6,2},{3,7},{7,3},{8,12},{12,8},{9,1... | collective-permute-start | bytes 1966088 | tf_op jit(solution)/shard_map/ppermute | solution.py:171
  102.5 1.9 %copy-start = (bf16[2560,640]{1,0:T(8,128)(2,1)S(1)}, bf16[2560,640]{1,0:T(8,128)(2,1)}, u32[]{:S(2)}) copy-start(bf16[2560,640]{1,0:T(8,128)(2,1)} %all-gather.2.cloned.1.call-done.weight_ref) | copy-start | bytes 9830404
  105.9 11.8 %collective-permute-start.1 = (bf16[128,640]{1,0:T(8,128)(2,1)S(1)}, bf16[128,640]{1,0:T(8,128)(2,1)S(1)}, u32[]{:S(2)}, u32[]{:S(2)}) collective-permute-start(bf16[128,640]{1,0:T(8,128)(2,1)S(1)} %slice_bitcast_fusion), channel_id=1, source_target_pairs={{0,4},{4,0},{1,5},{5,1},{2,6},{6,2},{3,7},{7,3},{8,12},{12,8},{9,1... | collective-permute-start | bytes 491528 | tf_op jit(solution)/shard_map/ppermute | solution.py:181
Sparse Core Ops, SparseCore 0:
  25.6 76.9 all-gather.1

commit v2 on v1

v2 whole, which is shorter than its diff:
```python
import functools
import math

import jax
import jax.numpy as jnp
from jax import lax
from jax.experimental import pallas as pl
from jax.experimental.pallas import tpu as pltpu
from jax.sharding import Mesh, PartitionSpec as P

HD = 128
TMAX = 3
FRAMES = 8
TOK = 128
LOCAL = 5
COLS = LOCAL * HD
PART = 384
SCALE = 1.0 / math.sqrt(HD)
TOKEN_AXES = ("frame", "half", "x", "core")
VMEM = pl.BlockSpec(memory_space=pltpu.VMEM)
SMEM = pl.BlockSpec(memory_space=pltpu.SMEM)
HBM = pl.BlockSpec(memory_space=pltpu.HBM)
PARAMS = pltpu.CompilerParams(vmem_limit_bytes=16 * 1024 * 1024)


def columns(head):
    return pl.ds(pl.multiple_of(head * HD, HD), HD)


def ranks(classes_ref, group):
    found, before = [], 0
    for head in range(LOCAL):
        temporal = classes_ref[group * LOCAL + head] == 1
        found.append((temporal, before))
        before = before + temporal.astype(jnp.int32)
    return found


def pack_kernel(group_ref, classes_ref, q_ref, k_ref, v_ref, out_ref, sems):
    slots = [0] * TMAX
    for head, (temporal, before) in enumerate(ranks(classes_ref, group_ref[0])):
        slots = [
            jnp.where(temporal & (before == slot), head, taken)
            for slot, taken in enumerate(slots)
        ]
    copies = []
    for part, source in enumerate((q_ref, k_ref, v_ref)):
        for slot in range(TMAX):
            place = part * TMAX + slot
            copies.append(
                pltpu.make_async_copy(
                    source.at[:, columns(slots[slot])],
                    out_ref.at[:, place * HD : (place + 1) * HD],
                    sems.at[place],
                )
            )
    for copy in copies:
        copy.start()
    for copy in copies:
        copy.wait()


def attend(query, key, value, same):
    scores = lax.dot_general(
        query, key, (((1,), (1,)), ((), ())), preferred_element_type=jnp.float32
    )
    scores = jnp.where(same, scores * SCALE, -1e30)
    weights = jnp.exp(scores - jnp.max(scores, axis=-1, keepdims=True))
    weights = weights / jnp.sum(weights, axis=-1, keepdims=True)
    return jnp.dot(
        weights.astype(jnp.bfloat16), value, preferred_element_type=jnp.float32
    ).astype(jnp.bfloat16)


def window_kernel(lengths_ref, q_ref, k_ref, v_ref, out_ref):
    rows = lax.broadcasted_iota(jnp.int32, (TOK, TOK), 0)
    cols = lax.broadcasted_iota(jnp.int32, (TOK, TOK), 1)
    row_id = jnp.zeros((TOK, TOK), jnp.int32)
    col_id = jnp.zeros((TOK, TOK), jnp.int32)
    end = 0
    for window in range(4):
        end = end + lengths_ref[0, window]
        row_id = row_id + (rows >= end).astype(jnp.int32)
        col_id = col_id + (cols >= end).astype(jnp.int32)
    same = row_id == col_id
    for head in range(LOCAL):
        span = slice(head * HD, (head + 1) * HD)
        out_ref[:, span] = attend(q_ref[:, span], k_ref[:, span], v_ref[:, span], same)


def frame_kernel(packed_ref, out_ref):
    width = TOK // FRAMES
    rows = lax.broadcasted_iota(jnp.int32, (TOK, TOK), 0)
    cols = lax.broadcasted_iota(jnp.int32, (TOK, TOK), 1)
    same = (rows & (width - 1)) == (cols & (width - 1))
    for slot in range(TMAX):
        span = [
            slice((part * TMAX + slot) * HD, (part * TMAX + slot + 1) * HD) for part in range(3)
        ]
        out_ref[:, slot * HD : (slot + 1) * HD] = attend(
            packed_ref[:, span[0]], packed_ref[:, span[1]], packed_ref[:, span[2]], same
        )


def mix_kernel(group_ref, classes_ref, spatial_ref, temporal_ref, order_ref, out_ref, mixed):
    for head, (temporal, before) in enumerate(ranks(classes_ref, group_ref[0])):
        span = slice(head * HD, (head + 1) * HD)

        @pl.when(jnp.logical_not(temporal))
        def _():
            mixed[:, span] = spatial_ref[:, span]

        @pl.when(temporal)
        def _():
            mixed[:, span] = temporal_ref[:, columns(before)]

    ordered = jnp.dot(mixed[...], order_ref[...], preferred_element_type=jnp.float32)
    ordered = ordered.astype(jnp.bfloat16)
    for copy in range(4):
        for core in range(2):
            out_ref[2 * copy + core] = ordered[:, core * PART : (core + 1) * PART]


def rows_kernel(weight_ref, out_ref):
    for group in range(4):
        out_ref[group * 80 : (group + 1) * 80, :] = jnp.concatenate(
            [weight_ref[4 * group + z] for z in range(4)], axis=0
        )


def project_kernel(core_ref, mixed_ref, w0_ref, w1_ref, w2_ref, w3_ref, own_ref, other_ref):
    core = core_ref[0]
    zeros = jnp.zeros((PART - 320, 2 * COLS), jnp.bfloat16)
    total = jnp.zeros((2 * TOK, 2 * COLS), jnp.float32)
    for group in range(4):
        span = slice(group * 80, (group + 1) * 80)
        rows = [w[span, :] for w in (w0_ref, w1_ref, w2_ref, w3_ref)]
        tokens = jnp.concatenate(
            [mixed_ref[2 * group + core], mixed_ref[2 * group + 1 - core]], axis=0
        )
        total = total + jnp.dot(
            tokens,
            jnp.concatenate(rows + [zeros], axis=0),
            preferred_element_type=jnp.float32,
        )
    own_ref[...] = total[:TOK]
    other_ref[...] = total[TOK:]


def sum_kernel(own_ref, arrived_ref, out_ref):
    out_ref[...] = (own_ref[...] + arrived_ref[...]).astype(jnp.bfloat16)


def call(kernel, out_shape, specs, *args, scratch=(), flops=0, out_dtype=jnp.bfloat16):
    shapes = out_shape if isinstance(out_shape, list) else [out_shape]
    size = sum(a.size * a.dtype.itemsize for a in args)
    size += sum(math.prod(shape) * jnp.dtype(out_dtype).itemsize for shape in shapes)
    results = pl.pallas_call(
        kernel,
        out_shape=[jax.ShapeDtypeStruct(shape, out_dtype) for shape in shapes],
        in_specs=specs,
        out_specs=[VMEM] * len(shapes),
        scratch_shapes=scratch,
        compiler_params=PARAMS,
        cost_estimate=pl.CostEstimate(flops=flops, bytes_accessed=size, transcendentals=0),
    )(*args)
    return results if isinstance(out_shape, list) else results[0]


def body(queries, keys, values, head_class, window_lengths, out_weight):
    core = lax.axis_index("core").astype(jnp.int32).reshape(1)
    group = lax.axis_index("head").astype(jnp.int32).reshape(1)
    width = TOK // FRAMES
    packed = call(
        pack_kernel,
        (TOK, 3 * TMAX * HD),
        [SMEM] * 2 + [HBM] * 3,
        group,
        head_class,
        queries,
        keys,
        values,
        scratch=[pltpu.SemaphoreType.DMA((3 * TMAX,))],
    )
    packed, weight = lax.optimization_barrier((packed, out_weight))
    weight = lax.all_gather(weight, ("frame", "half"), axis=0, tiled=False)
    packed = lax.all_to_all(
        packed.reshape(FRAMES, width, 3 * TMAX * HD), "frame", 0, 0, tiled=True
    ).reshape(TOK, 3 * TMAX * HD)
    packed, weight = lax.optimization_barrier((packed, weight))
    attended = call(frame_kernel, (TOK, TMAX * HD), [VMEM], packed)
    attended, weight, queries, keys, values = lax.optimization_barrier(
        (attended, weight, queries, keys, values)
    )
    weight = call(rows_kernel, (320, 2 * COLS), [VMEM], weight)
    around = [
        lax.ppermute(weight, "x", [((x + step) % 4, x) for x in range(4)]) for step in (1, 2, 3)
    ]
    spatial = call(
        window_kernel, (TOK, COLS), [SMEM] + [VMEM] * 3, window_lengths, queries, keys, values
    )
    attended = lax.all_to_all(
        attended.reshape(FRAMES, width, TMAX * HD), "frame", 0, 0, tiled=True
    ).reshape(TOK, TMAX * HD)

    source = jnp.arange(COLS, dtype=jnp.int32)[:, None]
    place = jnp.arange(2 * PART, dtype=jnp.int32)[None, :]
    rest = place % PART
    owner = (lax.axis_index("x") + rest // 80) % 4
    wanted = rest % 80 // 20 * 160 + owner * 40 + place // PART * 20 + rest % 20
    order = ((source == wanted) & (rest < 320)).astype(jnp.bfloat16)
    mixed = call(
        mix_kernel,
        (8, TOK, PART),
        [SMEM] * 2 + [VMEM] * 3,
        group,
        head_class,
        spatial,
        attended,
        order,
        scratch=[pltpu.VMEM((TOK, COLS), jnp.bfloat16)],
    )
    mixed = lax.all_to_all(mixed, ("head", "core"), 0, 0, tiled=True)
    own, other = call(
        project_kernel,
        [(TOK, 2 * COLS)] * 2,
        [SMEM] + [VMEM] * 5,
        core,
        mixed,
        weight,
        *around,
        flops=2 * TOK * 2560 * 1280,
        out_dtype=jnp.float32,
    )
    arrived = lax.ppermute(other, "core", [(0, 1), (1, 0)])
    return call(sum_kernel, (TOK, 2 * COLS), [VMEM] * 2, own, arrived)


def solution(mesh):
    mesh = Mesh(mesh.devices.reshape(8, 2, 4, 2, 4), TOKEN_AXES + ("head",))
    split = P(TOKEN_AXES, "head")
    placed = (split, split, split, P(), P(TOKEN_AXES, None), split)
    return jax.shard_map(body, mesh=mesh, in_specs=placed, out_specs=split, check_vma=False)
```

time: 126 us -> 122 us (0.968)
  starting transfers between devices: 37 us -> 52.2 us
  between operations: 13.5 us -> 0.17 us
  waiting for transfers between devices: 18.3 us -> 14 us
  Pallas kernels: 8.12 us -> 10.8 us
  other arithmetic: 1.76 us -> 0.43 us
  local copies, waits for them, and re-layouts: 6.31 us -> 5.01 us
    all_to_all x2 -> x0, blocking collectives: 40.3 us -> none  [the longest x1 26.8 us: body(): lax.all_to_all(packed.reshape(FRAMES, width, 3 * TMAX * HD), 'frame', 0,...]
    all_gather x0 -> x1, blocking collectives: none -> 39.2 us  [body(): weight = lax.all_gather(weight, ('frame', 'half'), axis=0, tiled=False)]
    all_to_all x1 -> x2, starting transfers between devices: 10.2 us -> 28.8 us  [the longest x1 15.7 us: body(): lax.all_to_all(packed.reshape(FRAMES, width, 3 * TMAX * HD), 'frame', 0,...]
    all_to_all x1, waiting for transfers between devices: 10.3 us -> 0.01 us  [body(): lax.all_to_all(attended.reshape(FRAMES, width, TMAX * HD), 'frame', 0, 0,...]
    ppermute x2 -> x4, waiting for transfers between devices: 2.7 us -> 12.3 us  [the longest x3 10.6 us: body(): lax.ppermute(weight, 'x', [((x + step) % 4, x) for x in range(4)])]
    all_gather x1 -> x0, waiting for transfers between devices: 4.03 us -> none  [body(): weight = lax.all_gather(weight, ('frame', 'half'), axis=0, tiled=True)]
    ppermute x2 -> x4, starting transfers between devices: 17.4 us -> 14.4 us  [the longest x3 10.7 us: body(): lax.ppermute(weight, 'x', [((x + step) % 4, x) for x in range(4)])]
    pallas_call x7, Pallas kernels: 8.12 us -> 10.8 us  [call(): pl.pallas_call(kernel, out_shape=[jax.ShapeDtypeStruct(shape, out_dtype)...]
  transfers between devices with their start and end apart: 5 -> 7, of which waited for: 5 -> 4; matrix products, arithmetic and copies ran while one was open for 1% -> 0% of each run, Pallas kernels for 4% -> 3%
where the time goes in v2:
time: 122 us
  starting transfers between devices  52.2 us (43%)
  blocking collectives  39.2 us (32%)
  waiting for transfers between devices  14 us (11%)
  Pallas kernels  10.8 us (9%)
  local copies, waits for them, and re-layouts  5.01 us (4%)
    all_gather x1, blocking collectives, body(): weight = lax.all_gather(weight, ('frame', 'half'), axis=0, tiled=False)  39.2 us
    all_to_all x1, starting transfers between devices, body(): lax.all_to_all(packed.reshape(FRAMES, width, 3 * TMAX * HD), 'frame', 0,...  15.7 us
    all_to_all x1, starting transfers between devices, body(): mixed = lax.all_to_all(mixed, ('head', 'core'), 0, 0, tiled=True)  13.2 us
    pallas_call x7, Pallas kernels, call(): pl.pallas_call(kernel, out_shape=[jax.ShapeDtypeStruct(shape, out_dtype)...  10.8 us
    ppermute x3, starting transfers between devices, body(): lax.ppermute(weight, 'x', [((x + step) % 4, x) for x in range(4)])  10.7 us
    ppermute x3, waiting for transfers between devices, body(): lax.ppermute(weight, 'x', [((x + step) % 4, x) for x in range(4)])  10.6 us
    all_to_all x1, starting transfers between devices, body(): lax.all_to_all(attended.reshape(FRAMES, width, TMAX * HD), 'frame', 0, 0,...  8.99 us
    unnamed x24, local copies, waits for them, and re-layouts  5.01 us
  transfers between devices with their start and end apart: 7, of which 4 were waited for; matrix products, arithmetic and copies ran while one was open for 0% of the time, Pallas kernels for 3%

profile of v2, /device:TPU:1, one launch (start us, length us, event | category | flops | bytes accessed | tf_op | source)
XLA Modules:
  0.0 121.8 jit_solution(18232024385463525907)
XLA Ops:
  0.0 0.9 copy-done.2
  0.9 0.9 copy-done.4
  1.8 0.9 copy-done.6
  2.8 0.7 copy-done.8
  3.4 1.4 %shard_map.64 = bf16[128,1152]{1,0:T(8,128)(2,1)} custom-call(s32[1]{0:T(128)} %bitcast.1.group_ref, s32[20]{0:T(128)S(1)} %copy-done.8, bf16[128,640]{1,0:T(8,128)(2,1)S(1)} %copy-done.2, bf16[128,640]{1,0:T(8,128)(2,1)S(1)} %copy-done.4, bf16[128,640]{1,0:T(8,128)(2,1)S(1)} %copy-done.6), custom_call_target="tpu_custom_call" | custom-call | bytes 786516 | tf_op jit(solution)/shard_map/pallas_call | solution.py:158
  4.8 15.7 %all-to-all-start = ((bf16[8,16,1152]{2,1,0:T(8,128)(2,1)}), bf16[8,16,1152]{2,1,0:T(8,128)(2,1)S(1)}, u32[]{:S(2)}, u32[]{:S(2)}) async-start(bf16[8,16,1152]{2,1,0:T(8,128)(2,1)} %bitcast.2), calls=%async_computation | async-start | bytes 589824 | tf_op jit(solution)/shard_map/all_to_all | solution.py:187
  20.5 39.2 %all-gather.1.weight_ref = bf16[16,20,1280]{2,1,0:T(8,128)(2,1)S(1)} all-gather(bf16[1,20,1280]{2,1,0:T(8,128)(2,1)S(1)} %bitcast.9), channel_id=2, replica_groups=mesh['frame'=8,'half'=2,'x'=4,'core'=2,'head'=4] {'frame','half'}, dimensions={0}, use_global_device_ids=true | all-gather | bytes 870400 | tf_op jit(solution)/shard_map/all_gather | solution.py:186
  59.8 0.0 all-to-all-done
  59.8 1.7 %shard_map.65 = bf16[128,384]{1,0:T(8,128)(2,1)} custom-call(bf16[128,1152]{1,0:T(8,128)(2,1)S(1)} %bitcast.7), custom_call_target="tpu_custom_call" | custom-call | bytes 393216 | tf_op jit(solution)/shard_map/pallas_call | solution.py:158
  61.5 9.0 %all-to-all-start.1 = ((bf16[8,16,384]{2,1,0:T(8,128)(2,1)}), bf16[8,16,384]{2,1,0:T(8,128)(2,1)S(1)}, u32[]{:S(2)}, u32[]{:S(2)}) async-start(bf16[8,16,384]{2,1,0:T(8,128)(2,1)} %bitcast.5), calls=%async_computation.1 | async-start | bytes 196608 | tf_op jit(solution)/shard_map/all_to_all | solution.py:202
  70.5 0.0 copy-start.5
  70.5 0.0 copy-start.7
  70.5 0.0 copy-start.10
  70.5 0.1 shard_map.68.w0_ref
  70.6 0.0 copy-start.9
  70.7 3.2 %collective-permute-start.2 = (bf16[320,1280]{1,0:T(8,128)(2,1)S(1)}, bf16[320,1280]{1,0:T(8,128)(2,1)S(1)}, u32[]{:S(2)}, u32[]{:S(2)}) collective-permute-start(bf16[320,1280]{1,0:T(8,128)(2,1)S(1)} %shard_map.68.w0_ref), channel_id=1, source_target_pairs={{24,0},{0,8},{8,16},{16,24},{25,1},{1,9},{9,17},{17,25},{26,2},{2,... | collective-permute-start | bytes 2457608 | tf_op jit(solution)/shard_map/ppermute | solution.py:197
  73.9 4.4 %collective-permute-start.1 = (bf16[320,1280]{1,0:T(8,128)(2,1)S(1)}, bf16[320,1280]{1,0:T(8,128)(2,1)S(1)}, u32[]{:S(2)}, u32[]{:S(2)}) collective-permute-start(bf16[320,1280]{1,0:T(8,128)(2,1)S(1)} %shard_map.68.w0_ref), channel_id=1, source_target_pairs={{16,0},{24,8},{0,16},{8,24},{17,1},{25,9},{1,17},{9,25},{18,2},{26... | collective-permute-start | bytes 2457608 | tf_op jit(solution)/shard_map/ppermute | solution.py:197
  78.3 3.1 %collective-permute-start = (bf16[320,1280]{1,0:T(8,128)(2,1)S(1)}, bf16[320,1280]{1,0:T(8,128)(2,1)}, u32[]{:S(2)}, u32[]{:S(2)}) collective-permute-start(bf16[320,1280]{1,0:T(8,128)(2,1)S(1)} %shard_map.68.w0_ref), channel_id=1, source_target_pairs={{8,0},{16,8},{24,16},{0,24},{9,1},{17,9},{25,17},{1,25},{10,2},{18... | collective-permute-start | bytes 2457608 | tf_op jit(solution)/shard_map/ppermute | solution.py:197
  81.4 0.4 fusion.1.order_ref
  81.8 2.3 %shard_map.66.spatial_ref = bf16[128,640]{1,0:T(8,128)(2,1)S(1)} custom-call(s32[1,4]{1,0:T(1,128)S(1)} %copy-done.10, bf16[128,640]{1,0:T(8,128)(2,1)S(1)} %copy-done.3, bf16[128,640]{1,0:T(8,128)(2,1)S(1)} %copy-done.5, bf16[128,640]{1,0:T(8,128)(2,1)S(1)} %copy-done.7), custom_call_target="tpu_custom_call" | custom-call | bytes 655376 | tf_op jit(solution)/shard_map/pallas_call | solution.py:158
  84.1 0.0 copy-start
  84.1 0.7 copy-done
  84.7 0.9 copy-done.1
  85.6 1.9 %shard_map.67 = bf16[8,128,384]{2,1,0:T(8,128)(2,1)} custom-call(s32[1]{0:T(128)} %bitcast.1.group_ref, s32[20]{0:T(128)S(1)} %copy-done.9, bf16[128,640]{1,0:T(8,128)(2,1)S(1)} %copy-done.1, bf16[128,384]{1,0:T(8,128)(2,1)S(1)} %bitcast.8, bf16[640,768]{1,0:T(8,128)(2,1)S(1)} %fusion.1.order_ref), custom_call_target="tpu_custom_call" | custom-call | bytes 2031700 | tf_op jit(solution)/shard_map/pallas_call | solution.py:158
  87.5 13.2 %all-to-all-start.2 = ((bf16[8,128,384]{2,1,0:T(8,128)(2,1)}), bf16[8,128,384]{2,1,0:T(8,128)(2,1)S(1)}, u32[]{:S(2)}, u32[]{:S(2)}) async-start(bf16[8,128,384]{2,1,0:T(8,128)(2,1)} %shard_map.67), calls=%async_computation.2 | async-start | bytes 1572864 | tf_op jit(solution)/shard_map/all_to_all | solution.py:223
  100.7 3.6 %collective-permute-done.1.w2_ref = bf16[320,1280]{1,0:T(8,128)(2,1)S(1)} collective-permute-done((bf16[320,1280]{1,0:T(8,128)(2,1)S(1)}, bf16[320,1280]{1,0:T(8,128)(2,1)S(1)}, u32[]{:S(2)}, u32[]{:S(2)}) %collective-permute-start.1) | collective-permute-done | bytes 819232 | tf_op jit(solution)/shard_map/ppermute | solution.py:197
  104.3 6.9 %collective-permute-done.w1_ref = bf16[320,1280]{1,0:T(8,128)(2,1)} collective-permute-done((bf16[320,1280]{1,0:T(8,128)(2,1)S(1)}, bf16[320,1280]{1,0:T(8,128)(2,1)}, u32[]{:S(2)}, u32[]{:S(2)}) %collective-permute-start) | collective-permute-done | bytes 819232 | tf_op jit(solution)/shard_map/ppermute | solution.py:197
  111.2 1.7 %all-to-all-done.2.mixed_ref = bf16[8,128,384]{2,1,0:T(8,128)(2,1)S(1)} async-done(((bf16[8,128,384]{2,1,0:T(8,128)(2,1)}), bf16[8,128,384]{2,1,0:T(8,128)(2,1)S(1)}, u32[]{:S(2)}, u32[]{:S(2)}) %all-to-all-start.2) | async-done | bytes 786464 | tf_op jit(solution)/shard_map/all_to_all | solution.py:223
  113.0 2.6 %shard_map.69 = (f32[128,1280]{1,0:T(8,128)S(1)}, f32[128,1280]{1,0:T(8,128)S(1)}) custom-call(s32[1]{0:T(128)} %bitcast.core_ref, bf16[8,128,384]{2,1,0:T(8,128)(2,1)S(1)} %all-to-all-done.2.mixed_ref, bf16[320,1280]{1,0:T(8,128)(2,1)S(1)} %shard_map.68.w0_ref, bf16[320,1280]{1,0:T(8,128)(2,1)} %collective-permute-done.w1_ref, ...), custom_call_target="tpu_custom_call" | custom-call | flops 838860800 | bytes 5373956 | tf_op jit(solution)/shard_map/pallas_call | solution.py:158
  115.6 3.7 %collective-permute-start.3 = (f32[128,1280]{1,0:T(8,128)S(1)}, f32[128,1280]{1,0:T(8,128)S(1)}, u32[]{:S(2)}, u32[]{:S(2)}) collective-permute-start(f32[128,1280]{1,0:T(8,128)S(1)} %get-tuple-element.26), channel_id=1, source_target_pairs={{0,4},{4,0},{1,5},{5,1},{2,6},{6,2},{3,7},{7,3},{8,12},{12,8},{9,1... | collective-permute-start | bytes 1966088 | tf_op jit(solution)/shard_map/ppermute | solution.py:235
  119.3 1.7 %collective-permute-done.3.arrived_ref = f32[128,1280]{1,0:T(8,128)S(1)} collective-permute-done((f32[128,1280]{1,0:T(8,128)S(1)}, f32[128,1280]{1,0:T(8,128)S(1)}, u32[]{:S(2)}, u32[]{:S(2)}) %collective-permute-start.3) | collective-permute-done | bytes 655392 | tf_op jit(solution)/shard_map/ppermute | solution.py:235
  121.0 0.8 shard_map.70
  (17 shorter events, 0.1 us)
Async XLA Ops:
  0.0 0.9 copy-start.2
  0.9 0.9 copy-start.4
  1.8 0.9 copy-start.6
  2.7 0.7 copy-start.8
  3.4 17.1 %copy-start.11 = (bf16[20,1280]{1,0:T(8,128)(2,1)S(1)}, bf16[20,1280]{1,0:T(8,128)(2,1)}, u32[]{:S(2)}) copy-start(bf16[20,1280]{1,0:T(8,128)(2,1)} %param.11) | copy-start | bytes 153604
  4.8 54.9 %all-to-all-start = ((bf16[8,16,1152]{2,1,0:T(8,128)(2,1)}), bf16[8,16,1152]{2,1,0:T(8,128)(2,1)S(1)}, u32[]{:S(2)}, u32[]{:S(2)}) async-start(bf16[8,16,1152]{2,1,0:T(8,128)(2,1)} %bitcast.2), calls=%async_computation | async-start | bytes 589824 | tf_op jit(solution)/shard_map/all_to_all | solution.py:187
  61.5 23.2 %all-to-all-start.1 = ((bf16[8,16,384]{2,1,0:T(8,128)(2,1)}), bf16[8,16,384]{2,1,0:T(8,128)(2,1)S(1)}, u32[]{:S(2)}, u32[]{:S(2)}) async-start(bf16[8,16,384]{2,1,0:T(8,128)(2,1)} %bitcast.5), calls=%async_computation.1 | async-start | bytes 196608 | tf_op jit(solution)/shard_map/all_to_all | solution.py:202
  70.5 11.3 %copy-start.3 = (bf16[128,640]{1,0:T(8,128)(2,1)S(1)}, bf16[128,640]{1,0:T(8,128)(2,1)}, u32[]{:S(2)}) copy-start(bf16[128,640]{1,0:T(8,128)(2,1)} %q_ref.2) | copy-start | bytes 491524
  70.5 11.3 %copy-start.5 = (bf16[128,640]{1,0:T(8,128)(2,1)S(1)}, bf16[128,640]{1,0:T(8,128)(2,1)}, u32[]{:S(2)}) copy-start(bf16[128,640]{1,0:T(8,128)(2,1)} %k_ref.2) | copy-start | bytes 491524
  70.5 11.3 %copy-start.7 = (bf16[128,640]{1,0:T(8,128)(2,1)S(1)}, bf16[128,640]{1,0:T(8,128)(2,1)}, u32[]{:S(2)}) copy-start(bf16[128,640]{1,0:T(8,128)(2,1)} %v_ref.2) | copy-start | bytes 491524
  70.5 11.3 %copy-start.10 = (s32[1,4]{1,0:T(1,128)S(1)}, s32[1,4]{1,0:T(1,128)}, u32[]{:S(2)}) copy-start(s32[1,4]{1,0:T(1,128)} %lengths_ref.1) | copy-start | bytes 52
  70.6 14.1 %copy-start.9 = (s32[20]{0:T(128)S(1)}, s32[20]{0:T(128)}, u32[]{:S(2)}) copy-start(s32[20]{0:T(128)} %classes_ref.3) | copy-start | bytes 244
  70.7 30.0 %collective-permute-start.2 = (bf16[320,1280]{1,0:T(8,128)(2,1)S(1)}, bf16[320,1280]{1,0:T(8,128)(2,1)S(1)}, u32[]{:S(2)}, u32[]{:S(2)}) collective-permute-start(bf16[320,1280]{1,0:T(8,128)(2,1)S(1)} %shard_map.68.w0_ref), channel_id=1, source_target_pairs={{24,0},{0,8},{8,16},{16,24},{25,1},{1,9},{9,17},{17,25},{26,2},{2,... | collective-permute-start | bytes 2457608 | tf_op jit(solution)/shard_map/ppermute | solution.py:197
  73.9 30.4 %collective-permute-start.1 = (bf16[320,1280]{1,0:T(8,128)(2,1)S(1)}, bf16[320,1280]{1,0:T(8,128)(2,1)S(1)}, u32[]{:S(2)}, u32[]{:S(2)}) collective-permute-start(bf16[320,1280]{1,0:T(8,128)(2,1)S(1)} %shard_map.68.w0_ref), channel_id=1, source_target_pairs={{16,0},{24,8},{0,16},{8,24},{17,1},{25,9},{1,17},{9,25},{18,2},{26... | collective-permute-start | bytes 2457608 | tf_op jit(solution)/shard_map/ppermute | solution.py:197
  78.3 33.0 %collective-permute-start = (bf16[320,1280]{1,0:T(8,128)(2,1)S(1)}, bf16[320,1280]{1,0:T(8,128)(2,1)}, u32[]{:S(2)}, u32[]{:S(2)}) collective-permute-start(bf16[320,1280]{1,0:T(8,128)(2,1)S(1)} %shard_map.68.w0_ref), channel_id=1, source_target_pairs={{8,0},{16,8},{24,16},{0,24},{9,1},{17,9},{25,17},{1,25},{10,2},{18... | collective-permute-start | bytes 2457608 | tf_op jit(solution)/shard_map/ppermute | solution.py:197
  84.1 0.7 copy-start
  84.7 0.9 copy-start.1
  87.5 25.5 %all-to-all-start.2 = ((bf16[8,128,384]{2,1,0:T(8,128)(2,1)}), bf16[8,128,384]{2,1,0:T(8,128)(2,1)S(1)}, u32[]{:S(2)}, u32[]{:S(2)}) async-start(bf16[8,128,384]{2,1,0:T(8,128)(2,1)} %shard_map.67), calls=%async_computation.2 | async-start | bytes 1572864 | tf_op jit(solution)/shard_map/all_to_all | solution.py:223
  115.6 5.4 %collective-permute-start.3 = (f32[128,1280]{1,0:T(8,128)S(1)}, f32[128,1280]{1,0:T(8,128)S(1)}, u32[]{:S(2)}, u32[]{:S(2)}) collective-permute-start(f32[128,1280]{1,0:T(8,128)S(1)} %get-tuple-element.26), channel_id=1, source_target_pairs={{0,4},{4,0},{1,5},{5,1},{2,6},{6,2},{3,7},{7,3},{8,12},{12,8},{9,1... | collective-permute-start | bytes 1966088 | tf_op jit(solution)/shard_map/ppermute | solution.py:235

commit v3 on v2

--- a/solution.py
+++ b/solution.py
@@ -14,13 +14,13 @@
 TOK = 128
 LOCAL = 5
 COLS = LOCAL * HD
-PART = 384
 SCALE = 1.0 / math.sqrt(HD)
-TOKEN_AXES = ("frame", "half", "x", "core")
+FRAME_AXES = ("far", "near")
+Z_AXES = ("far", "near", "half")
+TOKEN_AXES = Z_AXES + ("x", "core")
 VMEM = pl.BlockSpec(memory_space=pltpu.VMEM)
 SMEM = pl.BlockSpec(memory_space=pltpu.SMEM)
 HBM = pl.BlockSpec(memory_space=pltpu.HBM)
-PARAMS = pltpu.CompilerParams(vmem_limit_bytes=16 * 1024 * 1024)
 
 
 def columns(head):
@@ -72,7 +72,17 @@
     ).astype(jnp.bfloat16)
 
 
-def window_kernel(lengths_ref, q_ref, k_ref, v_ref, out_ref):
+def window_kernel(lengths_ref, q_hbm, k_hbm, v_hbm, out_ref, q_ref, k_ref, v_ref, sems):
+    copies = [
+        pltpu.make_async_copy(source, target, sems.at[place])
+        for place, (source, target) in enumerate(
+            ((q_hbm, q_ref), (k_hbm, k_ref), (v_hbm, v_ref))
+        )
+    ]
+    for copy in copies:
+        copy.start()
+    for copy in copies:
+        copy.wait()
     rows = lax.broadcasted_iota(jnp.int32, (TOK, TOK), 0)
     cols = lax.broadcasted_iota(jnp.int32, (TOK, TOK), 1)
     row_id = jnp.zeros((TOK, TOK), jnp.int32)
@@ -88,11 +98,12 @@
         out_ref[:, span] = attend(q_ref[:, span], k_ref[:, span], v_ref[:, span], same)
 
 
-def frame_kernel(packed_ref, out_ref):
+def frame_kernel(packed_ref, out_ref, mark_ref):
     width = TOK // FRAMES
     rows = lax.broadcasted_iota(jnp.int32, (TOK, TOK), 0)
     cols = lax.broadcasted_iota(jnp.int32, (TOK, TOK), 1)
     same = (rows & (width - 1)) == (cols & (width - 1))
+    mark_ref[...] = packed_ref[:16, :HD]
     for slot in range(TMAX):
         span = [
             slice((part * TMAX + slot) * HD, (part * TMAX + slot + 1) * HD) for part in range(3)
@@ -117,8 +128,7 @@
     ordered = jnp.dot(mixed[...], order_ref[...], preferred_element_type=jnp.float32)
     ordered = ordered.astype(jnp.bfloat16)
     for copy in range(4):
-        for core in range(2):
-            out_ref[2 * copy + core] = ordered[:, core * PART : (core + 1) * PART]
+        out_ref[copy] = ordered
 
 
 def rows_kernel(weight_ref, out_ref):
@@ -128,30 +138,20 @@
         )
 
 
-def project_kernel(core_ref, mixed_ref, w0_ref, w1_ref, w2_ref, w3_ref, own_ref, other_ref):
-    core = core_ref[0]
-    zeros = jnp.zeros((PART - 320, 2 * COLS), jnp.bfloat16)
-    total = jnp.zeros((2 * TOK, 2 * COLS), jnp.float32)
+def project_kernel(mixed_ref, mark_ref, *refs):
+    slabs, out_ref = refs[:8], refs[8]
+    total = jnp.zeros((TOK, 2 * COLS), jnp.float32)
     for group in range(4):
-        span = slice(group * 80, (group + 1) * 80)
-        rows = [w[span, :] for w in (w0_ref, w1_ref, w2_ref, w3_ref)]
-        tokens = jnp.concatenate(
-            [mixed_ref[2 * group + core], mixed_ref[2 * group + 1 - core]], axis=0
-        )
+        rows = [slab[group * 80 : (group + 1) * 80, :] for slab in slabs]
         total = total + jnp.dot(
-            tokens,
-            jnp.concatenate(rows + [zeros], axis=0),
+            mixed_ref[group],
+            jnp.concatenate(rows, axis=0),
             preferred_element_type=jnp.float32,
         )
-    own_ref[...] = total[:TOK]
-    other_ref[...] = total[TOK:]
-
-
-def sum_kernel(own_ref, arrived_ref, out_ref):
-    out_ref[...] = (own_ref[...] + arrived_ref[...]).astype(jnp.bfloat16)
-
-
-def call(kernel, out_shape, specs, *args, scratch=(), flops=0, out_dtype=jnp.bfloat16):
+    out_ref[...] = total.astype(jnp.bfloat16)
+
+
+def call(kernel, out_shape, specs, *args, scratch=(), flops=0, out_dtype=jnp.bfloat16, vmem=16):
     shapes = out_shape if isinstance(out_shape, list) else [out_shape]
     size = sum(a.size * a.dtype.itemsize for a in args)
     size += sum(math.prod(shape) * jnp.dtype(out_dtype).itemsize for shape in shapes)
@@ -161,14 +161,14 @@
         in_specs=specs,
         out_specs=[VMEM] * len(shapes),
         scratch_shapes=scratch,
-        compiler_params=PARAMS,
+        compiler_params=pltpu.CompilerParams(vmem_limit_bytes=vmem << 20),
         cost_estimate=pl.CostEstimate(flops=flops, bytes_accessed=size, transcendentals=0),
     )(*args)
     return results if isinstance(out_shape, list) else results[0]
 
 
 def body(queries, keys, values, head_class, window_lengths, out_weight):
-    core = lax.axis_index("core").astype(jnp.int32).reshape(1)
+    core = lax.axis_index("core")
     group = lax.axis_index("head").astype(jnp.int32).reshape(1)
     width = TOK // FRAMES
     packed = call(
@@ -181,37 +181,44 @@
         keys,
         values,
         scratch=[pltpu.SemaphoreType.DMA((3 * TMAX,))],
-    )
-    packed, weight = lax.optimization_barrier((packed, out_weight))
-    weight = lax.all_gather(weight, ("frame", "half"), axis=0, tiled=False)
+        vmem=60,
+    )
+    weight = lax.all_gather(out_weight, Z_AXES, axis=0, tiled=False)
+    packed, weight = lax.optimization_barrier((packed, weight))
     packed = lax.all_to_all(
-        packed.reshape(FRAMES, width, 3 * TMAX * HD), "frame", 0, 0, tiled=True
+        packed.reshape(FRAMES, width, 3 * TMAX * HD), FRAME_AXES, 0, 0, tiled=True
     ).reshape(TOK, 3 * TMAX * HD)
-    packed, weight = lax.optimization_barrier((packed, weight))
-    attended = call(frame_kernel, (TOK, TMAX * HD), [VMEM], packed)
-    attended, weight, queries, keys, values = lax.optimization_barrier(
-        (attended, weight, queries, keys, values)
-    )
     weight = call(rows_kernel, (320, 2 * COLS), [VMEM], weight)
     around = [
         lax.ppermute(weight, "x", [((x + step) % 4, x) for x in range(4)]) for step in (1, 2, 3)
     ]
+    attended, mark = call(frame_kernel, [(TOK, TMAX * HD), (16, HD)], [VMEM], packed)
     spatial = call(
-        window_kernel, (TOK, COLS), [SMEM] + [VMEM] * 3, window_lengths, queries, keys, values
-    )
+        window_kernel,
+        (TOK, COLS),
+        [SMEM] + [HBM] * 3,
+        window_lengths,
+        queries,
+        keys,
+        values,
+        scratch=[pltpu.VMEM((TOK, COLS), jnp.bfloat16)] * 3 + [pltpu.SemaphoreType.DMA((3,))],
+    )
+    mark, weight, around = lax.optimization_barrier((mark, weight, around))
+    swap = [(0, 1), (1, 0)]
+    slabs = [weight, *around]
+    slabs = slabs + [lax.ppermute(slab, "core", swap) for slab in slabs]
     attended = lax.all_to_all(
-        attended.reshape(FRAMES, width, TMAX * HD), "frame", 0, 0, tiled=True
+        attended.reshape(FRAMES, width, TMAX * HD), FRAME_AXES, 0, 0, tiled=True
     ).reshape(TOK, TMAX * HD)
 
     source = jnp.arange(COLS, dtype=jnp.int32)[:, None]
-    place = jnp.arange(2 * PART, dtype=jnp.int32)[None, :]
-    rest = place % PART
-    owner = (lax.axis_index("x") + rest // 80) % 4
-    wanted = rest % 80 // 20 * 160 + owner * 40 + place // PART * 20 + rest % 20
-    order = ((source == wanted) & (rest < 320)).astype(jnp.bfloat16)
+    place = jnp.arange(COLS, dtype=jnp.int32)[None, :]
+    owner = (lax.axis_index("x") + place // 80) % 4 * 2 + (core + place // 320) % 2
+    wanted = place % 80 // 20 * 160 + owner * 20 + place % 20
+    order = (source == wanted).astype(jnp.bfloat16)
     mixed = call(
         mix_kernel,
-        (8, TOK, PART),
+        (4, TOK, COLS),
         [SMEM] * 2 + [VMEM] * 3,
         group,
         head_class,
@@ -220,24 +227,20 @@
         order,
         scratch=[pltpu.VMEM((TOK, COLS), jnp.bfloat16)],
     )
-    mixed = lax.all_to_all(mixed, ("head", "core"), 0, 0, tiled=True)
-    own, other = call(
+    mixed = lax.all_to_all(mixed, "head", 0, 0, tiled=True)
+    return call(
         project_kernel,
-        [(TOK, 2 * COLS)] * 2,
-        [SMEM] + [VMEM] * 5,
-        core,
+        (TOK, 2 * COLS),
+        [VMEM] * 10,
         mixed,
-        weight,
-        *around,
+        mark,
+        *slabs,
         flops=2 * TOK * 2560 * 1280,
-        out_dtype=jnp.float32,
-    )
-    arrived = lax.ppermute(other, "core", [(0, 1), (1, 0)])
-    return call(sum_kernel, (TOK, 2 * COLS), [VMEM] * 2, own, arrived)
+    )
 
 
 def solution(mesh):
-    mesh = Mesh(mesh.devices.reshape(8, 2, 4, 2, 4), TOKEN_AXES + ("head",))
+    mesh = Mesh(mesh.devices.reshape(4, 2, 2, 4, 2, 4), TOKEN_AXES + ("head",))
     split = P(TOKEN_AXES, "head")
     placed = (split, split, split, P(), P(TOKEN_AXES, None), split)
     return jax.shard_map(body, mesh=mesh, in_specs=placed, out_specs=split, check_vma=False)

time: 122 us -> 119 us (0.975); the launches traced: 122 us -> 117 us
  waiting for transfers between devices: 14 us -> 26.1 us
  starting transfers between devices: 52.2 us -> 42 us
  local copies, waits for them, and re-layouts: 5.01 us -> 0.03 us
  blocking collectives: 39.2 us -> 35.3 us
  Pallas kernels: 10.8 us -> 13.2 us
    all_to_all x3, starting transfers between devices: 37.8 us -> 19.6 us  [the longest x1 9.12 us: body(): lax.all_to_all(attended.reshape(FRAMES, width, TMAX * HD), FRAME_AXES, 0,...]
    all_to_all x3, waiting for transfers between devices: 1.74 us -> 12.5 us  [the longest x1 10.1 us: body(): mixed = lax.all_to_all(mixed, 'head', 0, 0, tiled=True)]
    ppermute x1 -> x4, starting transfers between devices: 3.69 us -> 11.7 us  [body(): slabs = slabs + [lax.ppermute(slab, 'core', swap) for slab in slabs]]
    unnamed x24 -> x10, local copies, waits for them, and re-layouts: 5.01 us -> 0.03 us
    all_gather x1, blocking collectives: 39.2 us -> 35.3 us  [body(): weight = lax.all_gather(out_weight, Z_AXES, axis=0, tiled=False)]
    ppermute x3, waiting for transfers between devices: 10.6 us -> 13.7 us  [body(): lax.ppermute(weight, 'x', [((x + step) % 4, x) for x in range(4)])]
    pallas_call x7 -> x6, Pallas kernels: 10.8 us -> 13.2 us  [call(): pl.pallas_call(kernel, out_shape=[jax.ShapeDtypeStruct(shape, out_dtype)...]
    ppermute x1 -> x4, waiting for transfers between devices: 1.7 us -> 0.01 us  [body(): slabs = slabs + [lax.ppermute(slab, 'core', swap) for slab in slabs]]
  transfers between devices with their start and end apart: 7 -> 10, of which waited for: 4 -> 4; matrix products, arithmetic and copies ran while one was open for 0% -> 0% of each run, Pallas kernels for 3% -> 6%
where the time goes in v3:
time: 119 us; the launch traced here: 117 us
  starting transfers between devices  42 us (35%)
  blocking collectives  35.3 us (30%)
  waiting for transfers between devices  26.1 us (22%)
  Pallas kernels  13.2 us (11%)
    all_gather x1, blocking collectives, body(): weight = lax.all_gather(out_weight, Z_AXES, axis=0, tiled=False)  35.3 us
    ppermute x3, waiting for transfers between devices, body(): lax.ppermute(weight, 'x', [((x + step) % 4, x) for x in range(4)])  13.7 us
    pallas_call x6, Pallas kernels, call(): pl.pallas_call(kernel, out_shape=[jax.ShapeDtypeStruct(shape, out_dtype)...  13.2 us
    ppermute x4, starting transfers between devices, body(): slabs = slabs + [lax.ppermute(slab, 'core', swap) for slab in slabs]  11.7 us
    ppermute x3, starting transfers between devices, body(): lax.ppermute(weight, 'x', [((x + step) % 4, x) for x in range(4)])  10.7 us
    all_to_all x1, waiting for transfers between devices, body(): mixed = lax.all_to_all(mixed, 'head', 0, 0, tiled=True)  10.1 us
    all_to_all x1, starting transfers between devices, body(): lax.all_to_all(attended.reshape(FRAMES, width, TMAX * HD), FRAME_AXES, 0,...  9.12 us
    all_to_all x1, starting transfers between devices, body(): lax.all_to_all(packed.reshape(FRAMES, width, 3 * TMAX * HD), FRAME_AXES,...  6.27 us
  transfers between devices with their start and end apart: 10, of which 4 were waited for; matrix products, arithmetic and copies ran while one was open for 0% of the time, Pallas kernels for 6%

profile of v3, /device:TPU:1, one launch (start us, length us, event | category | flops | bytes accessed | tf_op | source)
XLA Modules:
  0.0 117.1 jit_solution(3965402304431430565)
XLA Ops:
  0.0 35.3 %all-gather.1.weight_ref = bf16[16,20,1280]{2,1,0:T(8,128)(2,1)S(1)} all-gather(bf16[1,20,1280]{2,1,0:T(8,128)(2,1)} %bitcast.9), channel_id=2, replica_groups=mesh['far'=4,'near'=2,'half'=2,'x'=4,'core'=2,'head'=4] {'far','near','h..., dimensions={0}, use_global_device_ids=true | all-gather | bytes 870400 | tf_op jit(solution)/shard_map/all_gather | solution.py:186
  35.3 2.4 %shard_map.65 = bf16[128,1152]{1,0:T(8,128)(2,1)} custom-call(s32[1]{0:T(128)} %bitcast.group_ref, s32[20]{0:T(128)} %classes_ref.3, bf16[128,640]{1,0:T(8,128)(2,1)} %q_ref.1, bf16[128,640]{1,0:T(8,128)(2,1)} %k_ref.1, bf16[128,640]{1,0:T(8,128)(2,1)} %v_ref.1), custom_call_target="tpu_custom_call" | custom-call | bytes 786516 | tf_op jit(solution)/shard_map/pallas_call | solution.py:158
  37.6 6.3 %all-to-all-start = ((bf16[8,16,1152]{2,1,0:T(8,128)(2,1)}), bf16[8,16,1152]{2,1,0:T(8,128)(2,1)S(1)}, u32[]{:S(2)}, u32[]{:S(2)}) async-start(bf16[8,16,1152]{2,1,0:T(8,128)(2,1)} %bitcast.8), calls=%async_computation | async-start | bytes 589824 | tf_op jit(solution)/shard_map/all_to_all | solution.py:188
  43.9 0.0 copy-start.1
  43.9 0.0 copy-start.2
  44.0 0.0 copy-start.4
  44.0 0.1 shard_map.68.refs_0_
  44.1 3.3 %collective-permute-start.2 = (bf16[320,1280]{1,0:T(8,128)(2,1)S(1)}, bf16[320,1280]{1,0:T(8,128)(2,1)S(1)}, u32[]{:S(2)}, u32[]{:S(2)}) collective-permute-start(bf16[320,1280]{1,0:T(8,128)(2,1)S(1)} %shard_map.68.refs_0_), channel_id=1, source_target_pairs={{24,0},{0,8},{8,16},{16,24},{25,1},{1,9},{9,17},{17,25},{26,2},{2,... | collective-permute-start | bytes 2457608 | tf_op jit(solution)/shard_map/ppermute | solution.py:193
  47.3 4.4 %collective-permute-start.1 = (bf16[320,1280]{1,0:T(8,128)(2,1)S(1)}, bf16[320,1280]{1,0:T(8,128)(2,1)}, u32[]{:S(2)}, u32[]{:S(2)}) collective-permute-start(bf16[320,1280]{1,0:T(8,128)(2,1)S(1)} %shard_map.68.refs_0_), channel_id=1, source_target_pairs={{16,0},{24,8},{0,16},{8,24},{17,1},{25,9},{1,17},{9,25},{18,2},{26... | collective-permute-start | bytes 2457608 | tf_op jit(solution)/shard_map/ppermute | solution.py:193
  51.7 3.1 %collective-permute-start = (bf16[320,1280]{1,0:T(8,128)(2,1)S(1)}, bf16[320,1280]{1,0:T(8,128)(2,1)}, u32[]{:S(2)}, u32[]{:S(2)}) collective-permute-start(bf16[320,1280]{1,0:T(8,128)(2,1)S(1)} %shard_map.68.refs_0_), channel_id=1, source_target_pairs={{8,0},{16,8},{24,16},{0,24},{9,1},{17,9},{25,17},{1,25},{10,2},{18... | collective-permute-start | bytes 2457608 | tf_op jit(solution)/shard_map/ppermute | solution.py:193
  54.8 0.0 copy-start.3
  54.8 2.9 %shard_map.64.spatial_ref = bf16[128,640]{1,0:T(8,128)(2,1)S(1)} custom-call(s32[1,4]{1,0:T(1,128)S(1)} %copy-done.4, bf16[128,640]{1,0:T(8,128)(2,1)S(1)} %copy-done, bf16[128,640]{1,0:T(8,128)(2,1)S(1)} %copy-done.1, bf16[128,640]{1,0:T(8,128)(2,1)S(1)} %copy-done.2), custom_call_target="tpu_custom_call" | custom-call | bytes 655376 | tf_op jit(solution)/shard_map/pallas_call | solution.py:158
  57.8 2.3 %all-to-all-done = bf16[8,16,1152]{2,1,0:T(8,128)(2,1)S(1)} async-done(((bf16[8,16,1152]{2,1,0:T(8,128)(2,1)}), bf16[8,16,1152]{2,1,0:T(8,128)(2,1)S(1)}, u32[]{:S(2)}, u32[]{:S(2)}) %all-to-all-start) | async-done | bytes 294944 | tf_op jit(solution)/shard_map/all_to_all | solution.py:188
  60.1 1.7 %shard_map.66 = (bf16[128,384]{1,0:T(8,128)(2,1)}, bf16[16,128]{1,0:T(8,128)(2,1)S(1)}) custom-call(bf16[128,1152]{1,0:T(8,128)(2,1)S(1)} %bitcast.6), custom_call_target="tpu_custom_call" | custom-call | bytes 397312 | tf_op jit(solution)/shard_map/pallas_call | solution.py:158
  61.8 9.1 %all-to-all-start.1 = ((bf16[8,16,384]{2,1,0:T(8,128)(2,1)}), bf16[8,16,384]{2,1,0:T(8,128)(2,1)S(1)}, u32[]{:S(2)}, u32[]{:S(2)}) async-start(bf16[8,16,384]{2,1,0:T(8,128)(2,1)} %bitcast.4), calls=%async_computation.1 | async-start | bytes 196608 | tf_op jit(solution)/shard_map/all_to_all | solution.py:210
  70.9 0.0 collective-permute-done.2.refs_3_
  70.9 6.8 %collective-permute-done.1.refs_2_ = bf16[320,1280]{1,0:T(8,128)(2,1)} collective-permute-done((bf16[320,1280]{1,0:T(8,128)(2,1)S(1)}, bf16[320,1280]{1,0:T(8,128)(2,1)}, u32[]{:S(2)}, u32[]{:S(2)}) %collective-permute-start.1) | collective-permute-done | bytes 819232 | tf_op jit(solution)/shard_map/ppermute | solution.py:193
  77.8 6.8 %collective-permute-done.refs_1_ = bf16[320,1280]{1,0:T(8,128)(2,1)} collective-permute-done((bf16[320,1280]{1,0:T(8,128)(2,1)S(1)}, bf16[320,1280]{1,0:T(8,128)(2,1)}, u32[]{:S(2)}, u32[]{:S(2)}) %collective-permute-start) | collective-permute-done | bytes 819232 | tf_op jit(solution)/shard_map/ppermute | solution.py:193
  84.6 5.5 %collective-permute-start.3 = (bf16[320,1280]{1,0:T(8,128)(2,1)S(1)}, bf16[320,1280]{1,0:T(8,128)(2,1)}, u32[]{:S(2)}, u32[]{:S(2)}) collective-permute-start(bf16[320,1280]{1,0:T(8,128)(2,1)S(1)} %shard_map.68.refs_0_), channel_id=1, source_target_pairs={{0,4},{4,0},{1,5},{5,1},{2,6},{6,2},{3,7},{7,3},{8,12},{12,8},{9,1... | collective-permute-start | bytes 2457608 | tf_op jit(solution)/shard_map/ppermute | solution.py:209
  90.1 1.9 %collective-permute-start.4 = (bf16[320,1280]{1,0:T(8,128)(2,1)}, bf16[320,1280]{1,0:T(8,128)(2,1)}, u32[]{:S(2)}, u32[]{:S(2)}) collective-permute-start(bf16[320,1280]{1,0:T(8,128)(2,1)} %collective-permute-done.refs_1_), channel_id=1, source_target_pairs={{0,4},{4,0},{1,5},{5,1},{2,6},{6,2},{3,7},{7,3},{8,12},{12,8},{9,1... | collective-permute-start | bytes 2457608 | tf_op jit(solution)/shard_map/ppermute | solution.py:209
  92.0 2.4 %collective-permute-start.5 = (bf16[320,1280]{1,0:T(8,128)(2,1)}, bf16[320,1280]{1,0:T(8,128)(2,1)}, u32[]{:S(2)}, u32[]{:S(2)}) collective-permute-start(bf16[320,1280]{1,0:T(8,128)(2,1)} %collective-permute-done.1.refs_2_), channel_id=1, source_target_pairs={{0,4},{4,0},{1,5},{5,1},{2,6},{6,2},{3,7},{7,3},{8,12},{12,8},{9,1... | collective-permute-start | bytes 2457608 | tf_op jit(solution)/shard_map/ppermute | solution.py:209
  94.4 1.9 %collective-permute-start.6 = (bf16[320,1280]{1,0:T(8,128)(2,1)S(1)}, bf16[320,1280]{1,0:T(8,128)(2,1)}, u32[]{:S(2)}, u32[]{:S(2)}) collective-permute-start(bf16[320,1280]{1,0:T(8,128)(2,1)S(1)} %collective-permute-done.2.refs_3_), channel_id=1, source_target_pairs={{0,4},{4,0},{1,5},{5,1},{2,6},{6,2},{3,7},{7,3},{8,12},{12,8},{9,1... | collective-permute-start | bytes 2457608 | tf_op jit(solution)/shard_map/ppermute | solution.py:209
  96.4 0.2 fusion.order_ref
  96.6 0.0 all-to-all-done.1
  96.6 1.8 %shard_map.67 = bf16[4,128,640]{2,1,0:T(8,128)(2,1)} custom-call(s32[1]{0:T(128)} %bitcast.group_ref, s32[20]{0:T(128)S(1)} %copy-done.3, bf16[128,640]{1,0:T(8,128)(2,1)S(1)} %shard_map.64.spatial_ref, bf16[128,384]{1,0:T(8,128)(2,1)S(1)} %bitcast.7, bf16[640,640]{1,0:T(8,128)(2,1)S(1)} %fusion.order_ref), custom_call_target="tpu_custom_call" | custom-call | bytes 1736788 | tf_op jit(solution)/shard_map/pallas_call | solution.py:158
  98.4 4.2 %all-to-all-start.2 = ((bf16[4,128,640]{2,1,0:T(8,128)(2,1)}), bf16[4,128,640]{2,1,0:T(8,128)(2,1)S(1)}, u32[]{:S(2)}, u32[]{:S(2)}) async-start(bf16[4,128,640]{2,1,0:T(8,128)(2,1)} %shard_map.67), calls=%async_computation.2 | async-start | bytes 1310720 | tf_op jit(solution)/shard_map/all_to_all | solution.py:230
  102.6 0.0 collective-permute-done.3.refs_4_
  102.6 0.0 collective-permute-done.4.refs_5_
  102.6 0.0 collective-permute-done.5.refs_6_
  102.6 0.0 collective-permute-done.6.refs_7_
  102.7 10.1 %all-to-all-done.2.mixed_ref = bf16[4,128,640]{2,1,0:T(8,128)(2,1)S(1)} async-done(((bf16[4,128,640]{2,1,0:T(8,128)(2,1)}), bf16[4,128,640]{2,1,0:T(8,128)(2,1)S(1)}, u32[]{:S(2)}, u32[]{:S(2)}) %all-to-all-start.2) | async-done | bytes 655392 | tf_op jit(solution)/shard_map/all_to_all | solution.py:230
  112.8 4.3 %shard_map.69 = bf16[128,1280]{1,0:T(8,128)(2,1)} custom-call(bf16[4,128,640]{2,1,0:T(8,128)(2,1)S(1)} %all-to-all-done.2.mixed_ref, bf16[16,128]{1,0:T(8,128)(2,1)S(1)} %get-tuple-element.18.mark_ref, bf16[320,1280]{1,0:T(8,128)(2,1)S(1)} %shard_map.68.refs_0_, bf16[320,1280]{1,0:T(8,128)(2,1)} %collective-permute-done.refs_1_, ...), custom_call_target="tpu_custom_call" | custom-call | flops 838860800 | bytes 7540736 | tf_op jit(solution)/shard_map/pallas_call | solution.py:158
  (7 shorter events, 0.0 us)
Async XLA Ops:
  37.6 22.4 %all-to-all-start = ((bf16[8,16,1152]{2,1,0:T(8,128)(2,1)}), bf16[8,16,1152]{2,1,0:T(8,128)(2,1)S(1)}, u32[]{:S(2)}, u32[]{:S(2)}) async-start(bf16[8,16,1152]{2,1,0:T(8,128)(2,1)} %bitcast.8), calls=%async_computation | async-start | bytes 589824 | tf_op jit(solution)/shard_map/all_to_all | solution.py:188
  43.9 10.9 %copy-start = (bf16[128,640]{1,0:T(8,128)(2,1)S(1)}, bf16[128,640]{1,0:T(8,128)(2,1)}, u32[]{:S(2)}) copy-start(bf16[128,640]{1,0:T(8,128)(2,1)} %q_ref.1) | copy-start | bytes 491524
  43.9 10.9 %copy-start.1 = (bf16[128,640]{1,0:T(8,128)(2,1)S(1)}, bf16[128,640]{1,0:T(8,128)(2,1)}, u32[]{:S(2)}) copy-start(bf16[128,640]{1,0:T(8,128)(2,1)} %k_ref.1) | copy-start | bytes 491524
  43.9 10.9 %copy-start.2 = (bf16[128,640]{1,0:T(8,128)(2,1)S(1)}, bf16[128,640]{1,0:T(8,128)(2,1)}, u32[]{:S(2)}) copy-start(bf16[128,640]{1,0:T(8,128)(2,1)} %v_ref.1) | copy-start | bytes 491524
  44.0 10.9 %copy-start.4 = (s32[1,4]{1,0:T(1,128)S(1)}, s32[1,4]{1,0:T(1,128)}, u32[]{:S(2)}) copy-start(s32[1,4]{1,0:T(1,128)} %lengths_ref.1) | copy-start | bytes 52
  44.1 26.9 %collective-permute-start.2 = (bf16[320,1280]{1,0:T(8,128)(2,1)S(1)}, bf16[320,1280]{1,0:T(8,128)(2,1)S(1)}, u32[]{:S(2)}, u32[]{:S(2)}) collective-permute-start(bf16[320,1280]{1,0:T(8,128)(2,1)S(1)} %shard_map.68.refs_0_), channel_id=1, source_target_pairs={{24,0},{0,8},{8,16},{16,24},{25,1},{1,9},{9,17},{17,25},{26,2},{2,... | collective-permute-start | bytes 2457608 | tf_op jit(solution)/shard_map/ppermute | solution.py:193
  47.3 30.4 %collective-permute-start.1 = (bf16[320,1280]{1,0:T(8,128)(2,1)S(1)}, bf16[320,1280]{1,0:T(8,128)(2,1)}, u32[]{:S(2)}, u32[]{:S(2)}) collective-permute-start(bf16[320,1280]{1,0:T(8,128)(2,1)S(1)} %shard_map.68.refs_0_), channel_id=1, source_target_pairs={{16,0},{24,8},{0,16},{8,24},{17,1},{25,9},{1,17},{9,25},{18,2},{26... | collective-permute-start | bytes 2457608 | tf_op jit(solution)/shard_map/ppermute | solution.py:193
  51.7 32.9 %collective-permute-start = (bf16[320,1280]{1,0:T(8,128)(2,1)S(1)}, bf16[320,1280]{1,0:T(8,128)(2,1)}, u32[]{:S(2)}, u32[]{:S(2)}) collective-permute-start(bf16[320,1280]{1,0:T(8,128)(2,1)S(1)} %shard_map.68.refs_0_), channel_id=1, source_target_pairs={{8,0},{16,8},{24,16},{0,24},{9,1},{17,9},{25,17},{1,25},{10,2},{18... | collective-permute-start | bytes 2457608 | tf_op jit(solution)/shard_map/ppermute | solution.py:193
  54.8 41.8 %copy-start.3 = (s32[20]{0:T(128)S(1)}, s32[20]{0:T(128)}, u32[]{:S(2)}) copy-start(s32[20]{0:T(128)} %classes_ref.3) | copy-start | bytes 244
  61.8 34.8 %all-to-all-start.1 = ((bf16[8,16,384]{2,1,0:T(8,128)(2,1)}), bf16[8,16,384]{2,1,0:T(8,128)(2,1)S(1)}, u32[]{:S(2)}, u32[]{:S(2)}) async-start(bf16[8,16,384]{2,1,0:T(8,128)(2,1)} %bitcast.4), calls=%async_computation.1 | async-start | bytes 196608 | tf_op jit(solution)/shard_map/all_to_all | solution.py:210
  84.6 18.0 %collective-permute-start.3 = (bf16[320,1280]{1,0:T(8,128)(2,1)S(1)}, bf16[320,1280]{1,0:T(8,128)(2,1)}, u32[]{:S(2)}, u32[]{:S(2)}) collective-permute-start(bf16[320,1280]{1,0:T(8,128)(2,1)S(1)} %shard_map.68.refs_0_), channel_id=1, source_target_pairs={{0,4},{4,0},{1,5},{5,1},{2,6},{6,2},{3,7},{7,3},{8,12},{12,8},{9,1... | collective-permute-start | bytes 2457608 | tf_op jit(solution)/shard_map/ppermute | solution.py:209
  90.1 12.6 %collective-permute-start.4 = (bf16[320,1280]{1,0:T(8,128)(2,1)}, bf16[320,1280]{1,0:T(8,128)(2,1)}, u32[]{:S(2)}, u32[]{:S(2)}) collective-permute-start(bf16[320,1280]{1,0:T(8,128)(2,1)} %collective-permute-done.refs_1_), channel_id=1, source_target_pairs={{0,4},{4,0},{1,5},{5,1},{2,6},{6,2},{3,7},{7,3},{8,12},{12,8},{9,1... | collective-permute-start | bytes 2457608 | tf_op jit(solution)/shard_map/ppermute | solution.py:209
  92.0 10.6 %collective-permute-start.5 = (bf16[320,1280]{1,0:T(8,128)(2,1)}, bf16[320,1280]{1,0:T(8,128)(2,1)}, u32[]{:S(2)}, u32[]{:S(2)}) collective-permute-start(bf16[320,1280]{1,0:T(8,128)(2,1)} %collective-permute-done.1.refs_2_), channel_id=1, source_target_pairs={{0,4},{4,0},{1,5},{5,1},{2,6},{6,2},{3,7},{7,3},{8,12},{12,8},{9,1... | collective-permute-start | bytes 2457608 | tf_op jit(solution)/shard_map/ppermute | solution.py:209
  94.4 8.2 %collective-permute-start.6 = (bf16[320,1280]{1,0:T(8,128)(2,1)S(1)}, bf16[320,1280]{1,0:T(8,128)(2,1)}, u32[]{:S(2)}, u32[]{:S(2)}) collective-permute-start(bf16[320,1280]{1,0:T(8,128)(2,1)S(1)} %collective-permute-done.2.refs_3_), channel_id=1, source_target_pairs={{0,4},{4,0},{1,5},{5,1},{2,6},{6,2},{3,7},{7,3},{8,12},{12,8},{9,1... | collective-permute-start | bytes 2457608 | tf_op jit(solution)/shard_map/ppermute | solution.py:209
  98.4 14.4 %all-to-all-start.2 = ((bf16[4,128,640]{2,1,0:T(8,128)(2,1)}), bf16[4,128,640]{2,1,0:T(8,128)(2,1)S(1)}, u32[]{:S(2)}, u32[]{:S(2)}) async-start(bf16[4,128,640]{2,1,0:T(8,128)(2,1)} %shard_map.67), calls=%async_computation.2 | async-start | bytes 1310720 | tf_op jit(solution)/shard_map/all_to_all | solution.py:230

commit v4 on v3

--- a/solution.py
+++ b/solution.py
@@ -171,6 +171,12 @@
     core = lax.axis_index("core")
     group = lax.axis_index("head").astype(jnp.int32).reshape(1)
     width = TOK // FRAMES
+    weight = lax.all_gather(out_weight, Z_AXES, axis=0, tiled=False)
+    weight = call(rows_kernel, (320, 2 * COLS), [VMEM], weight)
+    around = [
+        lax.ppermute(weight, "x", [((x + step) % 4, x) for x in range(4)]) for step in (1, 2, 3)
+    ]
+    queries, keys, values, weight = lax.optimization_barrier((queries, keys, values, weight))
     packed = call(
         pack_kernel,
         (TOK, 3 * TMAX * HD),
@@ -183,16 +189,9 @@
         scratch=[pltpu.SemaphoreType.DMA((3 * TMAX,))],
         vmem=60,
     )
-    weight = lax.all_gather(out_weight, Z_AXES, axis=0, tiled=False)
-    packed, weight = lax.optimization_barrier((packed, weight))
     packed = lax.all_to_all(
         packed.reshape(FRAMES, width, 3 * TMAX * HD), FRAME_AXES, 0, 0, tiled=True
     ).reshape(TOK, 3 * TMAX * HD)
-    weight = call(rows_kernel, (320, 2 * COLS), [VMEM], weight)
-    around = [
-        lax.ppermute(weight, "x", [((x + step) % 4, x) for x in range(4)]) for step in (1, 2, 3)
-    ]
-    attended, mark = call(frame_kernel, [(TOK, TMAX * HD), (16, HD)], [VMEM], packed)
     spatial = call(
         window_kernel,
         (TOK, COLS),
@@ -203,7 +202,10 @@
         values,
         scratch=[pltpu.VMEM((TOK, COLS), jnp.bfloat16)] * 3 + [pltpu.SemaphoreType.DMA((3,))],
     )
-    mark, weight, around = lax.optimization_barrier((mark, weight, around))
+    packed, spatial = lax.optimization_barrier((packed, spatial))
+    attended, mark = call(frame_kernel, [(TOK, TMAX * HD), (16, HD)], [VMEM], packed)
+    mark, weight = lax.optimization_barrier((mark, weight))
+    mark, around = lax.optimization_barrier((mark, around))
     swap = [(0, 1), (1, 0)]
     slabs = [weight, *around]
     slabs = slabs + [lax.ppermute(slab, "core", swap) for slab in slabs]

time: 119 us -> 117 us (0.983)
  waiting for transfers between devices: 26.1 us -> 15.7 us
  starting transfers between devices: 42 us -> 50.8 us
    ppermute x3, waiting for transfers between devices: 13.7 us -> 2.41 us  [body(): lax.ppermute(weight, 'x', [((x + step) % 4, x) for x in range(4)])]
    ppermute x4, starting transfers between devices: 11.7 us -> 21 us  [body(): slabs = slabs + [lax.ppermute(slab, 'core', swap) for slab in slabs]]
  transfers between devices with their start and end apart: 10 -> 10, of which waited for: 4 -> 3; matrix products, arithmetic and copies ran while one was open for 0% -> 0% of each run, Pallas kernels for 6% -> 6%
where the time goes in v4:
time: 117 us; the launch traced here: 115 us
  starting transfers between devices  50.8 us (43%)
  blocking collectives  35.3 us (30%)
  waiting for transfers between devices  15.7 us (13%)
  Pallas kernels  13.1 us (11%)
    all_gather x1, blocking collectives, body(): weight = lax.all_gather(out_weight, Z_AXES, axis=0, tiled=False)  35.3 us
    ppermute x4, starting transfers between devices, body(): slabs = slabs + [lax.ppermute(slab, 'core', swap) for slab in slabs]  21 us
    pallas_call x6, Pallas kernels, call(): pl.pallas_call(kernel, out_shape=[jax.ShapeDtypeStruct(shape, out_dtype)...  13.1 us
    all_to_all x1, waiting for transfers between devices, body(): mixed = lax.all_to_all(mixed, 'head', 0, 0, tiled=True)  10.7 us
    ppermute x3, starting transfers between devices, body(): lax.ppermute(weight, 'x', [((x + step) % 4, x) for x in range(4)])  10.5 us
    all_to_all x1, starting transfers between devices, body(): lax.all_to_all(attended.reshape(FRAMES, width, TMAX * HD), FRAME_AXES, 0,...  8.84 us
    all_to_all x1, starting transfers between devices, body(): lax.all_to_all(packed.reshape(FRAMES, width, 3 * TMAX * HD), FRAME_AXES,...  6.27 us
    all_to_all x1, starting transfers between devices, body(): mixed = lax.all_to_all(mixed, 'head', 0, 0, tiled=True)  4.18 us
  transfers between devices with their start and end apart: 10, of which 3 were waited for; matrix products, arithmetic and copies ran while one was open for 0% of the time, Pallas kernels for 6%

profile of v4, /device:TPU:1, one launch (start us, length us, event | category | flops | bytes accessed | tf_op | source)
XLA Modules:
  0.0 115.5 jit_solution(8058645387384855853)
XLA Ops:
  0.0 35.3 %all-gather.1.weight_ref = bf16[16,20,1280]{2,1,0:T(8,128)(2,1)S(1)} all-gather(bf16[1,20,1280]{2,1,0:T(8,128)(2,1)} %bitcast.9), channel_id=2, replica_groups=mesh['far'=4,'near'=2,'half'=2,'x'=4,'core'=2,'head'=4] {'far','near','h..., dimensions={0}, use_global_device_ids=true | all-gather | bytes 870400 | tf_op jit(solution)/shard_map/all_gather | solution.py:174
  35.3 0.1 shard_map.64.refs_0_
  35.4 0.0 copy-start
  35.4 0.0 copy-start.1
  35.4 0.0 copy-start.2
  35.4 0.0 copy-start.4
  35.4 2.5 %shard_map.65 = bf16[128,1152]{1,0:T(8,128)(2,1)} custom-call(s32[1]{0:T(128)} %bitcast.group_ref, s32[20]{0:T(128)} %classes_ref.3, bf16[128,640]{1,0:T(8,128)(2,1)} %q_hbm, bf16[128,640]{1,0:T(8,128)(2,1)} %k_hbm, bf16[128,640]{1,0:T(8,128)(2,1)} %v_hbm), custom_call_target="tpu_custom_call" | custom-call | bytes 786516 | tf_op jit(solution)/shard_map/pallas_call | solution.py:158
  37.9 6.3 %all-to-all-start = ((bf16[8,16,1152]{2,1,0:T(8,128)(2,1)}), bf16[8,16,1152]{2,1,0:T(8,128)(2,1)S(1)}, u32[]{:S(2)}, u32[]{:S(2)}) async-start(bf16[8,16,1152]{2,1,0:T(8,128)(2,1)} %bitcast.8), calls=%async_computation | async-start | bytes 589824 | tf_op jit(solution)/shard_map/all_to_all | solution.py:192
  44.2 3.1 %collective-permute-start.2 = (bf16[320,1280]{1,0:T(8,128)(2,1)S(1)}, bf16[320,1280]{1,0:T(8,128)(2,1)S(1)}, u32[]{:S(2)}, u32[]{:S(2)}) collective-permute-start(bf16[320,1280]{1,0:T(8,128)(2,1)S(1)} %shard_map.64.refs_0_), channel_id=1, source_target_pairs={{24,0},{0,8},{8,16},{16,24},{25,1},{1,9},{9,17},{17,25},{26,2},{2,... | collective-permute-start | bytes 2457608 | tf_op jit(solution)/shard_map/ppermute | solution.py:177
  47.3 4.4 %collective-permute-start.1 = (bf16[320,1280]{1,0:T(8,128)(2,1)S(1)}, bf16[320,1280]{1,0:T(8,128)(2,1)S(1)}, u32[]{:S(2)}, u32[]{:S(2)}) collective-permute-start(bf16[320,1280]{1,0:T(8,128)(2,1)S(1)} %shard_map.64.refs_0_), channel_id=1, source_target_pairs={{16,0},{24,8},{0,16},{8,24},{17,1},{25,9},{1,17},{9,25},{18,2},{26... | collective-permute-start | bytes 2457608 | tf_op jit(solution)/shard_map/ppermute | solution.py:177
  51.7 3.1 %collective-permute-start = (bf16[320,1280]{1,0:T(8,128)(2,1)S(1)}, bf16[320,1280]{1,0:T(8,128)(2,1)}, u32[]{:S(2)}, u32[]{:S(2)}) collective-permute-start(bf16[320,1280]{1,0:T(8,128)(2,1)S(1)} %shard_map.64.refs_0_), channel_id=1, source_target_pairs={{8,0},{16,8},{24,16},{0,24},{9,1},{17,9},{25,17},{1,25},{10,2},{18... | collective-permute-start | bytes 2457608 | tf_op jit(solution)/shard_map/ppermute | solution.py:177
  54.8 0.0 copy-start.3
  54.8 2.9 %shard_map.66.spatial_ref = bf16[128,640]{1,0:T(8,128)(2,1)S(1)} custom-call(s32[1,4]{1,0:T(1,128)S(1)} %copy-done.4, bf16[128,640]{1,0:T(8,128)(2,1)S(1)} %copy-done, bf16[128,640]{1,0:T(8,128)(2,1)S(1)} %copy-done.1, bf16[128,640]{1,0:T(8,128)(2,1)S(1)} %copy-done.2), custom_call_target="tpu_custom_call" | custom-call | bytes 655376 | tf_op jit(solution)/shard_map/pallas_call | solution.py:158
  57.8 2.6 %all-to-all-done = bf16[8,16,1152]{2,1,0:T(8,128)(2,1)S(1)} async-done(((bf16[8,16,1152]{2,1,0:T(8,128)(2,1)}), bf16[8,16,1152]{2,1,0:T(8,128)(2,1)S(1)}, u32[]{:S(2)}, u32[]{:S(2)}) %all-to-all-start) | async-done | bytes 294944 | tf_op jit(solution)/shard_map/all_to_all | solution.py:192
  60.4 1.7 %shard_map.67 = (bf16[128,384]{1,0:T(8,128)(2,1)}, bf16[16,128]{1,0:T(8,128)(2,1)S(1)}) custom-call(bf16[128,1152]{1,0:T(8,128)(2,1)S(1)} %bitcast.6), custom_call_target="tpu_custom_call" | custom-call | bytes 397312 | tf_op jit(solution)/shard_map/pallas_call | solution.py:158
  62.1 8.8 %all-to-all-start.1 = ((bf16[8,16,384]{2,1,0:T(8,128)(2,1)}), bf16[8,16,384]{2,1,0:T(8,128)(2,1)S(1)}, u32[]{:S(2)}, u32[]{:S(2)}) async-start(bf16[8,16,384]{2,1,0:T(8,128)(2,1)} %bitcast.4), calls=%async_computation.1 | async-start | bytes 196608 | tf_op jit(solution)/shard_map/all_to_all | solution.py:212
  70.9 11.2 %collective-permute-start.3 = (bf16[320,1280]{1,0:T(8,128)(2,1)S(1)}, bf16[320,1280]{1,0:T(8,128)(2,1)}, u32[]{:S(2)}, u32[]{:S(2)}) collective-permute-start(bf16[320,1280]{1,0:T(8,128)(2,1)S(1)} %shard_map.64.refs_0_), channel_id=1, source_target_pairs={{0,4},{4,0},{1,5},{5,1},{2,6},{6,2},{3,7},{7,3},{8,12},{12,8},{9,1... | collective-permute-start | bytes 2457608 | tf_op jit(solution)/shard_map/ppermute | solution.py:211
  82.2 0.0 collective-permute-done.2.refs_3_
  82.2 0.0 collective-permute-done.1.refs_2_
  82.2 2.4 %collective-permute-done.refs_1_ = bf16[320,1280]{1,0:T(8,128)(2,1)} collective-permute-done((bf16[320,1280]{1,0:T(8,128)(2,1)S(1)}, bf16[320,1280]{1,0:T(8,128)(2,1)}, u32[]{:S(2)}, u32[]{:S(2)}) %collective-permute-start) | collective-permute-done | bytes 819232 | tf_op jit(solution)/shard_map/ppermute | solution.py:177
  84.6 5.5 %collective-permute-start.4 = (bf16[320,1280]{1,0:T(8,128)(2,1)}, bf16[320,1280]{1,0:T(8,128)(2,1)}, u32[]{:S(2)}, u32[]{:S(2)}) collective-permute-start(bf16[320,1280]{1,0:T(8,128)(2,1)} %collective-permute-done.refs_1_), channel_id=1, source_target_pairs={{0,4},{4,0},{1,5},{5,1},{2,6},{6,2},{3,7},{7,3},{8,12},{12,8},{9,1... | collective-permute-start | bytes 2457608 | tf_op jit(solution)/shard_map/ppermute | solution.py:211
  90.1 1.9 %collective-permute-start.5 = (bf16[320,1280]{1,0:T(8,128)(2,1)S(1)}, bf16[320,1280]{1,0:T(8,128)(2,1)}, u32[]{:S(2)}, u32[]{:S(2)}) collective-permute-start(bf16[320,1280]{1,0:T(8,128)(2,1)S(1)} %collective-permute-done.1.refs_2_), channel_id=1, source_target_pairs={{0,4},{4,0},{1,5},{5,1},{2,6},{6,2},{3,7},{7,3},{8,12},{12,8},{9,1... | collective-permute-start | bytes 2457608 | tf_op jit(solution)/shard_map/ppermute | solution.py:211
  92.0 2.4 %collective-permute-start.6 = (bf16[320,1280]{1,0:T(8,128)(2,1)S(1)}, bf16[320,1280]{1,0:T(8,128)(2,1)}, u32[]{:S(2)}, u32[]{:S(2)}) collective-permute-start(bf16[320,1280]{1,0:T(8,128)(2,1)S(1)} %collective-permute-done.2.refs_3_), channel_id=1, source_target_pairs={{0,4},{4,0},{1,5},{5,1},{2,6},{6,2},{3,7},{7,3},{8,12},{12,8},{9,1... | collective-permute-start | bytes 2457608 | tf_op jit(solution)/shard_map/ppermute | solution.py:211
  94.4 0.2 fusion.order_ref
  94.7 0.0 all-to-all-done.1
  94.7 1.8 %shard_map.68 = bf16[4,128,640]{2,1,0:T(8,128)(2,1)} custom-call(s32[1]{0:T(128)} %bitcast.group_ref, s32[20]{0:T(128)S(1)} %copy-done.3, bf16[128,640]{1,0:T(8,128)(2,1)S(1)} %shard_map.66.spatial_ref, bf16[128,384]{1,0:T(8,128)(2,1)S(1)} %bitcast.7, bf16[640,640]{1,0:T(8,128)(2,1)S(1)} %fusion.order_ref), custom_call_target="tpu_custom_call" | custom-call | bytes 1736788 | tf_op jit(solution)/shard_map/pallas_call | solution.py:158
  96.5 4.2 %all-to-all-start.2 = ((bf16[4,128,640]{2,1,0:T(8,128)(2,1)}), bf16[4,128,640]{2,1,0:T(8,128)(2,1)S(1)}, u32[]{:S(2)}, u32[]{:S(2)}) async-start(bf16[4,128,640]{2,1,0:T(8,128)(2,1)} %shard_map.68), calls=%async_computation.2 | async-start | bytes 1310720 | tf_op jit(solution)/shard_map/all_to_all | solution.py:232
  100.7 0.0 collective-permute-done.3.refs_4_
  100.7 0.0 collective-permute-done.5.refs_6_
  100.7 0.0 collective-permute-done.6.refs_7_
  100.7 10.7 %all-to-all-done.2.mixed_ref = bf16[4,128,640]{2,1,0:T(8,128)(2,1)S(1)} async-done(((bf16[4,128,640]{2,1,0:T(8,128)(2,1)}), bf16[4,128,640]{2,1,0:T(8,128)(2,1)S(1)}, u32[]{:S(2)}, u32[]{:S(2)}) %all-to-all-start.2) | async-done | bytes 655392 | tf_op jit(solution)/shard_map/all_to_all | solution.py:232
  111.4 4.1 %shard_map.69 = bf16[128,1280]{1,0:T(8,128)(2,1)} custom-call(bf16[4,128,640]{2,1,0:T(8,128)(2,1)S(1)} %all-to-all-done.2.mixed_ref, bf16[16,128]{1,0:T(8,128)(2,1)S(1)} %get-tuple-element.28.mark_ref, bf16[320,1280]{1,0:T(8,128)(2,1)S(1)} %shard_map.64.refs_0_, bf16[320,1280]{1,0:T(8,128)(2,1)} %collective-permute-done.refs_1_, ...), custom_call_target="tpu_custom_call" | custom-call | flops 838860800 | bytes 7540736 | tf_op jit(solution)/shard_map/pallas_call | solution.py:158
  (7 shorter events, 0.0 us)
Async XLA Ops:
  35.4 19.4 %copy-start = (bf16[128,640]{1,0:T(8,128)(2,1)S(1)}, bf16[128,640]{1,0:T(8,128)(2,1)}, u32[]{:S(2)}) copy-start(bf16[128,640]{1,0:T(8,128)(2,1)} %q_hbm) | copy-start | bytes 491524
  35.4 19.4 %copy-start.1 = (bf16[128,640]{1,0:T(8,128)(2,1)S(1)}, bf16[128,640]{1,0:T(8,128)(2,1)}, u32[]{:S(2)}) copy-start(bf16[128,640]{1,0:T(8,128)(2,1)} %k_hbm) | copy-start | bytes 491524
  35.4 19.4 %copy-start.2 = (bf16[128,640]{1,0:T(8,128)(2,1)S(1)}, bf16[128,640]{1,0:T(8,128)(2,1)}, u32[]{:S(2)}) copy-start(bf16[128,640]{1,0:T(8,128)(2,1)} %v_hbm) | copy-start | bytes 491524
  35.4 19.4 %copy-start.4 = (s32[1,4]{1,0:T(1,128)S(1)}, s32[1,4]{1,0:T(1,128)}, u32[]{:S(2)}) copy-start(s32[1,4]{1,0:T(1,128)} %lengths_ref.1) | copy-start | bytes 52
  37.9 22.4 %all-to-all-start = ((bf16[8,16,1152]{2,1,0:T(8,128)(2,1)}), bf16[8,16,1152]{2,1,0:T(8,128)(2,1)S(1)}, u32[]{:S(2)}, u32[]{:S(2)}) async-start(bf16[8,16,1152]{2,1,0:T(8,128)(2,1)} %bitcast.8), calls=%async_computation | async-start | bytes 589824 | tf_op jit(solution)/shard_map/all_to_all | solution.py:192
  44.2 38.0 %collective-permute-start.2 = (bf16[320,1280]{1,0:T(8,128)(2,1)S(1)}, bf16[320,1280]{1,0:T(8,128)(2,1)S(1)}, u32[]{:S(2)}, u32[]{:S(2)}) collective-permute-start(bf16[320,1280]{1,0:T(8,128)(2,1)S(1)} %shard_map.64.refs_0_), channel_id=1, source_target_pairs={{24,0},{0,8},{8,16},{16,24},{25,1},{1,9},{9,17},{17,25},{26,2},{2,... | collective-permute-start | bytes 2457608 | tf_op jit(solution)/shard_map/ppermute | solution.py:177
  47.3 34.9 %collective-permute-start.1 = (bf16[320,1280]{1,0:T(8,128)(2,1)S(1)}, bf16[320,1280]{1,0:T(8,128)(2,1)S(1)}, u32[]{:S(2)}, u32[]{:S(2)}) collective-permute-start(bf16[320,1280]{1,0:T(8,128)(2,1)S(1)} %shard_map.64.refs_0_), channel_id=1, source_target_pairs={{16,0},{24,8},{0,16},{8,24},{17,1},{25,9},{1,17},{9,25},{18,2},{26... | collective-permute-start | bytes 2457608 | tf_op jit(solution)/shard_map/ppermute | solution.py:177
  51.7 32.9 %collective-permute-start = (bf16[320,1280]{1,0:T(8,128)(2,1)S(1)}, bf16[320,1280]{1,0:T(8,128)(2,1)}, u32[]{:S(2)}, u32[]{:S(2)}) collective-permute-start(bf16[320,1280]{1,0:T(8,128)(2,1)S(1)} %shard_map.64.refs_0_), channel_id=1, source_target_pairs={{8,0},{16,8},{24,16},{0,24},{9,1},{17,9},{25,17},{1,25},{10,2},{18... | collective-permute-start | bytes 2457608 | tf_op jit(solution)/shard_map/ppermute | solution.py:177
  54.8 39.9 %copy-start.3 = (s32[20]{0:T(128)S(1)}, s32[20]{0:T(128)}, u32[]{:S(2)}) copy-start(s32[20]{0:T(128)} %classes_ref.3) | copy-start | bytes 244
  62.1 32.6 %all-to-all-start.1 = ((bf16[8,16,384]{2,1,0:T(8,128)(2,1)}), bf16[8,16,384]{2,1,0:T(8,128)(2,1)S(1)}, u32[]{:S(2)}, u32[]{:S(2)}) async-start(bf16[8,16,384]{2,1,0:T(8,128)(2,1)} %bitcast.4), calls=%async_computation.1 | async-start | bytes 196608 | tf_op jit(solution)/shard_map/all_to_all | solution.py:212
  70.9 29.7 %collective-permute-start.3 = (bf16[320,1280]{1,0:T(8,128)(2,1)S(1)}, bf16[320,1280]{1,0:T(8,128)(2,1)}, u32[]{:S(2)}, u32[]{:S(2)}) collective-permute-start(bf16[320,1280]{1,0:T(8,128)(2,1)S(1)} %shard_map.64.refs_0_), channel_id=1, source_target_pairs={{0,4},{4,0},{1,5},{5,1},{2,6},{6,2},{3,7},{7,3},{8,12},{12,8},{9,1... | collective-permute-start | bytes 2457608 | tf_op jit(solution)/shard_map/ppermute | solution.py:211
  84.6 16.1 %collective-permute-start.4 = (bf16[320,1280]{1,0:T(8,128)(2,1)}, bf16[320,1280]{1,0:T(8,128)(2,1)}, u32[]{:S(2)}, u32[]{:S(2)}) collective-permute-start(bf16[320,1280]{1,0:T(8,128)(2,1)} %collective-permute-done.refs_1_), channel_id=1, source_target_pairs={{0,4},{4,0},{1,5},{5,1},{2,6},{6,2},{3,7},{7,3},{8,12},{12,8},{9,1... | collective-permute-start | bytes 2457608 | tf_op jit(solution)/shard_map/ppermute | solution.py:211
  90.1 10.6 %collective-permute-start.5 = (bf16[320,1280]{1,0:T(8,128)(2,1)S(1)}, bf16[320,1280]{1,0:T(8,128)(2,1)}, u32[]{:S(2)}, u32[]{:S(2)}) collective-permute-start(bf16[320,1280]{1,0:T(8,128)(2,1)S(1)} %collective-permute-done.1.refs_2_), channel_id=1, source_target_pairs={{0,4},{4,0},{1,5},{5,1},{2,6},{6,2},{3,7},{7,3},{8,12},{12,8},{9,1... | collective-permute-start | bytes 2457608 | tf_op jit(solution)/shard_map/ppermute | solution.py:211
  92.0 8.7 %collective-permute-start.6 = (bf16[320,1280]{1,0:T(8,128)(2,1)S(1)}, bf16[320,1280]{1,0:T(8,128)(2,1)}, u32[]{:S(2)}, u32[]{:S(2)}) collective-permute-start(bf16[320,1280]{1,0:T(8,128)(2,1)S(1)} %collective-permute-done.2.refs_3_), channel_id=1, source_target_pairs={{0,4},{4,0},{1,5},{5,1},{2,6},{6,2},{3,7},{7,3},{8,12},{12,8},{9,1... | collective-permute-start | bytes 2457608 | tf_op jit(solution)/shard_map/ppermute | solution.py:211
  96.5 14.9 %all-to-all-start.2 = ((bf16[4,128,640]{2,1,0:T(8,128)(2,1)}), bf16[4,128,640]{2,1,0:T(8,128)(2,1)S(1)}, u32[]{:S(2)}, u32[]{:S(2)}) async-start(bf16[4,128,640]{2,1,0:T(8,128)(2,1)} %shard_map.68), calls=%async_computation.2 | async-start | bytes 1310720 | tf_op jit(solution)/shard_map/all_to_all | solution.py:232

commit v5 on v4

--- a/solution.py
+++ b/solution.py
@@ -36,28 +36,17 @@
     return found
 
 
-def pack_kernel(group_ref, classes_ref, q_ref, k_ref, v_ref, out_ref, sems):
+def pack_kernel(group_ref, classes_ref, q_ref, k_ref, v_ref, out_ref):
     slots = [0] * TMAX
     for head, (temporal, before) in enumerate(ranks(classes_ref, group_ref[0])):
         slots = [
             jnp.where(temporal & (before == slot), head, taken)
             for slot, taken in enumerate(slots)
         ]
-    copies = []
     for part, source in enumerate((q_ref, k_ref, v_ref)):
         for slot in range(TMAX):
-            place = part * TMAX + slot
-            copies.append(
-                pltpu.make_async_copy(
-                    source.at[:, columns(slots[slot])],
-                    out_ref.at[:, place * HD : (place + 1) * HD],
-                    sems.at[place],
-                )
-            )
-    for copy in copies:
-        copy.start()
-    for copy in copies:
-        copy.wait()
+            place = (part * TMAX + slot) * HD
+            out_ref[:, place : place + HD] = source[:, columns(slots[slot])]
 
 
 def attend(query, key, value, same):
@@ -72,17 +61,7 @@
     ).astype(jnp.bfloat16)
 
 
-def window_kernel(lengths_ref, q_hbm, k_hbm, v_hbm, out_ref, q_ref, k_ref, v_ref, sems):
-    copies = [
-        pltpu.make_async_copy(source, target, sems.at[place])
-        for place, (source, target) in enumerate(
-            ((q_hbm, q_ref), (k_hbm, k_ref), (v_hbm, v_ref))
-        )
-    ]
-    for copy in copies:
-        copy.start()
-    for copy in copies:
-        copy.wait()
+def window_kernel(lengths_ref, q_ref, k_ref, v_ref, out_ref):
     rows = lax.broadcasted_iota(jnp.int32, (TOK, TOK), 0)
     cols = lax.broadcasted_iota(jnp.int32, (TOK, TOK), 1)
     row_id = jnp.zeros((TOK, TOK), jnp.int32)
@@ -174,38 +153,33 @@
     weight = lax.all_gather(out_weight, Z_AXES, axis=0, tiled=False)
     weight = call(rows_kernel, (320, 2 * COLS), [VMEM], weight)
     around = [
-        lax.ppermute(weight, "x", [((x + step) % 4, x) for x in range(4)]) for step in (1, 2, 3)
+        lax.ppermute(weight, "x", [((x + step) % 4, x) for x in range(4)]) for step in (1, 3, 2)
     ]
-    queries, keys, values, weight = lax.optimization_barrier((queries, keys, values, weight))
+    after, weight = lax.optimization_barrier((group, weight))
     packed = call(
         pack_kernel,
         (TOK, 3 * TMAX * HD),
-        [SMEM] * 2 + [HBM] * 3,
-        group,
+        [SMEM] * 2 + [VMEM] * 3,
+        after,
         head_class,
         queries,
         keys,
         values,
-        scratch=[pltpu.SemaphoreType.DMA((3 * TMAX,))],
-        vmem=60,
-    )
+    )
+    packed, window_lengths = lax.optimization_barrier((packed, window_lengths))
     packed = lax.all_to_all(
         packed.reshape(FRAMES, width, 3 * TMAX * HD), FRAME_AXES, 0, 0, tiled=True
     ).reshape(TOK, 3 * TMAX * HD)
     spatial = call(
-        window_kernel,
-        (TOK, COLS),
-        [SMEM] + [HBM] * 3,
-        window_lengths,
-        queries,
-        keys,
-        values,
-        scratch=[pltpu.VMEM((TOK, COLS), jnp.bfloat16)] * 3 + [pltpu.SemaphoreType.DMA((3,))],
+        window_kernel, (TOK, COLS), [SMEM] + [VMEM] * 3, window_lengths, queries, keys, values
     )
     packed, spatial = lax.optimization_barrier((packed, spatial))
     attended, mark = call(frame_kernel, [(TOK, TMAX * HD), (16, HD)], [VMEM], packed)
     mark, weight = lax.optimization_barrier((mark, weight))
-    mark, around = lax.optimization_barrier((mark, around))
+    mark, last = lax.optimization_barrier((mark, around[2]))
+    mark, middle = lax.optimization_barrier((mark, around[1]))
+    mark, first = lax.optimization_barrier((mark, around[0]))
+    around = [first, middle, last]
     swap = [(0, 1), (1, 0)]
     slabs = [weight, *around]
     slabs = slabs + [lax.ppermute(slab, "core", swap) for slab in slabs]
@@ -215,7 +189,9 @@
 
     source = jnp.arange(COLS, dtype=jnp.int32)[:, None]
     place = jnp.arange(COLS, dtype=jnp.int32)[None, :]
-    owner = (lax.axis_index("x") + place // 80) % 4 * 2 + (core + place // 320) % 2
+    turn = place // 80 % 4
+    turn = turn + (turn == 2) - (turn == 3)
+    owner = (lax.axis_index("x") + turn) % 4 * 2 + (core + place // 320) % 2
     wanted = place % 80 // 20 * 160 + owner * 20 + place % 20
     order = (source == wanted).astype(jnp.bfloat16)
     mixed = call(

time: 117 us -> 113 us (0.966)
  waiting for transfers between devices: 15.7 us -> 12.6 us
  Pallas kernels: 13.1 us -> 11.2 us
    all_to_all x1, waiting for transfers between devices: 10.7 us -> 8.58 us  [body(): mixed = lax.all_to_all(mixed, 'head', 0, 0, tiled=True)]
    pallas_call x6, Pallas kernels: 13.1 us -> 11.2 us  [call(): pl.pallas_call(kernel, out_shape=[jax.ShapeDtypeStruct(shape, out_dtype)...]
  transfers between devices with their start and end apart: 10 -> 10, of which waited for: 3 -> 3; matrix products, arithmetic and copies ran while one was open for 0% -> 0% of each run, Pallas kernels for 6% -> 5%
where the time goes in v5:
time: 113 us; the launch traced here: 111 us
  starting transfers between devices  50.4 us (45%)
  blocking collectives  35.3 us (31%)
  waiting for transfers between devices  12.6 us (11%)
  Pallas kernels  11.2 us (10%)
    all_gather x1, blocking collectives, body(): weight = lax.all_gather(out_weight, Z_AXES, axis=0, tiled=False)  35.3 us
    ppermute x4, starting transfers between devices, body(): slabs = slabs + [lax.ppermute(slab, 'core', swap) for slab in slabs]  20.1 us
    pallas_call x6, Pallas kernels, call(): pl.pallas_call(kernel, out_shape=[jax.ShapeDtypeStruct(shape, out_dtype)...  11.2 us
    ppermute x3, starting transfers between devices, body(): lax.ppermute(weight, 'x', [((x + step) % 4, x) for x in range(4)])  11.1 us
    all_to_all x1, starting transfers between devices, body(): lax.all_to_all(attended.reshape(FRAMES, width, TMAX * HD), FRAME_AXES, 0,...  8.74 us
    all_to_all x1, waiting for transfers between devices, body(): mixed = lax.all_to_all(mixed, 'head', 0, 0, tiled=True)  8.58 us
    all_to_all x1, starting transfers between devices, body(): lax.all_to_all(packed.reshape(FRAMES, width, 3 * TMAX * HD), FRAME_AXES,...  6.26 us
    all_to_all x1, starting transfers between devices, body(): mixed = lax.all_to_all(mixed, 'head', 0, 0, tiled=True)  4.18 us
  transfers between devices with their start and end apart: 10, of which 3 were waited for; matrix products, arithmetic and copies ran while one was open for 0% of the time, Pallas kernels for 5%

profile of v5, /device:TPU:1, one launch (start us, length us, event | category | flops | bytes accessed | tf_op | source)
XLA Modules:
  0.0 110.9 jit_solution(13187060351667733589)
XLA Ops:
  0.0 35.3 %all-gather.1.weight_ref = bf16[16,20,1280]{2,1,0:T(8,128)(2,1)S(1)} all-gather(bf16[1,20,1280]{2,1,0:T(8,128)(2,1)} %bitcast.8), channel_id=2, replica_groups=mesh['far'=4,'near'=2,'half'=2,'x'=4,'core'=2,'head'=4] {'far','near','h..., dimensions={0}, use_global_device_ids=true | all-gather | bytes 870400 | tf_op jit(solution)/shard_map/all_gather | solution.py:153
  35.3 0.1 shard_map.64.refs_0_
  35.4 0.0 copy-start.4
  35.4 0.8 copy-done
  36.2 0.1 copy-done.1
  36.3 0.1 copy-done.2
  36.4 1.3 %shard_map.65 = bf16[128,1152]{1,0:T(8,128)(2,1)} custom-call(s32[1]{0:T(128)} %bitcast.group_ref, s32[20]{0:T(128)S(1)} %copy-done.3, bf16[128,640]{1,0:T(8,128)(2,1)S(1)} %copy-done, bf16[128,640]{1,0:T(8,128)(2,1)S(1)} %copy-done.1, bf16[128,640]{1,0:T(8,128)(2,1)S(1)} %copy-done.2), custom_call_target="tpu_custom_call" | custom-call | bytes 786516 | tf_op jit(solution)/shard_map/pallas_call | solution.py:137
  37.7 6.3 %all-to-all-start = ((bf16[8,16,1152]{2,1,0:T(8,128)(2,1)}), bf16[8,16,1152]{2,1,0:T(8,128)(2,1)S(1)}, u32[]{:S(2)}, u32[]{:S(2)}) async-start(bf16[8,16,1152]{2,1,0:T(8,128)(2,1)} %bitcast.2), calls=%async_computation | async-start | bytes 589824 | tf_op jit(solution)/shard_map/all_to_all | solution.py:170
  43.9 4.6 %collective-permute-start = (bf16[320,1280]{1,0:T(8,128)(2,1)S(1)}, bf16[320,1280]{1,0:T(8,128)(2,1)S(1)}, u32[]{:S(2)}, u32[]{:S(2)}) collective-permute-start(bf16[320,1280]{1,0:T(8,128)(2,1)S(1)} %shard_map.64.refs_0_), channel_id=1, source_target_pairs={{16,0},{24,8},{0,16},{8,24},{17,1},{25,9},{1,17},{9,25},{18,2},{26... | collective-permute-start | bytes 2457608 | tf_op jit(solution)/shard_map/ppermute | solution.py:156
  48.6 2.2 %collective-permute-start.1 = (bf16[320,1280]{1,0:T(8,128)(2,1)S(1)}, bf16[320,1280]{1,0:T(8,128)(2,1)S(1)}, u32[]{:S(2)}, u32[]{:S(2)}) collective-permute-start(bf16[320,1280]{1,0:T(8,128)(2,1)S(1)} %shard_map.64.refs_0_), channel_id=1, source_target_pairs={{24,0},{0,8},{8,16},{16,24},{25,1},{1,9},{9,17},{17,25},{26,2},{2,... | collective-permute-start | bytes 2457608 | tf_op jit(solution)/shard_map/ppermute | solution.py:156
  50.8 4.3 %collective-permute-start.2 = (bf16[320,1280]{1,0:T(8,128)(2,1)S(1)}, bf16[320,1280]{1,0:T(8,128)(2,1)}, u32[]{:S(2)}, u32[]{:S(2)}) collective-permute-start(bf16[320,1280]{1,0:T(8,128)(2,1)S(1)} %shard_map.64.refs_0_), channel_id=1, source_target_pairs={{8,0},{16,8},{24,16},{0,24},{9,1},{17,9},{25,17},{1,25},{10,2},{18... | collective-permute-start | bytes 2457608 | tf_op jit(solution)/shard_map/ppermute | solution.py:156
  55.1 2.3 %shard_map.66.spatial_ref = bf16[128,640]{1,0:T(8,128)(2,1)S(1)} custom-call(s32[1,4]{1,0:T(1,128)S(1)} %copy-done.4, bf16[128,640]{1,0:T(8,128)(2,1)S(1)} %copy-done, bf16[128,640]{1,0:T(8,128)(2,1)S(1)} %copy-done.1, bf16[128,640]{1,0:T(8,128)(2,1)S(1)} %copy-done.2), custom_call_target="tpu_custom_call" | custom-call | bytes 655376 | tf_op jit(solution)/shard_map/pallas_call | solution.py:137
  57.4 2.7 %all-to-all-done = bf16[8,16,1152]{2,1,0:T(8,128)(2,1)S(1)} async-done(((bf16[8,16,1152]{2,1,0:T(8,128)(2,1)}), bf16[8,16,1152]{2,1,0:T(8,128)(2,1)S(1)}, u32[]{:S(2)}, u32[]{:S(2)}) %all-to-all-start) | async-done | bytes 294944 | tf_op jit(solution)/shard_map/all_to_all | solution.py:170
  60.1 1.7 %shard_map.67 = (bf16[128,384]{1,0:T(8,128)(2,1)}, bf16[16,128]{1,0:T(8,128)(2,1)S(1)}) custom-call(bf16[128,1152]{1,0:T(8,128)(2,1)S(1)} %bitcast.6), custom_call_target="tpu_custom_call" | custom-call | bytes 397312 | tf_op jit(solution)/shard_map/pallas_call | solution.py:137
  61.8 8.7 %all-to-all-start.1 = ((bf16[8,16,384]{2,1,0:T(8,128)(2,1)}), bf16[8,16,384]{2,1,0:T(8,128)(2,1)S(1)}, u32[]{:S(2)}, u32[]{:S(2)}) async-start(bf16[8,16,384]{2,1,0:T(8,128)(2,1)} %bitcast.4), calls=%async_computation.1 | async-start | bytes 196608 | tf_op jit(solution)/shard_map/all_to_all | solution.py:186
  70.6 11.2 %collective-permute-start.3 = (bf16[320,1280]{1,0:T(8,128)(2,1)S(1)}, bf16[320,1280]{1,0:T(8,128)(2,1)}, u32[]{:S(2)}, u32[]{:S(2)}) collective-permute-start(bf16[320,1280]{1,0:T(8,128)(2,1)S(1)} %shard_map.64.refs_0_), channel_id=1, source_target_pairs={{0,4},{4,0},{1,5},{5,1},{2,6},{6,2},{3,7},{7,3},{8,12},{12,8},{9,1... | collective-permute-start | bytes 2457608 | tf_op jit(solution)/shard_map/ppermute | solution.py:185
  81.8 0.0 collective-permute-done.refs_3_
  81.8 1.3 %collective-permute-done.1.refs_2_ = bf16[320,1280]{1,0:T(8,128)(2,1)S(1)} collective-permute-done((bf16[320,1280]{1,0:T(8,128)(2,1)S(1)}, bf16[320,1280]{1,0:T(8,128)(2,1)S(1)}, u32[]{:S(2)}, u32[]{:S(2)}) %collective-permute-start.1) | collective-permute-done | bytes 819232 | tf_op jit(solution)/shard_map/ppermute | solution.py:156
  83.1 0.0 collective-permute-done.2.refs_1_
  83.1 4.5 %collective-permute-start.4 = (bf16[320,1280]{1,0:T(8,128)(2,1)}, bf16[320,1280]{1,0:T(8,128)(2,1)}, u32[]{:S(2)}, u32[]{:S(2)}) collective-permute-start(bf16[320,1280]{1,0:T(8,128)(2,1)} %collective-permute-done.2.refs_1_), channel_id=1, source_target_pairs={{0,4},{4,0},{1,5},{5,1},{2,6},{6,2},{3,7},{7,3},{8,12},{12,8},{9,1... | collective-permute-start | bytes 2457608 | tf_op jit(solution)/shard_map/ppermute | solution.py:185
  87.7 1.9 %collective-permute-start.5 = (bf16[320,1280]{1,0:T(8,128)(2,1)S(1)}, bf16[320,1280]{1,0:T(8,128)(2,1)}, u32[]{:S(2)}, u32[]{:S(2)}) collective-permute-start(bf16[320,1280]{1,0:T(8,128)(2,1)S(1)} %collective-permute-done.1.refs_2_), channel_id=1, source_target_pairs={{0,4},{4,0},{1,5},{5,1},{2,6},{6,2},{3,7},{7,3},{8,12},{12,8},{9,1... | collective-permute-start | bytes 2457608 | tf_op jit(solution)/shard_map/ppermute | solution.py:185
  89.6 2.4 %collective-permute-start.6 = (bf16[320,1280]{1,0:T(8,128)(2,1)S(1)}, bf16[320,1280]{1,0:T(8,128)(2,1)}, u32[]{:S(2)}, u32[]{:S(2)}) collective-permute-start(bf16[320,1280]{1,0:T(8,128)(2,1)S(1)} %collective-permute-done.refs_3_), channel_id=1, source_target_pairs={{0,4},{4,0},{1,5},{5,1},{2,6},{6,2},{3,7},{7,3},{8,12},{12,8},{9,1... | collective-permute-start | bytes 2457608 | tf_op jit(solution)/shard_map/ppermute | solution.py:185
  92.1 0.3 fusion.order_ref
  92.3 0.0 all-to-all-done.1
  92.3 1.8 %shard_map.68 = bf16[4,128,640]{2,1,0:T(8,128)(2,1)} custom-call(s32[1]{0:T(128)} %bitcast.group_ref, s32[20]{0:T(128)S(1)} %copy-done.3, bf16[128,640]{1,0:T(8,128)(2,1)S(1)} %shard_map.66.spatial_ref, bf16[128,384]{1,0:T(8,128)(2,1)S(1)} %bitcast.7, bf16[640,640]{1,0:T(8,128)(2,1)S(1)} %fusion.order_ref), custom_call_target="tpu_custom_call" | custom-call | bytes 1736788 | tf_op jit(solution)/shard_map/pallas_call | solution.py:137
  94.1 4.2 %all-to-all-start.2 = ((bf16[4,128,640]{2,1,0:T(8,128)(2,1)}), bf16[4,128,640]{2,1,0:T(8,128)(2,1)S(1)}, u32[]{:S(2)}, u32[]{:S(2)}) async-start(bf16[4,128,640]{2,1,0:T(8,128)(2,1)} %shard_map.68), calls=%async_computation.2 | async-start | bytes 1310720 | tf_op jit(solution)/shard_map/all_to_all | solution.py:208
  98.3 0.0 collective-permute-done.3.refs_4_
  98.3 0.0 collective-permute-done.4.refs_5_
  98.3 0.0 collective-permute-done.5.refs_6_
  98.3 0.0 collective-permute-done.6.refs_7_
  98.3 8.6 %all-to-all-done.2.mixed_ref = bf16[4,128,640]{2,1,0:T(8,128)(2,1)S(1)} async-done(((bf16[4,128,640]{2,1,0:T(8,128)(2,1)}), bf16[4,128,640]{2,1,0:T(8,128)(2,1)S(1)}, u32[]{:S(2)}, u32[]{:S(2)}) %all-to-all-start.2) | async-done | bytes 655392 | tf_op jit(solution)/shard_map/all_to_all | solution.py:208
  106.9 4.0 %shard_map.69 = bf16[128,1280]{1,0:T(8,128)(2,1)} custom-call(bf16[4,128,640]{2,1,0:T(8,128)(2,1)S(1)} %all-to-all-done.2.mixed_ref, bf16[16,128]{1,0:T(8,128)(2,1)S(1)} %get-tuple-element.32.mark_ref, bf16[320,1280]{1,0:T(8,128)(2,1)S(1)} %shard_map.64.refs_0_, bf16[320,1280]{1,0:T(8,128)(2,1)} %collective-permute-done.2.refs_1_, ...), custom_call_target="tpu_custom_call" | custom-call | flops 838860800 | bytes 7540736 | tf_op jit(solution)/shard_map/pallas_call | solution.py:137
  (7 shorter events, 0.0 us)
Async XLA Ops:
  35.3 0.9 copy-start
  35.3 1.0 copy-start.1
  35.3 1.1 copy-start.2
  35.3 1.1 copy-start.3
  35.4 19.7 %copy-start.4 = (s32[1,4]{1,0:T(1,128)S(1)}, s32[1,4]{1,0:T(1,128)}, u32[]{:S(2)}) copy-start(s32[1,4]{1,0:T(1,128)} %lengths_ref) | copy-start | bytes 52
  37.7 22.4 %all-to-all-start = ((bf16[8,16,1152]{2,1,0:T(8,128)(2,1)}), bf16[8,16,1152]{2,1,0:T(8,128)(2,1)S(1)}, u32[]{:S(2)}, u32[]{:S(2)}) async-start(bf16[8,16,1152]{2,1,0:T(8,128)(2,1)} %bitcast.2), calls=%async_computation | async-start | bytes 589824 | tf_op jit(solution)/shard_map/all_to_all | solution.py:170
  43.9 37.9 %collective-permute-start = (bf16[320,1280]{1,0:T(8,128)(2,1)S(1)}, bf16[320,1280]{1,0:T(8,128)(2,1)S(1)}, u32[]{:S(2)}, u32[]{:S(2)}) collective-permute-start(bf16[320,1280]{1,0:T(8,128)(2,1)S(1)} %shard_map.64.refs_0_), channel_id=1, source_target_pairs={{16,0},{24,8},{0,16},{8,24},{17,1},{25,9},{1,17},{9,25},{18,2},{26... | collective-permute-start | bytes 2457608 | tf_op jit(solution)/shard_map/ppermute | solution.py:156
  48.6 34.5 %collective-permute-start.1 = (bf16[320,1280]{1,0:T(8,128)(2,1)S(1)}, bf16[320,1280]{1,0:T(8,128)(2,1)S(1)}, u32[]{:S(2)}, u32[]{:S(2)}) collective-permute-start(bf16[320,1280]{1,0:T(8,128)(2,1)S(1)} %shard_map.64.refs_0_), channel_id=1, source_target_pairs={{24,0},{0,8},{8,16},{16,24},{25,1},{1,9},{9,17},{17,25},{26,2},{2,... | collective-permute-start | bytes 2457608 | tf_op jit(solution)/shard_map/ppermute | solution.py:156
  50.8 32.3 %collective-permute-start.2 = (bf16[320,1280]{1,0:T(8,128)(2,1)S(1)}, bf16[320,1280]{1,0:T(8,128)(2,1)}, u32[]{:S(2)}, u32[]{:S(2)}) collective-permute-start(bf16[320,1280]{1,0:T(8,128)(2,1)S(1)} %shard_map.64.refs_0_), channel_id=1, source_target_pairs={{8,0},{16,8},{24,16},{0,24},{9,1},{17,9},{25,17},{1,25},{10,2},{18... | collective-permute-start | bytes 2457608 | tf_op jit(solution)/shard_map/ppermute | solution.py:156
  61.8 30.5 %all-to-all-start.1 = ((bf16[8,16,384]{2,1,0:T(8,128)(2,1)}), bf16[8,16,384]{2,1,0:T(8,128)(2,1)S(1)}, u32[]{:S(2)}, u32[]{:S(2)}) async-start(bf16[8,16,384]{2,1,0:T(8,128)(2,1)} %bitcast.4), calls=%async_computation.1 | async-start | bytes 196608 | tf_op jit(solution)/shard_map/all_to_all | solution.py:186
  70.6 27.7 %collective-permute-start.3 = (bf16[320,1280]{1,0:T(8,128)(2,1)S(1)}, bf16[320,1280]{1,0:T(8,128)(2,1)}, u32[]{:S(2)}, u32[]{:S(2)}) collective-permute-start(bf16[320,1280]{1,0:T(8,128)(2,1)S(1)} %shard_map.64.refs_0_), channel_id=1, source_target_pairs={{0,4},{4,0},{1,5},{5,1},{2,6},{6,2},{3,7},{7,3},{8,12},{12,8},{9,1... | collective-permute-start | bytes 2457608 | tf_op jit(solution)/shard_map/ppermute | solution.py:185
  83.1 15.2 %collective-permute-start.4 = (bf16[320,1280]{1,0:T(8,128)(2,1)}, bf16[320,1280]{1,0:T(8,128)(2,1)}, u32[]{:S(2)}, u32[]{:S(2)}) collective-permute-start(bf16[320,1280]{1,0:T(8,128)(2,1)} %collective-permute-done.2.refs_1_), channel_id=1, source_target_pairs={{0,4},{4,0},{1,5},{5,1},{2,6},{6,2},{3,7},{7,3},{8,12},{12,8},{9,1... | collective-permute-start | bytes 2457608 | tf_op jit(solution)/shard_map/ppermute | solution.py:185
  87.7 10.6 %collective-permute-start.5 = (bf16[320,1280]{1,0:T(8,128)(2,1)S(1)}, bf16[320,1280]{1,0:T(8,128)(2,1)}, u32[]{:S(2)}, u32[]{:S(2)}) collective-permute-start(bf16[320,1280]{1,0:T(8,128)(2,1)S(1)} %collective-permute-done.1.refs_2_), channel_id=1, source_target_pairs={{0,4},{4,0},{1,5},{5,1},{2,6},{6,2},{3,7},{7,3},{8,12},{12,8},{9,1... | collective-permute-start | bytes 2457608 | tf_op jit(solution)/shard_map/ppermute | solution.py:185
  89.6 8.7 %collective-permute-start.6 = (bf16[320,1280]{1,0:T(8,128)(2,1)S(1)}, bf16[320,1280]{1,0:T(8,128)(2,1)}, u32[]{:S(2)}, u32[]{:S(2)}) collective-permute-start(bf16[320,1280]{1,0:T(8,128)(2,1)S(1)} %collective-permute-done.refs_3_), channel_id=1, source_target_pairs={{0,4},{4,0},{1,5},{5,1},{2,6},{6,2},{3,7},{7,3},{8,12},{12,8},{9,1... | collective-permute-start | bytes 2457608 | tf_op jit(solution)/shard_map/ppermute | solution.py:185
  94.1 12.8 %all-to-all-start.2 = ((bf16[4,128,640]{2,1,0:T(8,128)(2,1)}), bf16[4,128,640]{2,1,0:T(8,128)(2,1)S(1)}, u32[]{:S(2)}, u32[]{:S(2)}) async-start(bf16[4,128,640]{2,1,0:T(8,128)(2,1)} %shard_map.68), calls=%async_computation.2 | async-start | bytes 1310720 | tf_op jit(solution)/shard_map/all_to_all | solution.py:208

commit v6 on v5

--- a/solution.py
+++ b/solution.py
@@ -106,8 +106,7 @@
 
     ordered = jnp.dot(mixed[...], order_ref[...], preferred_element_type=jnp.float32)
     ordered = ordered.astype(jnp.bfloat16)
-    for copy in range(4):
-        out_ref[copy] = ordered
+    out_ref[...] = ordered
 
 
 def rows_kernel(weight_ref, out_ref):
@@ -166,19 +165,18 @@
         keys,
         values,
     )
-    packed, window_lengths = lax.optimization_barrier((packed, window_lengths))
     packed = lax.all_to_all(
         packed.reshape(FRAMES, width, 3 * TMAX * HD), FRAME_AXES, 0, 0, tiled=True
     ).reshape(TOK, 3 * TMAX * HD)
+    attended, mark = call(frame_kernel, [(TOK, TMAX * HD), (16, HD)], [VMEM], packed)
+    mark, weight = lax.optimization_barrier((mark, weight))
+    mark, window_lengths = lax.optimization_barrier((mark, window_lengths))
     spatial = call(
         window_kernel, (TOK, COLS), [SMEM] + [VMEM] * 3, window_lengths, queries, keys, values
     )
-    packed, spatial = lax.optimization_barrier((packed, spatial))
-    attended, mark = call(frame_kernel, [(TOK, TMAX * HD), (16, HD)], [VMEM], packed)
-    mark, weight = lax.optimization_barrier((mark, weight))
-    mark, last = lax.optimization_barrier((mark, around[2]))
-    mark, middle = lax.optimization_barrier((mark, around[1]))
-    mark, first = lax.optimization_barrier((mark, around[0]))
+    spatial, last = lax.optimization_barrier((spatial, around[2]))
+    spatial, middle = lax.optimization_barrier((spatial, around[1]))
+    spatial, first = lax.optimization_barrier((spatial, around[0]))
     around = [first, middle, last]
     swap = [(0, 1), (1, 0)]
     slabs = [weight, *around]
@@ -196,7 +194,7 @@
     order = (source == wanted).astype(jnp.bfloat16)
     mixed = call(
         mix_kernel,
-        (4, TOK, COLS),
+        (TOK, COLS),
         [SMEM] * 2 + [VMEM] * 3,
         group,
         head_class,
@@ -205,7 +203,8 @@
         order,
         scratch=[pltpu.VMEM((TOK, COLS), jnp.bfloat16)],
     )
-    mixed = lax.all_to_all(mixed, "head", 0, 0, tiled=True)
+    mixed = lax.all_gather(mixed, "head", axis=0, tiled=False)
+    mark = mark + mixed[0, :16, :HD]
     return call(
         project_kernel,
         (TOK, 2 * COLS),

time: 113 us -> 111 us (0.982)
  blocking collectives: 35.3 us -> 47.2 us
  starting transfers between devices: 50.4 us -> 44 us
  waiting for transfers between devices: 12.6 us -> 6.33 us
    all_gather x0 -> x1, blocking collectives: none -> 11.9 us  [body(): mixed = lax.all_gather(mixed, 'head', axis=0, tiled=False)]
    all_to_all x1 -> x0, waiting for transfers between devices: 8.58 us -> none  [body(): mixed = lax.all_to_all(mixed, 'head', 0, 0, tiled=True)]
    all_to_all x1 -> x0, starting transfers between devices: 4.18 us -> none  [body(): mixed = lax.all_to_all(mixed, 'head', 0, 0, tiled=True)]
    all_to_all x1, waiting for transfers between devices: 2.72 us -> 5 us  [body(): lax.all_to_all(packed.reshape(FRAMES, width, 3 * TMAX * HD), FRAME_AXES,...]
    all_to_all x1, starting transfers between devices: 8.74 us -> 6.46 us  [body(): lax.all_to_all(attended.reshape(FRAMES, width, TMAX * HD), FRAME_AXES, 0,...]
  transfers between devices with their start and end apart: 10 -> 9, of which waited for: 3 -> 2; matrix products, arithmetic and copies ran while one was open for 0% -> 0% of each run, Pallas kernels for 5% -> 4%
where the time goes in v6:
time: 111 us; the launch traced here: 109 us
  blocking collectives  47.2 us (43%)
  starting transfers between devices  44 us (40%)
  Pallas kernels  10.4 us (9%)
  waiting for transfers between devices  6.33 us (6%)
    all_gather x1, blocking collectives, body(): weight = lax.all_gather(out_weight, Z_AXES, axis=0, tiled=False)  35.3 us
    ppermute x4, starting transfers between devices, body(): slabs = slabs + [lax.ppermute(slab, 'core', swap) for slab in slabs]  20.1 us
    all_gather x1, blocking collectives, body(): mixed = lax.all_gather(mixed, 'head', axis=0, tiled=False)  11.9 us
    ppermute x3, starting transfers between devices, body(): lax.ppermute(weight, 'x', [((x + step) % 4, x) for x in range(4)])  11.1 us
    pallas_call x6, Pallas kernels, call(): pl.pallas_call(kernel, out_shape=[jax.ShapeDtypeStruct(shape, out_dtype)...  10.4 us
    all_to_all x1, starting transfers between devices, body(): lax.all_to_all(attended.reshape(FRAMES, width, TMAX * HD), FRAME_AXES, 0,...  6.46 us
    all_to_all x1, starting transfers between devices, body(): lax.all_to_all(packed.reshape(FRAMES, width, 3 * TMAX * HD), FRAME_AXES,...  6.26 us
    all_to_all x1, waiting for transfers between devices, body(): lax.all_to_all(packed.reshape(FRAMES, width, 3 * TMAX * HD), FRAME_AXES,...  5 us
  transfers between devices with their start and end apart: 9, of which 2 were waited for; matrix products, arithmetic and copies ran while one was open for 0% of the time, Pallas kernels for 4%

profile of v6, /device:TPU:1, one launch (start us, length us, event | category | flops | bytes accessed | tf_op | source)
XLA Modules:
  0.0 109.2 jit_solution(14530732996038847141)
XLA Ops:
  0.0 35.3 %all-gather.2.weight_ref = bf16[16,20,1280]{2,1,0:T(8,128)(2,1)S(1)} all-gather(bf16[1,20,1280]{2,1,0:T(8,128)(2,1)} %bitcast.15), channel_id=2, replica_groups=mesh['far'=4,'near'=2,'half'=2,'x'=4,'core'=2,'head'=4] {'far','near','h..., dimensions={0}, use_global_device_ids=true | all-gather | bytes 870400 | tf_op jit(solution)/shard_map/all_gather | solution.py:152
  35.3 0.1 shard_map.64.refs_0_
  35.4 0.0 copy-start.4
  35.4 0.8 copy-done
  36.2 0.1 copy-done.1
  36.3 0.1 copy-done.2
  36.4 0.0 copy-done.3
  36.4 1.3 %shard_map.65 = bf16[128,1152]{1,0:T(8,128)(2,1)} custom-call(s32[1]{0:T(128)} %bitcast.group_ref, s32[20]{0:T(128)S(1)} %copy-done.3, bf16[128,640]{1,0:T(8,128)(2,1)S(1)} %copy-done, bf16[128,640]{1,0:T(8,128)(2,1)S(1)} %copy-done.1, bf16[128,640]{1,0:T(8,128)(2,1)S(1)} %copy-done.2), custom_call_target="tpu_custom_call" | custom-call | bytes 786516 | tf_op jit(solution)/shard_map/pallas_call | solution.py:136
  37.7 6.3 %all-to-all-start = ((bf16[8,16,1152]{2,1,0:T(8,128)(2,1)}), bf16[8,16,1152]{2,1,0:T(8,128)(2,1)S(1)}, u32[]{:S(2)}, u32[]{:S(2)}) async-start(bf16[8,16,1152]{2,1,0:T(8,128)(2,1)} %bitcast.2), calls=%async_computation | async-start | bytes 589824 | tf_op jit(solution)/shard_map/all_to_all | solution.py:168
  43.9 4.6 %collective-permute-start = (bf16[320,1280]{1,0:T(8,128)(2,1)S(1)}, bf16[320,1280]{1,0:T(8,128)(2,1)S(1)}, u32[]{:S(2)}, u32[]{:S(2)}) collective-permute-start(bf16[320,1280]{1,0:T(8,128)(2,1)S(1)} %shard_map.64.refs_0_), channel_id=1, source_target_pairs={{16,0},{24,8},{0,16},{8,24},{17,1},{25,9},{1,17},{9,25},{18,2},{26... | collective-permute-start | bytes 2457608 | tf_op jit(solution)/shard_map/ppermute | solution.py:155
  48.6 2.2 %collective-permute-start.1 = (bf16[320,1280]{1,0:T(8,128)(2,1)S(1)}, bf16[320,1280]{1,0:T(8,128)(2,1)S(1)}, u32[]{:S(2)}, u32[]{:S(2)}) collective-permute-start(bf16[320,1280]{1,0:T(8,128)(2,1)S(1)} %shard_map.64.refs_0_), channel_id=1, source_target_pairs={{24,0},{0,8},{8,16},{16,24},{25,1},{1,9},{9,17},{17,25},{26,2},{2,... | collective-permute-start | bytes 2457608 | tf_op jit(solution)/shard_map/ppermute | solution.py:155
  50.8 4.3 %collective-permute-start.2 = (bf16[320,1280]{1,0:T(8,128)(2,1)S(1)}, bf16[320,1280]{1,0:T(8,128)(2,1)}, u32[]{:S(2)}, u32[]{:S(2)}) collective-permute-start(bf16[320,1280]{1,0:T(8,128)(2,1)S(1)} %shard_map.64.refs_0_), channel_id=1, source_target_pairs={{8,0},{16,8},{24,16},{0,24},{9,1},{17,9},{25,17},{1,25},{10,2},{18... | collective-permute-start | bytes 2457608 | tf_op jit(solution)/shard_map/ppermute | solution.py:155
  55.1 5.0 %all-to-all-done = bf16[8,16,1152]{2,1,0:T(8,128)(2,1)S(1)} async-done(((bf16[8,16,1152]{2,1,0:T(8,128)(2,1)}), bf16[8,16,1152]{2,1,0:T(8,128)(2,1)S(1)}, u32[]{:S(2)}, u32[]{:S(2)}) %all-to-all-start) | async-done | bytes 294944 | tf_op jit(solution)/shard_map/all_to_all | solution.py:168
  60.1 1.7 %shard_map.66 = (bf16[128,384]{1,0:T(8,128)(2,1)}, bf16[16,128]{1,0:T(8,128)(2,1)S(1)}) custom-call(bf16[128,1152]{1,0:T(8,128)(2,1)S(1)} %bitcast.13), custom_call_target="tpu_custom_call" | custom-call | bytes 397312 | tf_op jit(solution)/shard_map/pallas_call | solution.py:136
  61.8 6.5 %all-to-all-start.1 = ((bf16[8,16,384]{2,1,0:T(8,128)(2,1)}), bf16[8,16,384]{2,1,0:T(8,128)(2,1)S(1)}, u32[]{:S(2)}, u32[]{:S(2)}) async-start(bf16[8,16,384]{2,1,0:T(8,128)(2,1)} %bitcast.4), calls=%async_computation.1 | async-start | bytes 196608 | tf_op jit(solution)/shard_map/all_to_all | solution.py:184
  68.3 2.3 %shard_map.67.spatial_ref = bf16[128,640]{1,0:T(8,128)(2,1)S(1)} custom-call(s32[1,4]{1,0:T(1,128)S(1)} %copy-done.4, bf16[128,640]{1,0:T(8,128)(2,1)S(1)} %copy-done, bf16[128,640]{1,0:T(8,128)(2,1)S(1)} %copy-done.1, bf16[128,640]{1,0:T(8,128)(2,1)S(1)} %copy-done.2), custom_call_target="tpu_custom_call" | custom-call | bytes 655376 | tf_op jit(solution)/shard_map/pallas_call | solution.py:136
  70.6 11.2 %collective-permute-start.3 = (bf16[320,1280]{1,0:T(8,128)(2,1)S(1)}, bf16[320,1280]{1,0:T(8,128)(2,1)}, u32[]{:S(2)}, u32[]{:S(2)}) collective-permute-start(bf16[320,1280]{1,0:T(8,128)(2,1)S(1)} %shard_map.64.refs_0_), channel_id=1, source_target_pairs={{0,4},{4,0},{1,5},{5,1},{2,6},{6,2},{3,7},{7,3},{8,12},{12,8},{9,1... | collective-permute-start | bytes 2457608 | tf_op jit(solution)/shard_map/ppermute | solution.py:183
  81.8 0.0 collective-permute-done.refs_3_
  81.8 1.3 %collective-permute-done.1.refs_2_ = bf16[320,1280]{1,0:T(8,128)(2,1)S(1)} collective-permute-done((bf16[320,1280]{1,0:T(8,128)(2,1)S(1)}, bf16[320,1280]{1,0:T(8,128)(2,1)S(1)}, u32[]{:S(2)}, u32[]{:S(2)}) %collective-permute-start.1) | collective-permute-done | bytes 819232 | tf_op jit(solution)/shard_map/ppermute | solution.py:155
  83.1 0.0 collective-permute-done.2.refs_1_
  83.1 4.5 %collective-permute-start.4 = (bf16[320,1280]{1,0:T(8,128)(2,1)}, bf16[320,1280]{1,0:T(8,128)(2,1)}, u32[]{:S(2)}, u32[]{:S(2)}) collective-permute-start(bf16[320,1280]{1,0:T(8,128)(2,1)} %collective-permute-done.2.refs_1_), channel_id=1, source_target_pairs={{0,4},{4,0},{1,5},{5,1},{2,6},{6,2},{3,7},{7,3},{8,12},{12,8},{9,1... | collective-permute-start | bytes 2457608 | tf_op jit(solution)/shard_map/ppermute | solution.py:183
  87.7 1.9 %collective-permute-start.5 = (bf16[320,1280]{1,0:T(8,128)(2,1)S(1)}, bf16[320,1280]{1,0:T(8,128)(2,1)}, u32[]{:S(2)}, u32[]{:S(2)}) collective-permute-start(bf16[320,1280]{1,0:T(8,128)(2,1)S(1)} %collective-permute-done.1.refs_2_), channel_id=1, source_target_pairs={{0,4},{4,0},{1,5},{5,1},{2,6},{6,2},{3,7},{7,3},{8,12},{12,8},{9,1... | collective-permute-start | bytes 2457608 | tf_op jit(solution)/shard_map/ppermute | solution.py:183
  89.6 2.4 %collective-permute-start.6 = (bf16[320,1280]{1,0:T(8,128)(2,1)S(1)}, bf16[320,1280]{1,0:T(8,128)(2,1)}, u32[]{:S(2)}, u32[]{:S(2)}) collective-permute-start(bf16[320,1280]{1,0:T(8,128)(2,1)S(1)} %collective-permute-done.refs_3_), channel_id=1, source_target_pairs={{0,4},{4,0},{1,5},{5,1},{2,6},{6,2},{3,7},{7,3},{8,12},{12,8},{9,1... | collective-permute-start | bytes 2457608 | tf_op jit(solution)/shard_map/ppermute | solution.py:183
  92.1 0.3 fusion.order_ref
  92.3 0.0 all-to-all-done.1
  92.3 0.9 shard_map.68
  93.3 11.9 %all-gather.1 = bf16[512,640]{1,0:T(8,128)(2,1)S(1)} all-gather(bf16[128,640]{1,0:T(8,128)(2,1)S(1)} %shard_map.68), channel_id=3, replica_groups=mesh['far'=4,'near'=2,'half'=2,'x'=4,'core'=2,'head'=4] {'head'}, dimensions={0}, use_global_device_ids=true | all-gather | bytes 819200 | tf_op jit(solution)/shard_map/all_gather | solution.py:206
  105.2 0.0 collective-permute-done.3.refs_4_
  105.2 0.0 collective-permute-done.4.refs_5_
  105.2 0.0 collective-permute-done.5.refs_6_
  105.2 0.0 collective-permute-done.6.refs_7_
  105.2 4.0 %shard_map.69 = bf16[128,1280]{1,0:T(8,128)(2,1)} custom-call(bf16[4,128,640]{2,1,0:T(8,128)(2,1)S(1)} %bitcast.12, bf16[16,128]{1,0:T(8,128)(2,1)S(1)} %fusion.15.mark_ref, bf16[320,1280]{1,0:T(8,128)(2,1)S(1)} %shard_map.64.refs_0_, bf16[320,1280]{1,0:T(8,128)(2,1)} %collective-permute-done.2.refs_1_, ...), custom_call_target="tpu_custom_call" | custom-call | flops 838860800 | bytes 7540736 | tf_op jit(solution)/shard_map/pallas_call | solution.py:136
  (7 shorter events, 0.0 us)
Async XLA Ops:
  35.3 0.9 copy-start
  35.3 1.0 copy-start.1
  35.3 1.1 copy-start.2
  35.3 1.1 copy-start.3
  35.4 32.9 %copy-start.4 = (s32[1,4]{1,0:T(1,128)S(1)}, s32[1,4]{1,0:T(1,128)}, u32[]{:S(2)}) copy-start(s32[1,4]{1,0:T(1,128)} %lengths_ref) | copy-start | bytes 52
  37.7 22.4 %all-to-all-start = ((bf16[8,16,1152]{2,1,0:T(8,128)(2,1)}), bf16[8,16,1152]{2,1,0:T(8,128)(2,1)S(1)}, u32[]{:S(2)}, u32[]{:S(2)}) async-start(bf16[8,16,1152]{2,1,0:T(8,128)(2,1)} %bitcast.2), calls=%async_computation | async-start | bytes 589824 | tf_op jit(solution)/shard_map/all_to_all | solution.py:168
  43.9 37.9 %collective-permute-start = (bf16[320,1280]{1,0:T(8,128)(2,1)S(1)}, bf16[320,1280]{1,0:T(8,128)(2,1)S(1)}, u32[]{:S(2)}, u32[]{:S(2)}) collective-permute-start(bf16[320,1280]{1,0:T(8,128)(2,1)S(1)} %shard_map.64.refs_0_), channel_id=1, source_target_pairs={{16,0},{24,8},{0,16},{8,24},{17,1},{25,9},{1,17},{9,25},{18,2},{26... | collective-permute-start | bytes 2457608 | tf_op jit(solution)/shard_map/ppermute | solution.py:155
  48.6 34.5 %collective-permute-start.1 = (bf16[320,1280]{1,0:T(8,128)(2,1)S(1)}, bf16[320,1280]{1,0:T(8,128)(2,1)S(1)}, u32[]{:S(2)}, u32[]{:S(2)}) collective-permute-start(bf16[320,1280]{1,0:T(8,128)(2,1)S(1)} %shard_map.64.refs_0_), channel_id=1, source_target_pairs={{24,0},{0,8},{8,16},{16,24},{25,1},{1,9},{9,17},{17,25},{26,2},{2,... | collective-permute-start | bytes 2457608 | tf_op jit(solution)/shard_map/ppermute | solution.py:155
  50.8 32.3 %collective-permute-start.2 = (bf16[320,1280]{1,0:T(8,128)(2,1)S(1)}, bf16[320,1280]{1,0:T(8,128)(2,1)}, u32[]{:S(2)}, u32[]{:S(2)}) collective-permute-start(bf16[320,1280]{1,0:T(8,128)(2,1)S(1)} %shard_map.64.refs_0_), channel_id=1, source_target_pairs={{8,0},{16,8},{24,16},{0,24},{9,1},{17,9},{25,17},{1,25},{10,2},{18... | collective-permute-start | bytes 2457608 | tf_op jit(solution)/shard_map/ppermute | solution.py:155
  61.8 30.5 %all-to-all-start.1 = ((bf16[8,16,384]{2,1,0:T(8,128)(2,1)}), bf16[8,16,384]{2,1,0:T(8,128)(2,1)S(1)}, u32[]{:S(2)}, u32[]{:S(2)}) async-start(bf16[8,16,384]{2,1,0:T(8,128)(2,1)} %bitcast.4), calls=%async_computation.1 | async-start | bytes 196608 | tf_op jit(solution)/shard_map/all_to_all | solution.py:184
  70.6 34.6 %collective-permute-start.3 = (bf16[320,1280]{1,0:T(8,128)(2,1)S(1)}, bf16[320,1280]{1,0:T(8,128)(2,1)}, u32[]{:S(2)}, u32[]{:S(2)}) collective-permute-start(bf16[320,1280]{1,0:T(8,128)(2,1)S(1)} %shard_map.64.refs_0_), channel_id=1, source_target_pairs={{0,4},{4,0},{1,5},{5,1},{2,6},{6,2},{3,7},{7,3},{8,12},{12,8},{9,1... | collective-permute-start | bytes 2457608 | tf_op jit(solution)/shard_map/ppermute | solution.py:183
  83.1 22.1 %collective-permute-start.4 = (bf16[320,1280]{1,0:T(8,128)(2,1)}, bf16[320,1280]{1,0:T(8,128)(2,1)}, u32[]{:S(2)}, u32[]{:S(2)}) collective-permute-start(bf16[320,1280]{1,0:T(8,128)(2,1)} %collective-permute-done.2.refs_1_), channel_id=1, source_target_pairs={{0,4},{4,0},{1,5},{5,1},{2,6},{6,2},{3,7},{7,3},{8,12},{12,8},{9,1... | collective-permute-start | bytes 2457608 | tf_op jit(solution)/shard_map/ppermute | solution.py:183
  87.7 17.5 %collective-permute-start.5 = (bf16[320,1280]{1,0:T(8,128)(2,1)S(1)}, bf16[320,1280]{1,0:T(8,128)(2,1)}, u32[]{:S(2)}, u32[]{:S(2)}) collective-permute-start(bf16[320,1280]{1,0:T(8,128)(2,1)S(1)} %collective-permute-done.1.refs_2_), channel_id=1, source_target_pairs={{0,4},{4,0},{1,5},{5,1},{2,6},{6,2},{3,7},{7,3},{8,12},{12,8},{9,1... | collective-permute-start | bytes 2457608 | tf_op jit(solution)/shard_map/ppermute | solution.py:183
  89.6 15.6 %collective-permute-start.6 = (bf16[320,1280]{1,0:T(8,128)(2,1)S(1)}, bf16[320,1280]{1,0:T(8,128)(2,1)}, u32[]{:S(2)}, u32[]{:S(2)}) collective-permute-start(bf16[320,1280]{1,0:T(8,128)(2,1)S(1)} %collective-permute-done.refs_3_), channel_id=1, source_target_pairs={{0,4},{4,0},{1,5},{5,1},{2,6},{6,2},{3,7},{7,3},{8,12},{12,8},{9,1... | collective-permute-start | bytes 2457608 | tf_op jit(solution)/shard_map/ppermute | solution.py:183

commit v7 on v6

--- a/solution.py
+++ b/solution.py
@@ -117,27 +117,37 @@
 
 
 def project_kernel(mixed_ref, mark_ref, *refs):
-    slabs, out_ref = refs[:8], refs[8]
-    total = jnp.zeros((TOK, 2 * COLS), jnp.float32)
-    for group in range(4):
-        rows = [slab[group * 80 : (group + 1) * 80, :] for slab in slabs]
-        total = total + jnp.dot(
-            mixed_ref[group],
-            jnp.concatenate(rows, axis=0),
-            preferred_element_type=jnp.float32,
-        )
-    out_ref[...] = total.astype(jnp.bfloat16)
-
-
-def call(kernel, out_shape, specs, *args, scratch=(), flops=0, out_dtype=jnp.bfloat16, vmem=16):
+    slabs, (out_ref, total) = refs[:8], refs[8:]
+    group = pl.program_id(0)
+    product = jnp.dot(
+        mixed_ref[0],
+        jnp.concatenate([slab[...] for slab in slabs], axis=0),
+        preferred_element_type=jnp.float32,
+    )
+
+    @pl.when(group == 0)
+    def _():
+        total[...] = product
+
+    @pl.when(group > 0)
+    def _():
+        total[...] += product
+
+    @pl.when(group == 3)
+    def _():
+        out_ref[...] = total[...].astype(jnp.bfloat16)
+
+
+def call(kernel, out_shape, specs, *args, scratch=(), flops=0, out_dtype=jnp.bfloat16, vmem=16, grid=(), out_specs=None):
     shapes = out_shape if isinstance(out_shape, list) else [out_shape]
     size = sum(a.size * a.dtype.itemsize for a in args)
     size += sum(math.prod(shape) * jnp.dtype(out_dtype).itemsize for shape in shapes)
     results = pl.pallas_call(
         kernel,
+        grid=grid,
         out_shape=[jax.ShapeDtypeStruct(shape, out_dtype) for shape in shapes],
         in_specs=specs,
-        out_specs=[VMEM] * len(shapes),
+        out_specs=out_specs or [VMEM] * len(shapes),
         scratch_shapes=scratch,
         compiler_params=pltpu.CompilerParams(vmem_limit_bytes=vmem << 20),
         cost_estimate=pl.CostEstimate(flops=flops, bytes_accessed=size, transcendentals=0),
@@ -208,10 +218,17 @@
     return call(
         project_kernel,
         (TOK, 2 * COLS),
-        [VMEM] * 10,
+        [
+            pl.BlockSpec((1, TOK, COLS), lambda group: (group, 0, 0)),
+            pl.BlockSpec((16, HD), lambda group: (0, 0)),
+        ]
+        + [pl.BlockSpec((80, 2 * COLS), lambda group: (group, 0))] * 8,
         mixed,
         mark,
         *slabs,
+        grid=(4,),
+        out_specs=[pl.BlockSpec((TOK, 2 * COLS), lambda group: (0, 0))],
+        scratch=[pltpu.VMEM((TOK, 2 * COLS), jnp.float32)],
         flops=2 * TOK * 2560 * 1280,
     )
 

time: 111 us -> 112 us (level)
  no operation moved by 1% of the time
where the time goes in v7:
time: 112 us; the launch traced here: 110 us
  blocking collectives  47.2 us (42%)
  starting transfers between devices  44 us (39%)
  Pallas kernels  11.2 us (10%)
  waiting for transfers between devices  6.33 us (6%)
    all_gather x1, blocking collectives, body(): weight = lax.all_gather(out_weight, Z_AXES, axis=0, tiled=False)  35.3 us
    ppermute x4, starting transfers between devices, body(): slabs = slabs + [lax.ppermute(slab, 'core', swap) for slab in slabs]  20.1 us
    all_gather x1, blocking collectives, body(): mixed = lax.all_gather(mixed, 'head', axis=0, tiled=False)  11.9 us
    pallas_call x6, Pallas kernels, call(): pl.pallas_call(kernel, grid=grid, out_shape=[jax.ShapeDtypeStruct(shape,...  11.2 us
    ppermute x3, starting transfers between devices, body(): lax.ppermute(weight, 'x', [((x + step) % 4, x) for x in range(4)])  11.1 us
    all_to_all x1, starting transfers between devices, body(): lax.all_to_all(attended.reshape(FRAMES, width, TMAX * HD), FRAME_AXES, 0,...  6.46 us
    all_to_all x1, starting transfers between devices, body(): lax.all_to_all(packed.reshape(FRAMES, width, 3 * TMAX * HD), FRAME_AXES,...  6.26 us
    all_to_all x1, waiting for transfers between devices, body(): lax.all_to_all(packed.reshape(FRAMES, width, 3 * TMAX * HD), FRAME_AXES,...  5 us
  transfers between devices with their start and end apart: 9, of which 2 were waited for; matrix products, arithmetic and copies ran while one was open for 0% of the time, Pallas kernels for 4%

profile of v7, /device:TPU:1, one launch (start us, length us, event | category | flops | bytes accessed | tf_op | source)
XLA Modules:
  0.0 110.1 jit_solution(9282608152362021974)
XLA Ops:
  0.0 35.3 %all-gather.2.weight_ref = bf16[16,20,1280]{2,1,0:T(8,128)(2,1)S(1)} all-gather(bf16[1,20,1280]{2,1,0:T(8,128)(2,1)} %bitcast.15), channel_id=2, replica_groups=mesh['far'=4,'near'=2,'half'=2,'x'=4,'core'=2,'head'=4] {'far','near','h..., dimensions={0}, use_global_device_ids=true | all-gather | bytes 870400 | tf_op jit(solution)/shard_map/all_gather | solution.py:162
  35.3 0.1 shard_map.64.refs_0_
  35.4 0.0 copy-start.4
  35.4 0.8 copy-done
  36.2 0.1 copy-done.1
  36.3 0.1 copy-done.2
  36.4 0.0 copy-done.3
  36.4 1.3 %shard_map.65 = bf16[128,1152]{1,0:T(8,128)(2,1)} custom-call(s32[1]{0:T(128)} %bitcast.group_ref, s32[20]{0:T(128)S(1)} %copy-done.3, bf16[128,640]{1,0:T(8,128)(2,1)S(1)} %copy-done, bf16[128,640]{1,0:T(8,128)(2,1)S(1)} %copy-done.1, bf16[128,640]{1,0:T(8,128)(2,1)S(1)} %copy-done.2), custom_call_target="tpu_custom_call" | custom-call | bytes 786516 | tf_op jit(solution)/shard_map/pallas_call | solution.py:145
  37.7 6.3 %all-to-all-start = ((bf16[8,16,1152]{2,1,0:T(8,128)(2,1)}), bf16[8,16,1152]{2,1,0:T(8,128)(2,1)S(1)}, u32[]{:S(2)}, u32[]{:S(2)}) async-start(bf16[8,16,1152]{2,1,0:T(8,128)(2,1)} %bitcast.2), calls=%async_computation | async-start | bytes 589824 | tf_op jit(solution)/shard_map/all_to_all | solution.py:178
  43.9 4.6 %collective-permute-start = (bf16[320,1280]{1,0:T(8,128)(2,1)S(1)}, bf16[320,1280]{1,0:T(8,128)(2,1)S(1)}, u32[]{:S(2)}, u32[]{:S(2)}) collective-permute-start(bf16[320,1280]{1,0:T(8,128)(2,1)S(1)} %shard_map.64.refs_0_), channel_id=1, source_target_pairs={{16,0},{24,8},{0,16},{8,24},{17,1},{25,9},{1,17},{9,25},{18,2},{26... | collective-permute-start | bytes 2457608 | tf_op jit(solution)/shard_map/ppermute | solution.py:165
  48.6 2.2 %collective-permute-start.1 = (bf16[320,1280]{1,0:T(8,128)(2,1)S(1)}, bf16[320,1280]{1,0:T(8,128)(2,1)S(1)}, u32[]{:S(2)}, u32[]{:S(2)}) collective-permute-start(bf16[320,1280]{1,0:T(8,128)(2,1)S(1)} %shard_map.64.refs_0_), channel_id=1, source_target_pairs={{24,0},{0,8},{8,16},{16,24},{25,1},{1,9},{9,17},{17,25},{26,2},{2,... | collective-permute-start | bytes 2457608 | tf_op jit(solution)/shard_map/ppermute | solution.py:165
  50.8 4.3 %collective-permute-start.2 = (bf16[320,1280]{1,0:T(8,128)(2,1)S(1)}, bf16[320,1280]{1,0:T(8,128)(2,1)}, u32[]{:S(2)}, u32[]{:S(2)}) collective-permute-start(bf16[320,1280]{1,0:T(8,128)(2,1)S(1)} %shard_map.64.refs_0_), channel_id=1, source_target_pairs={{8,0},{16,8},{24,16},{0,24},{9,1},{17,9},{25,17},{1,25},{10,2},{18... | collective-permute-start | bytes 2457608 | tf_op jit(solution)/shard_map/ppermute | solution.py:165
  55.1 5.0 %all-to-all-done = bf16[8,16,1152]{2,1,0:T(8,128)(2,1)S(1)} async-done(((bf16[8,16,1152]{2,1,0:T(8,128)(2,1)}), bf16[8,16,1152]{2,1,0:T(8,128)(2,1)S(1)}, u32[]{:S(2)}, u32[]{:S(2)}) %all-to-all-start) | async-done | bytes 294944 | tf_op jit(solution)/shard_map/all_to_all | solution.py:178
  60.1 1.7 %shard_map.66 = (bf16[128,384]{1,0:T(8,128)(2,1)}, bf16[16,128]{1,0:T(8,128)(2,1)S(1)}) custom-call(bf16[128,1152]{1,0:T(8,128)(2,1)S(1)} %bitcast.13), custom_call_target="tpu_custom_call" | custom-call | bytes 397312 | tf_op jit(solution)/shard_map/pallas_call | solution.py:145
  61.8 6.5 %all-to-all-start.1 = ((bf16[8,16,384]{2,1,0:T(8,128)(2,1)}), bf16[8,16,384]{2,1,0:T(8,128)(2,1)S(1)}, u32[]{:S(2)}, u32[]{:S(2)}) async-start(bf16[8,16,384]{2,1,0:T(8,128)(2,1)} %bitcast.4), calls=%async_computation.1 | async-start | bytes 196608 | tf_op jit(solution)/shard_map/all_to_all | solution.py:194
  68.3 2.3 %shard_map.67.spatial_ref = bf16[128,640]{1,0:T(8,128)(2,1)S(1)} custom-call(s32[1,4]{1,0:T(1,128)S(1)} %copy-done.4, bf16[128,640]{1,0:T(8,128)(2,1)S(1)} %copy-done, bf16[128,640]{1,0:T(8,128)(2,1)S(1)} %copy-done.1, bf16[128,640]{1,0:T(8,128)(2,1)S(1)} %copy-done.2), custom_call_target="tpu_custom_call" | custom-call | bytes 655376 | tf_op jit(solution)/shard_map/pallas_call | solution.py:145
  70.6 11.2 %collective-permute-start.3 = (bf16[320,1280]{1,0:T(8,128)(2,1)S(1)}, bf16[320,1280]{1,0:T(8,128)(2,1)}, u32[]{:S(2)}, u32[]{:S(2)}) collective-permute-start(bf16[320,1280]{1,0:T(8,128)(2,1)S(1)} %shard_map.64.refs_0_), channel_id=1, source_target_pairs={{0,4},{4,0},{1,5},{5,1},{2,6},{6,2},{3,7},{7,3},{8,12},{12,8},{9,1... | collective-permute-start | bytes 2457608 | tf_op jit(solution)/shard_map/ppermute | solution.py:193
  81.8 0.0 collective-permute-done.refs_3_
  81.8 1.3 %collective-permute-done.1.refs_2_ = bf16[320,1280]{1,0:T(8,128)(2,1)S(1)} collective-permute-done((bf16[320,1280]{1,0:T(8,128)(2,1)S(1)}, bf16[320,1280]{1,0:T(8,128)(2,1)S(1)}, u32[]{:S(2)}, u32[]{:S(2)}) %collective-permute-start.1) | collective-permute-done | bytes 819232 | tf_op jit(solution)/shard_map/ppermute | solution.py:165
  83.1 0.0 collective-permute-done.2.refs_1_
  83.1 4.5 %collective-permute-start.4 = (bf16[320,1280]{1,0:T(8,128)(2,1)}, bf16[320,1280]{1,0:T(8,128)(2,1)}, u32[]{:S(2)}, u32[]{:S(2)}) collective-permute-start(bf16[320,1280]{1,0:T(8,128)(2,1)} %collective-permute-done.2.refs_1_), channel_id=1, source_target_pairs={{0,4},{4,0},{1,5},{5,1},{2,6},{6,2},{3,7},{7,3},{8,12},{12,8},{9,1... | collective-permute-start | bytes 2457608 | tf_op jit(solution)/shard_map/ppermute | solution.py:193
  87.7 1.9 %collective-permute-start.5 = (bf16[320,1280]{1,0:T(8,128)(2,1)S(1)}, bf16[320,1280]{1,0:T(8,128)(2,1)}, u32[]{:S(2)}, u32[]{:S(2)}) collective-permute-start(bf16[320,1280]{1,0:T(8,128)(2,1)S(1)} %collective-permute-done.1.refs_2_), channel_id=1, source_target_pairs={{0,4},{4,0},{1,5},{5,1},{2,6},{6,2},{3,7},{7,3},{8,12},{12,8},{9,1... | collective-permute-start | bytes 2457608 | tf_op jit(solution)/shard_map/ppermute | solution.py:193
  89.6 2.4 %collective-permute-start.6 = (bf16[320,1280]{1,0:T(8,128)(2,1)S(1)}, bf16[320,1280]{1,0:T(8,128)(2,1)}, u32[]{:S(2)}, u32[]{:S(2)}) collective-permute-start(bf16[320,1280]{1,0:T(8,128)(2,1)S(1)} %collective-permute-done.refs_3_), channel_id=1, source_target_pairs={{0,4},{4,0},{1,5},{5,1},{2,6},{6,2},{3,7},{7,3},{8,12},{12,8},{9,1... | collective-permute-start | bytes 2457608 | tf_op jit(solution)/shard_map/ppermute | solution.py:193
  92.1 0.3 fusion.order_ref
  92.3 0.0 all-to-all-done.1
  92.3 0.9 shard_map.68
  93.3 11.9 %all-gather.1 = bf16[512,640]{1,0:T(8,128)(2,1)S(1)} all-gather(bf16[128,640]{1,0:T(8,128)(2,1)S(1)} %shard_map.68), channel_id=3, replica_groups=mesh['far'=4,'near'=2,'half'=2,'x'=4,'core'=2,'head'=4] {'head'}, dimensions={0}, use_global_device_ids=true | all-gather | bytes 819200 | tf_op jit(solution)/shard_map/all_gather | solution.py:216
  105.2 0.0 collective-permute-done.3.refs_4_
  105.2 0.0 collective-permute-done.4.refs_5_
  105.2 0.0 collective-permute-done.5.refs_6_
  105.2 0.0 collective-permute-done.6.refs_7_
  105.2 4.9 %shard_map.69 = bf16[128,1280]{1,0:T(8,128)(2,1)} custom-call(bf16[4,128,640]{2,1,0:T(8,128)(2,1)S(1)} %bitcast.12, bf16[16,128]{1,0:T(8,128)(2,1)S(1)} %fusion.15.mark_ref, bf16[320,1280]{1,0:T(8,128)(2,1)S(1)} %shard_map.64.refs_0_, bf16[320,1280]{1,0:T(8,128)(2,1)} %collective-permute-done.2.refs_1_, ...), custom_call_target="tpu_custom_call" | custom-call | flops 838860800 | bytes 7540736 | tf_op jit(solution)/shard_map/pallas_call | solution.py:145
  (7 shorter events, 0.0 us)
Async XLA Ops:
  35.3 0.9 copy-start
  35.3 1.0 copy-start.1
  35.3 1.1 copy-start.2
  35.3 1.1 copy-start.3
  35.4 32.9 %copy-start.4 = (s32[1,4]{1,0:T(1,128)S(1)}, s32[1,4]{1,0:T(1,128)}, u32[]{:S(2)}) copy-start(s32[1,4]{1,0:T(1,128)} %lengths_ref) | copy-start | bytes 52
  37.7 22.4 %all-to-all-start = ((bf16[8,16,1152]{2,1,0:T(8,128)(2,1)}), bf16[8,16,1152]{2,1,0:T(8,128)(2,1)S(1)}, u32[]{:S(2)}, u32[]{:S(2)}) async-start(bf16[8,16,1152]{2,1,0:T(8,128)(2,1)} %bitcast.2), calls=%async_computation | async-start | bytes 589824 | tf_op jit(solution)/shard_map/all_to_all | solution.py:178
  43.9 37.9 %collective-permute-start = (bf16[320,1280]{1,0:T(8,128)(2,1)S(1)}, bf16[320,1280]{1,0:T(8,128)(2,1)S(1)}, u32[]{:S(2)}, u32[]{:S(2)}) collective-permute-start(bf16[320,1280]{1,0:T(8,128)(2,1)S(1)} %shard_map.64.refs_0_), channel_id=1, source_target_pairs={{16,0},{24,8},{0,16},{8,24},{17,1},{25,9},{1,17},{9,25},{18,2},{26... | collective-permute-start | bytes 2457608 | tf_op jit(solution)/shard_map/ppermute | solution.py:165
  48.6 34.5 %collective-permute-start.1 = (bf16[320,1280]{1,0:T(8,128)(2,1)S(1)}, bf16[320,1280]{1,0:T(8,128)(2,1)S(1)}, u32[]{:S(2)}, u32[]{:S(2)}) collective-permute-start(bf16[320,1280]{1,0:T(8,128)(2,1)S(1)} %shard_map.64.refs_0_), channel_id=1, source_target_pairs={{24,0},{0,8},{8,16},{16,24},{25,1},{1,9},{9,17},{17,25},{26,2},{2,... | collective-permute-start | bytes 2457608 | tf_op jit(solution)/shard_map/ppermute | solution.py:165
  50.8 32.3 %collective-permute-start.2 = (bf16[320,1280]{1,0:T(8,128)(2,1)S(1)}, bf16[320,1280]{1,0:T(8,128)(2,1)}, u32[]{:S(2)}, u32[]{:S(2)}) collective-permute-start(bf16[320,1280]{1,0:T(8,128)(2,1)S(1)} %shard_map.64.refs_0_), channel_id=1, source_target_pairs={{8,0},{16,8},{24,16},{0,24},{9,1},{17,9},{25,17},{1,25},{10,2},{18... | collective-permute-start | bytes 2457608 | tf_op jit(solution)/shard_map/ppermute | solution.py:165
  61.8 30.5 %all-to-all-start.1 = ((bf16[8,16,384]{2,1,0:T(8,128)(2,1)}), bf16[8,16,384]{2,1,0:T(8,128)(2,1)S(1)}, u32[]{:S(2)}, u32[]{:S(2)}) async-start(bf16[8,16,384]{2,1,0:T(8,128)(2,1)} %bitcast.4), calls=%async_computation.1 | async-start | bytes 196608 | tf_op jit(solution)/shard_map/all_to_all | solution.py:194
  70.6 34.6 %collective-permute-start.3 = (bf16[320,1280]{1,0:T(8,128)(2,1)S(1)}, bf16[320,1280]{1,0:T(8,128)(2,1)}, u32[]{:S(2)}, u32[]{:S(2)}) collective-permute-start(bf16[320,1280]{1,0:T(8,128)(2,1)S(1)} %shard_map.64.refs_0_), channel_id=1, source_target_pairs={{0,4},{4,0},{1,5},{5,1},{2,6},{6,2},{3,7},{7,3},{8,12},{12,8},{9,1... | collective-permute-start | bytes 2457608 | tf_op jit(solution)/shard_map/ppermute | solution.py:193
  83.1 22.1 %collective-permute-start.4 = (bf16[320,1280]{1,0:T(8,128)(2,1)}, bf16[320,1280]{1,0:T(8,128)(2,1)}, u32[]{:S(2)}, u32[]{:S(2)}) collective-permute-start(bf16[320,1280]{1,0:T(8,128)(2,1)} %collective-permute-done.2.refs_1_), channel_id=1, source_target_pairs={{0,4},{4,0},{1,5},{5,1},{2,6},{6,2},{3,7},{7,3},{8,12},{12,8},{9,1... | collective-permute-start | bytes 2457608 | tf_op jit(solution)/shard_map/ppermute | solution.py:193
  87.7 17.5 %collective-permute-start.5 = (bf16[320,1280]{1,0:T(8,128)(2,1)S(1)}, bf16[320,1280]{1,0:T(8,128)(2,1)}, u32[]{:S(2)}, u32[]{:S(2)}) collective-permute-start(bf16[320,1280]{1,0:T(8,128)(2,1)S(1)} %collective-permute-done.1.refs_2_), channel_id=1, source_target_pairs={{0,4},{4,0},{1,5},{5,1},{2,6},{6,2},{3,7},{7,3},{8,12},{12,8},{9,1... | collective-permute-start | bytes 2457608 | tf_op jit(solution)/shard_map/ppermute | solution.py:193
  89.6 15.6 %collective-permute-start.6 = (bf16[320,1280]{1,0:T(8,128)(2,1)S(1)}, bf16[320,1280]{1,0:T(8,128)(2,1)}, u32[]{:S(2)}, u32[]{:S(2)}) collective-permute-start(bf16[320,1280]{1,0:T(8,128)(2,1)S(1)} %collective-permute-done.refs_3_), channel_id=1, source_target_pairs={{0,4},{4,0},{1,5},{5,1},{2,6},{6,2},{3,7},{7,3},{8,12},{12,8},{9,1... | collective-permute-start | bytes 2457608 | tf_op jit(solution)/shard_map/ppermute | solution.py:193

commit v8 on v6

--- a/solution.py
+++ b/solution.py
@@ -170,7 +170,14 @@
     ).reshape(TOK, 3 * TMAX * HD)
     attended, mark = call(frame_kernel, [(TOK, TMAX * HD), (16, HD)], [VMEM], packed)
     mark, weight = lax.optimization_barrier((mark, weight))
-    mark, window_lengths = lax.optimization_barrier((mark, window_lengths))
+    source = jnp.arange(COLS, dtype=jnp.int32)[:, None]
+    place = jnp.arange(COLS, dtype=jnp.int32)[None, :]
+    turn = place // 80 % 4
+    turn = turn + (turn == 2) - (turn == 3)
+    owner = (lax.axis_index("x") + turn) % 4 * 2 + (core + place // 320) % 2
+    wanted = place % 80 // 20 * 160 + owner * 20 + place % 20
+    order = (source == wanted).astype(jnp.bfloat16)
+    mark, window_lengths, order = lax.optimization_barrier((mark, window_lengths, order))
     spatial = call(
         window_kernel, (TOK, COLS), [SMEM] + [VMEM] * 3, window_lengths, queries, keys, values
     )
@@ -185,13 +192,6 @@
         attended.reshape(FRAMES, width, TMAX * HD), FRAME_AXES, 0, 0, tiled=True
     ).reshape(TOK, TMAX * HD)
 
-    source = jnp.arange(COLS, dtype=jnp.int32)[:, None]
-    place = jnp.arange(COLS, dtype=jnp.int32)[None, :]
-    turn = place // 80 % 4
-    turn = turn + (turn == 2) - (turn == 3)
-    owner = (lax.axis_index("x") + turn) % 4 * 2 + (core + place // 320) % 2
-    wanted = place % 80 // 20 * 160 + owner * 20 + place % 20
-    order = (source == wanted).astype(jnp.bfloat16)
     mixed = call(
         mix_kernel,
         (TOK, COLS),

time: 111 us -> 136 us (1.23)
  the two profiles are of different devices: /device:TPU:1 before, /device:TPU:2 now
where the time goes in v8:
time: 136 us
  blocking collectives  82.4 us (61%)
  starting transfers between devices  24.8 us (18%)
  waiting for transfers between devices  18.4 us (14%)
  Pallas kernels  9 us (7%)
    all_gather x1, blocking collectives, body(): weight = lax.all_gather(out_weight, Z_AXES, axis=0, tiled=False)  41.3 us
    all_to_all x1, blocking collectives, body(): lax.all_to_all(attended.reshape(FRAMES, width, TMAX * HD), FRAME_AXES, 0,...  26.8 us
    all_gather x1, blocking collectives, body(): mixed = lax.all_gather(mixed, 'head', axis=0, tiled=False)  14.3 us
    ppermute x3, waiting for transfers between devices, body(): lax.ppermute(weight, 'x', [((x + step) % 4, x) for x in range(4)])  10.7 us
    ppermute x3, starting transfers between devices, body(): lax.ppermute(weight, 'x', [((x + step) % 4, x) for x in range(4)])  9.87 us
    pallas_call x6, Pallas kernels, call(): pl.pallas_call(kernel, out_shape=[jax.ShapeDtypeStruct(shape, out_dtype)...  9 us
    ppermute x4, starting transfers between devices, body(): slabs = slabs + [lax.ppermute(slab, 'core', swap) for slab in slabs]  8.16 us
    all_to_all x1, waiting for transfers between devices, body(): lax.all_to_all(packed.reshape(FRAMES, width, 3 * TMAX * HD), FRAME_AXES,...  7.65 us
  transfers between devices with their start and end apart: 8, of which 3 were waited for; matrix products, arithmetic and copies ran while one was open for 0% of the time, Pallas kernels for 3%

profile of v8, /device:TPU:2, one launch (start us, length us, event | category | flops | bytes accessed | tf_op | source)
XLA Modules:
  0.0 136.0 jit_solution(477522161195198180)
XLA Ops:
  0.0 41.3 %all-gather.2.weight_ref = bf16[16,20,1280]{2,1,0:T(8,128)(2,1)S(1)} all-gather(bf16[1,20,1280]{2,1,0:T(8,128)(2,1)} %bitcast.16), channel_id=2, replica_groups=mesh['far'=4,'near'=2,'half'=2,'x'=4,'core'=2,'head'=4] {'far','near','h..., dimensions={0}, use_global_device_ids=true | all-gather | bytes 870400 | tf_op jit(solution)/shard_map/all_gather | solution.py:152
  41.3 0.0 copy-start
  41.3 0.1 shard_map.64.refs_0_
  41.5 0.8 copy-done
  42.2 0.1 copy-done.1
  42.3 0.1 copy-done.2
  42.4 0.0 copy-done.3
  42.4 1.3 shard_map.65
  43.7 6.7 %all-to-all-start = ((bf16[8,16,1152]{2,1,0:T(8,128)(2,1)}), bf16[8,16,1152]{2,1,0:T(8,128)(2,1)S(1)}, u32[]{:S(2)}, u32[]{:S(2)}) async-start(bf16[8,16,1152]{2,1,0:T(8,128)(2,1)} %bitcast.2), calls=%async_computation | async-start | bytes 589824 | tf_op jit(solution)/shard_map/all_to_all | solution.py:168
  50.5 4.0 %collective-permute-start = (bf16[320,1280]{1,0:T(8,128)(2,1)S(1)}, bf16[320,1280]{1,0:T(8,128)(2,1)S(1)}, u32[]{:S(2)}, u32[]{:S(2)}) collective-permute-start(bf16[320,1280]{1,0:T(8,128)(2,1)S(1)} %shard_map.64.refs_0_), channel_id=1, source_target_pairs={{16,0},{24,8},{0,16},{8,24},{17,1},{25,9},{1,17},{9,25},{18,2},{26... | collective-permute-start | bytes 2457608 | tf_op jit(solution)/shard_map/ppermute | solution.py:155
  54.5 1.9 %collective-permute-start.1 = (bf16[320,1280]{1,0:T(8,128)(2,1)S(1)}, bf16[320,1280]{1,0:T(8,128)(2,1)}, u32[]{:S(2)}, u32[]{:S(2)}) collective-permute-start(bf16[320,1280]{1,0:T(8,128)(2,1)S(1)} %shard_map.64.refs_0_), channel_id=1, source_target_pairs={{24,0},{0,8},{8,16},{16,24},{25,1},{1,9},{9,17},{17,25},{26,2},{2,... | collective-permute-start | bytes 2457608 | tf_op jit(solution)/shard_map/ppermute | solution.py:155
  56.4 3.9 %collective-permute-start.2 = (bf16[320,1280]{1,0:T(8,128)(2,1)S(1)}, bf16[320,1280]{1,0:T(8,128)(2,1)}, u32[]{:S(2)}, u32[]{:S(2)}) collective-permute-start(bf16[320,1280]{1,0:T(8,128)(2,1)S(1)} %shard_map.64.refs_0_), channel_id=1, source_target_pairs={{8,0},{16,8},{24,16},{0,24},{9,1},{17,9},{25,17},{1,25},{10,2},{18... | collective-permute-start | bytes 2457608 | tf_op jit(solution)/shard_map/ppermute | solution.py:155
  60.4 0.3 fusion.order_ref
  60.7 7.7 %all-to-all-done = bf16[8,16,1152]{2,1,0:T(8,128)(2,1)S(1)} async-done(((bf16[8,16,1152]{2,1,0:T(8,128)(2,1)}), bf16[8,16,1152]{2,1,0:T(8,128)(2,1)S(1)}, u32[]{:S(2)}, u32[]{:S(2)}) %all-to-all-start) | async-done | bytes 294944 | tf_op jit(solution)/shard_map/all_to_all | solution.py:168
  68.3 1.1 shard_map.66
  69.4 0.0 copy-done.4
  69.4 2.3 %shard_map.67.spatial_ref = bf16[128,640]{1,0:T(8,128)(2,1)S(1)} custom-call(s32[1,4]{1,0:T(1,128)S(1)} %copy-done.4, bf16[128,640]{1,0:T(8,128)(2,1)S(1)} %copy-done, bf16[128,640]{1,0:T(8,128)(2,1)S(1)} %copy-done.1, bf16[128,640]{1,0:T(8,128)(2,1)S(1)} %copy-done.2), custom_call_target="tpu_custom_call" | custom-call | bytes 655376 | tf_op jit(solution)/shard_map/pallas_call | solution.py:136
  71.7 1.9 %collective-permute-start.3 = (bf16[320,1280]{1,0:T(8,128)(2,1)S(1)}, bf16[320,1280]{1,0:T(8,128)(2,1)S(1)}, u32[]{:S(2)}, u32[]{:S(2)}) collective-permute-start(bf16[320,1280]{1,0:T(8,128)(2,1)S(1)} %shard_map.64.refs_0_), channel_id=1, source_target_pairs={{0,4},{4,0},{1,5},{5,1},{2,6},{6,2},{3,7},{7,3},{8,12},{12,8},{9,1... | collective-permute-start | bytes 2457608 | tf_op jit(solution)/shard_map/ppermute | solution.py:190
  73.6 1.4 %collective-permute-done.refs_3_ = bf16[320,1280]{1,0:T(8,128)(2,1)S(1)} collective-permute-done((bf16[320,1280]{1,0:T(8,128)(2,1)S(1)}, bf16[320,1280]{1,0:T(8,128)(2,1)S(1)}, u32[]{:S(2)}, u32[]{:S(2)}) %collective-permute-start) | collective-permute-done | bytes 819232 | tf_op jit(solution)/shard_map/ppermute | solution.py:155
  75.1 9.3 %collective-permute-done.1.refs_2_ = bf16[320,1280]{1,0:T(8,128)(2,1)} collective-permute-done((bf16[320,1280]{1,0:T(8,128)(2,1)S(1)}, bf16[320,1280]{1,0:T(8,128)(2,1)}, u32[]{:S(2)}, u32[]{:S(2)}) %collective-permute-start.1) | collective-permute-done | bytes 819232 | tf_op jit(solution)/shard_map/ppermute | solution.py:155
  84.3 0.0 collective-permute-done.2.refs_1_
  84.3 1.9 %collective-permute-start.4 = (bf16[320,1280]{1,0:T(8,128)(2,1)}, bf16[320,1280]{1,0:T(8,128)(2,1)S(1)}, u32[]{:S(2)}, u32[]{:S(2)}) collective-permute-start(bf16[320,1280]{1,0:T(8,128)(2,1)} %collective-permute-done.2.refs_1_), channel_id=1, source_target_pairs={{0,4},{4,0},{1,5},{5,1},{2,6},{6,2},{3,7},{7,3},{8,12},{12,8},{9,1... | collective-permute-start | bytes 2457608 | tf_op jit(solution)/shard_map/ppermute | solution.py:190
  86.3 2.4 %collective-permute-start.5 = (bf16[320,1280]{1,0:T(8,128)(2,1)}, bf16[320,1280]{1,0:T(8,128)(2,1)S(1)}, u32[]{:S(2)}, u32[]{:S(2)}) collective-permute-start(bf16[320,1280]{1,0:T(8,128)(2,1)} %collective-permute-done.1.refs_2_), channel_id=1, source_target_pairs={{0,4},{4,0},{1,5},{5,1},{2,6},{6,2},{3,7},{7,3},{8,12},{12,8},{9,1... | collective-permute-start | bytes 2457608 | tf_op jit(solution)/shard_map/ppermute | solution.py:190
  88.7 1.9 %collective-permute-start.6 = (bf16[320,1280]{1,0:T(8,128)(2,1)S(1)}, bf16[320,1280]{1,0:T(8,128)(2,1)S(1)}, u32[]{:S(2)}, u32[]{:S(2)}) collective-permute-start(bf16[320,1280]{1,0:T(8,128)(2,1)S(1)} %collective-permute-done.refs_3_), channel_id=1, source_target_pairs={{0,4},{4,0},{1,5},{5,1},{2,6},{6,2},{3,7},{7,3},{8,12},{12,8},{9,1... | collective-permute-start | bytes 2457608 | tf_op jit(solution)/shard_map/ppermute | solution.py:190
  90.6 26.8 %all_to_all.10 = bf16[8,16,384]{2,1,0:T(8,128)(2,1)S(1)} all-to-all(bf16[8,16,384]{2,1,0:T(8,128)(2,1)S(1)} %bitcast.15), channel_id=1, replica_groups=mesh['far'=4,'near'=2,'half'=2,'x'=4,'core'=2,'head'=4] {'far','near'}, dimensions={0} | all-to-all | bytes 196608 | tf_op jit(solution)/shard_map/all_to_all | solution.py:191
  117.4 0.9 shard_map.68
  118.3 14.3 %all-gather.1 = bf16[512,640]{1,0:T(8,128)(2,1)S(1)} all-gather(bf16[128,640]{1,0:T(8,128)(2,1)S(1)} %shard_map.68), channel_id=3, replica_groups=mesh['far'=4,'near'=2,'half'=2,'x'=4,'core'=2,'head'=4] {'head'}, dimensions={0}, use_global_device_ids=true | all-gather | bytes 819200 | tf_op jit(solution)/shard_map/all_gather | solution.py:206
  132.6 0.0 collective-permute-done.3.refs_4_
  132.6 0.0 collective-permute-done.4.refs_5_
  132.6 0.0 collective-permute-done.5.refs_6_
  132.6 0.0 collective-permute-done.6.refs_7_
  132.7 3.3 %shard_map.69 = bf16[128,1280]{1,0:T(8,128)(2,1)} custom-call(bf16[4,128,640]{2,1,0:T(8,128)(2,1)S(1)} %bitcast.12, bf16[16,128]{1,0:T(8,128)(2,1)S(1)} %fusion.15.mark_ref, bf16[320,1280]{1,0:T(8,128)(2,1)S(1)} %shard_map.64.refs_0_, bf16[320,1280]{1,0:T(8,128)(2,1)} %collective-permute-done.2.refs_1_, bf16[320,1280]{1,0:T(8,128)(2,1)} %collective-permute-done.1.refs_2_, ...), custom_call_target="tpu_custom_call" | custom-call | flops 838860800 | bytes 7540736 | tf_op jit(solution)/shard_map/pallas_call | solution.py:136
  (6 shorter events, 0.0 us)
Async XLA Ops:
  41.3 0.9 copy-start
  41.3 1.0 copy-start.1
  41.3 1.1 copy-start.2
  41.3 1.1 copy-start.3
  43.7 25.7 %copy-start.4 = (s32[1,4]{1,0:T(1,128)S(1)}, s32[1,4]{1,0:T(1,128)}, u32[]{:S(2)}) copy-start(s32[1,4]{1,0:T(1,128)} %lengths_ref) | copy-start | bytes 52
  43.7 24.6 %all-to-all-start = ((bf16[8,16,1152]{2,1,0:T(8,128)(2,1)}), bf16[8,16,1152]{2,1,0:T(8,128)(2,1)S(1)}, u32[]{:S(2)}, u32[]{:S(2)}) async-start(bf16[8,16,1152]{2,1,0:T(8,128)(2,1)} %bitcast.2), calls=%async_computation | async-start | bytes 589824 | tf_op jit(solution)/shard_map/all_to_all | solution.py:168
  50.5 24.6 %collective-permute-start = (bf16[320,1280]{1,0:T(8,128)(2,1)S(1)}, bf16[320,1280]{1,0:T(8,128)(2,1)S(1)}, u32[]{:S(2)}, u32[]{:S(2)}) collective-permute-start(bf16[320,1280]{1,0:T(8,128)(2,1)S(1)} %shard_map.64.refs_0_), channel_id=1, source_target_pairs={{16,0},{24,8},{0,16},{8,24},{17,1},{25,9},{1,17},{9,25},{18,2},{26... | collective-permute-start | bytes 2457608 | tf_op jit(solution)/shard_map/ppermute | solution.py:155
  54.5 29.8 %collective-permute-start.1 = (bf16[320,1280]{1,0:T(8,128)(2,1)S(1)}, bf16[320,1280]{1,0:T(8,128)(2,1)}, u32[]{:S(2)}, u32[]{:S(2)}) collective-permute-start(bf16[320,1280]{1,0:T(8,128)(2,1)S(1)} %shard_map.64.refs_0_), channel_id=1, source_target_pairs={{24,0},{0,8},{8,16},{16,24},{25,1},{1,9},{9,17},{17,25},{26,2},{2,... | collective-permute-start | bytes 2457608 | tf_op jit(solution)/shard_map/ppermute | solution.py:155
  56.4 27.9 %collective-permute-start.2 = (bf16[320,1280]{1,0:T(8,128)(2,1)S(1)}, bf16[320,1280]{1,0:T(8,128)(2,1)}, u32[]{:S(2)}, u32[]{:S(2)}) collective-permute-start(bf16[320,1280]{1,0:T(8,128)(2,1)S(1)} %shard_map.64.refs_0_), channel_id=1, source_target_pairs={{8,0},{16,8},{24,16},{0,24},{9,1},{17,9},{25,17},{1,25},{10,2},{18... | collective-permute-start | bytes 2457608 | tf_op jit(solution)/shard_map/ppermute | solution.py:155
  71.7 60.9 %collective-permute-start.3 = (bf16[320,1280]{1,0:T(8,128)(2,1)S(1)}, bf16[320,1280]{1,0:T(8,128)(2,1)S(1)}, u32[]{:S(2)}, u32[]{:S(2)}) collective-permute-start(bf16[320,1280]{1,0:T(8,128)(2,1)S(1)} %shard_map.64.refs_0_), channel_id=1, source_target_pairs={{0,4},{4,0},{1,5},{5,1},{2,6},{6,2},{3,7},{7,3},{8,12},{12,8},{9,1... | collective-permute-start | bytes 2457608 | tf_op jit(solution)/shard_map/ppermute | solution.py:190
  84.3 48.3 %collective-permute-start.4 = (bf16[320,1280]{1,0:T(8,128)(2,1)}, bf16[320,1280]{1,0:T(8,128)(2,1)S(1)}, u32[]{:S(2)}, u32[]{:S(2)}) collective-permute-start(bf16[320,1280]{1,0:T(8,128)(2,1)} %collective-permute-done.2.refs_1_), channel_id=1, source_target_pairs={{0,4},{4,0},{1,5},{5,1},{2,6},{6,2},{3,7},{7,3},{8,12},{12,8},{9,1... | collective-permute-start | bytes 2457608 | tf_op jit(solution)/shard_map/ppermute | solution.py:190
  86.3 46.4 %collective-permute-start.5 = (bf16[320,1280]{1,0:T(8,128)(2,1)}, bf16[320,1280]{1,0:T(8,128)(2,1)S(1)}, u32[]{:S(2)}, u32[]{:S(2)}) collective-permute-start(bf16[320,1280]{1,0:T(8,128)(2,1)} %collective-permute-done.1.refs_2_), channel_id=1, source_target_pairs={{0,4},{4,0},{1,5},{5,1},{2,6},{6,2},{3,7},{7,3},{8,12},{12,8},{9,1... | collective-permute-start | bytes 2457608 | tf_op jit(solution)/shard_map/ppermute | solution.py:190
  88.7 44.0 %collective-permute-start.6 = (bf16[320,1280]{1,0:T(8,128)(2,1)S(1)}, bf16[320,1280]{1,0:T(8,128)(2,1)S(1)}, u32[]{:S(2)}, u32[]{:S(2)}) collective-permute-start(bf16[320,1280]{1,0:T(8,128)(2,1)S(1)} %collective-permute-done.refs_3_), channel_id=1, source_target_pairs={{0,4},{4,0},{1,5},{5,1},{2,6},{6,2},{3,7},{7,3},{8,12},{12,8},{9,1... | collective-permute-start | bytes 2457608 | tf_op jit(solution)/shard_map/ppermute | solution.py:190
